TPU v7x, 32 devices: a whole 2x2x4 slice. The times are simulated.
32 devices in a mesh: groups: 2 (over y), dp: 4 (over z), replica: 4 (over x, core).
Axes of the slice: x: 2, y: 2, z: 4, core: 2. Of those that a mesh axis runs over, the one named last changes fastest.
Arguments:
- embeddings: bfloat16 [32768, 768], P(('groups', 'dp', 'replica')), parts along dimension 0, may hold values from -8 to 8
- codes: int32 [32768, 96], P(('groups', 'dp', 'replica')), parts along dimension 0, may hold values from 0 to 255
- rotation: bfloat16 [1536, 768], P('groups'), parts along dimension 0, may hold values from -2 to 2
- codebook: bfloat16 [512, 768], P(('groups', 'dp')), parts along dimension 0, may hold values from -8 to 8
Outputs:
- new_codebook: float32 [512, 768], P(('groups', 'dp')), parts along dimension 0
- cross: float32 [1536, 768], P(('groups', 'dp')), parts along dimension 0
There are 2 independent parts, one for each index of `groups`. A program takes and returns all parts, laid end to end along the dimension named above; each array names one. Nothing has to cross between parts.
All inputs are finite; a program needn't handle non-finite values.
Results may differ from a plain program's by a relative error of at most 0.00044.
Values may be sent and summed in bfloat16 or wider, within the bound.
No kernel may reach another device: no remote copies, remote signals or barrier semaphores. Data moves between devices by JAX's collectives and lax.ppermute only.
A program may use at most 64 MiB of HBM per device.

v0:
```python
import jax
import jax.numpy as jnp
from jax import lax
from jax.sharding import PartitionSpec as P

prior_count = 4.0


def local(embeddings, codes, rotation, codebook):
    rows = embeddings.shape[0]
    width = embeddings.shape[1]
    n_sub = codes.shape[1]
    sub_width = width // n_sub
    n_words = codebook.shape[0] * lax.axis_size("dp")
    full_book = lax.all_gather(codebook, "dp", axis=0, tiled=True)
    rotated = jnp.dot(embeddings, rotation, preferred_element_type=jnp.float32).astype(jnp.bfloat16)
    word_ids = jnp.arange(n_words, dtype=jnp.int32)
    block = 16
    recon_parts = []
    sum_parts = []
    count_parts = []
    for first in range(0, n_sub, block):
        lo_col = first * sub_width
        hi_col = (first + block) * sub_width
        onehot = (codes[:, first : first + block, None] == word_ids[None, None, :]).astype(
            jnp.bfloat16
        )
        book_group = full_book[:, lo_col:hi_col].reshape(n_words, block, sub_width)
        recon_group = jnp.einsum(
            "rgk,kgd->rgd", onehot, book_group, preferred_element_type=jnp.float32
        )
        recon_parts.append(recon_group.astype(jnp.bfloat16).reshape(rows, block * sub_width))
        rot_group = rotated[:, lo_col:hi_col].reshape(rows, block, sub_width)
        sum_group = jnp.einsum(
            "rgk,rgd->kgd", onehot, rot_group, preferred_element_type=jnp.float32
        )
        sum_parts.append(sum_group.reshape(n_words, block * sub_width))
        count_parts.append(jnp.sum(onehot, axis=0, dtype=jnp.float32).T)
    recon = jnp.concatenate(recon_parts, axis=1)
    sums = jnp.concatenate(sum_parts, axis=1)
    counts = jnp.concatenate(count_parts, axis=1)
    total_rows = rows * lax.axis_size("dp") * lax.axis_size("replica")
    owner_rows = width // lax.axis_size("dp")
    summed = lax.psum(
        lax.dot_general(
            embeddings, recon, (((0,), (0,)), ((), ())), preferred_element_type=jnp.float32
        ),
        ("dp", "replica"),
    )
    cross = lax.dynamic_slice_in_dim(summed, lax.axis_index("dp") * owner_rows, owner_rows, 0)
    cross = cross / total_rows
    part_sums, part_counts = (
        lax.psum_scatter(sums, "dp", scatter_dimension=0, tiled=True),
        lax.psum_scatter(counts, "dp", scatter_dimension=0, tiled=True),
    )
    word_sums, word_counts = lax.psum((part_sums, part_counts), "replica")
    spread_counts = jnp.repeat(word_counts, sub_width, axis=1)
    new_codebook = (word_sums + prior_count * codebook.astype(jnp.float32)) / (
        spread_counts + prior_count
    )
    return (new_codebook, cross)


def solution(mesh):
    in_specs = (
        P(("groups", "dp", "replica"), None),
        P(("groups", "dp", "replica"), None),
        P("groups", None),
        P(("groups", "dp"), None),
    )
    out_specs = (P(("groups", "dp"), None), P(("groups", "dp"), None))
    return jax.shard_map(local, mesh=mesh, in_specs=in_specs, out_specs=out_specs, check_vma=False)
```

profile of v0, /device:TPU:0, one launch (start us, length us, event | category | flops | bytes accessed | tf_op | source)
XLA Modules:
  0.0 262.2 jit_solution(9186591435815987085)
XLA Ops:
  8.1 1.1 fusion.67
  9.2 5.9 %convert_reduce_fusion.4 = (f32[16,256]{1,0:T(8,128)S(1)}, f32[16,256]{1,0:T(8,128)S(1)}) fusion(s32[1024,16]{0,1:T(8,128)S(1)} %get-tuple-element.17, s32[1024,16]{0,1:T(8,128)S(1)} %get-tuple-element.18), kind=kLoop, calls=%fused_computation.4 | loop fusion | flops 33546240 | bytes 163840 | tf_op jit(solution)/shard_map/reduce_sum | solution.py:38
  15.2 5.9 %convert_reduce_fusion.2 = (f32[16,256]{1,0:T(8,128)S(1)}, f32[16,256]{1,0:T(8,128)S(1)}) fusion(s32[1024,16]{0,1:T(8,128)S(1)} %get-tuple-element.15, s32[1024,16]{0,1:T(8,128)S(1)} %get-tuple-element.16), kind=kLoop, calls=%fused_computation.2 | loop fusion | flops 33546240 | bytes 163840 | tf_op jit(solution)/shard_map/reduce_sum | solution.py:38
  21.1 5.9 %convert_reduce_fusion = (f32[16,256]{1,0:T(8,128)S(1)}, f32[16,256]{1,0:T(8,128)S(1)}) fusion(s32[1024,16]{0,1:T(8,128)S(1)} %get-tuple-element.14, s32[1024,16]{0,1:T(8,128)S(1)} %get-tuple-element.19), kind=kLoop, calls=%fused_computation | loop fusion | flops 33546240 | bytes 163840 | tf_op jit(solution)/shard_map/reduce_sum | solution.py:38
  27.1 0.8 copy.39
  27.9 2.7 %convolution_convert_fusion = bf16[1024,768]{0,1:T(8,128)(2,1)S(1)} fusion(bf16[1024,768]{1,0:T(8,128)(2,1)S(1)} %copy-done, bf16[768,768]{1,0:T(8,128)(2,1)} %param.6), kind=kOutput, calls=%fused_computation.43 | convolution fusion | flops 1208745984 | bytes 4325376 | tf_op jit(solution)/shard_map/dot_general | solution.py:16
  30.7 5.6 %fusion.49 = f32[256,768]{0,1:T(8,128)S(1)} fusion(s32[1024,16]{0,1:T(8,128)S(1)} %get-tuple-element.18, bf16[1024,768]{0,1:T(8,128)(2,1)S(1)} %convolution_convert_fusion), kind=kOutput, calls=%fused_computation.63 | convolution fusion | flops 71303168 | bytes 458752 | tf_op jit(solution)/shard_map/rgk,rgd->kgd/dot_general | solution.py:34
  36.2 5.5 %fusion.51 = f32[256,768]{0,1:T(8,128)S(1)} fusion(f32[256,768]{0,1:T(8,128)S(1)} %fusion.49, s32[1024,16]{0,1:T(8,128)S(1)} %get-tuple-element.17, bf16[1024,768]{0,1:T(8,128)(2,1)S(1)} %convolution_convert_fusion), kind=kOutput, calls=%fused_computation.65 | convolution fusion | flops 71303168 | bytes 458752 | tf_op jit(solution)/shard_map/rgk,rgd->kgd/dot_general | solution.py:34
  41.7 5.5 %fusion.53 = f32[256,768]{0,1:T(8,128)S(1)} fusion(f32[256,768]{0,1:T(8,128)S(1)} %fusion.51, s32[1024,16]{0,1:T(8,128)S(1)} %get-tuple-element.16, bf16[1024,768]{0,1:T(8,128)(2,1)S(1)} %convolution_convert_fusion), kind=kOutput, calls=%fused_computation.67 | convolution fusion | flops 71303168 | bytes 458752 | tf_op jit(solution)/shard_map/rgk,rgd->kgd/dot_general | solution.py:34
  47.3 5.5 %fusion.55 = f32[256,768]{0,1:T(8,128)S(1)} fusion(f32[256,768]{0,1:T(8,128)S(1)} %fusion.53, s32[1024,16]{0,1:T(8,128)S(1)} %get-tuple-element.15, bf16[1024,768]{0,1:T(8,128)(2,1)S(1)} %convolution_convert_fusion), kind=kOutput, calls=%fused_computation.69 | convolution fusion | flops 71303168 | bytes 458752 | tf_op jit(solution)/shard_map/rgk,rgd->kgd/dot_general | solution.py:34
  52.8 5.5 %fusion.57 = f32[256,768]{0,1:T(8,128)S(1)} fusion(f32[256,768]{0,1:T(8,128)S(1)} %fusion.55, s32[1024,16]{0,1:T(8,128)S(1)} %get-tuple-element.19, bf16[1024,768]{0,1:T(8,128)(2,1)S(1)} %convolution_convert_fusion), kind=kOutput, calls=%fused_computation.71 | convolution fusion | flops 71303168 | bytes 458752 | tf_op jit(solution)/shard_map/rgk,rgd->kgd/dot_general | solution.py:34
  58.4 5.5 %fusion.59 = f32[256,768]{0,1:T(8,128)S(1)} fusion(f32[256,768]{0,1:T(8,128)S(1)} %fusion.57, s32[1024,16]{0,1:T(8,128)S(1)} %get-tuple-element.14, bf16[1024,768]{0,1:T(8,128)(2,1)S(1)} %convolution_convert_fusion), kind=kOutput, calls=%fused_computation.73 | convolution fusion | flops 71303168 | bytes 458752 | tf_op jit(solution)/shard_map/rgk,rgd->kgd/dot_general | solution.py:34
  63.9 1.2 copy.37
  65.2 19.5 %all_gather.3 = bf16[256,768]{1,0:T(8,128)(2,1)S(1)} all-gather(bf16[64,768]{1,0:T(8,128)(2,1)S(1)} %copy-done.1), channel_id=1, replica_groups=mesh['groups'=2,'dp'=4,'replica'=4] {'dp'}, dimensions={0}, use_global_device_ids=true | all-gather | bytes 491520 | tf_op jit(solution)/shard_map/all_gather | solution.py:15
  84.7 0.1 copy.29
  84.8 4.9 %fusion.47 = bf16[1024,768]{0,1:T(8,128)(2,1)} fusion(s32[1024,16]{0,1:T(8,128)S(1)} %get-tuple-element.18, bf16[256,128]{0,1:T(8,128)(2,1)S(1)} %copy.29), kind=kOutput, calls=%fused_computation.61 | convolution fusion | flops 71434240 | bytes 393216 | tf_op jit(solution)/shard_map/rgk,kgd->rgd/dot_general | solution.py:29
  90.3 4.9 %fusion.45 = bf16[1024,768]{0,1:T(8,128)(2,1)} fusion(bf16[1024,768]{0,1:T(8,128)(2,1)} %fusion.47, s32[1024,16]{0,1:T(8,128)S(1)} %get-tuple-element.17, bf16[256,128]{0,1:T(8,128)(2,1)S(1)} %copy.30), kind=kOutput, calls=%fused_computation.59 | convolution fusion | flops 71434240 | bytes 393216 | tf_op jit(solution)/shard_map/rgk,kgd->rgd/dot_general | solution.py:29
  95.2 4.9 %fusion.43 = bf16[1024,768]{0,1:T(8,128)(2,1)} fusion(bf16[1024,768]{0,1:T(8,128)(2,1)} %fusion.45, s32[1024,16]{0,1:T(8,128)S(1)} %get-tuple-element.16, bf16[256,128]{0,1:T(8,128)(2,1)S(1)} %copy.31), kind=kOutput, calls=%fused_computation.57 | convolution fusion | flops 71434240 | bytes 393216 | tf_op jit(solution)/shard_map/rgk,kgd->rgd/dot_general | solution.py:29
  100.1 4.9 %fusion.41 = bf16[1024,768]{0,1:T(8,128)(2,1)} fusion(bf16[1024,768]{0,1:T(8,128)(2,1)} %fusion.43, s32[1024,16]{0,1:T(8,128)S(1)} %get-tuple-element.15, bf16[256,128]{0,1:T(8,128)(2,1)S(1)} %copy.32), kind=kOutput, calls=%fused_computation.55 | convolution fusion | flops 71434240 | bytes 393216 | tf_op jit(solution)/shard_map/rgk,kgd->rgd/dot_general | solution.py:29
  105.0 4.9 %fusion.39 = bf16[1024,768]{0,1:T(8,128)(2,1)} fusion(bf16[1024,768]{0,1:T(8,128)(2,1)} %fusion.41, s32[1024,16]{0,1:T(8,128)S(1)} %get-tuple-element.19, bf16[256,128]{0,1:T(8,128)(2,1)S(1)} %copy.33), kind=kOutput, calls=%fused_computation.53 | convolution fusion | flops 71434240 | bytes 393216 | tf_op jit(solution)/shard_map/rgk,kgd->rgd/dot_general | solution.py:29
  109.9 4.9 %fusion.37 = bf16[1024,768]{0,1:T(8,128)(2,1)} fusion(bf16[1024,768]{0,1:T(8,128)(2,1)} %fusion.39, s32[1024,16]{0,1:T(8,128)S(1)} %get-tuple-element.14, bf16[256,128]{0,1:T(8,128)(2,1)S(1)} %copy.34), kind=kOutput, calls=%fused_computation.51 | convolution fusion | flops 71434240 | bytes 393216 | tf_op jit(solution)/shard_map/rgk,kgd->rgd/dot_general | solution.py:29
  114.9 4.2 %convolution_bitcast_fusion = f32[768,768]{0,1:T(8,128)} fusion(bf16[1024,768]{0,1:T(8,128)(2,1)} %fusion.37, bf16[1024,768]{1,0:T(8,128)(2,1)S(1)} %copy-done), kind=kOutput, calls=%fused_computation.42 | convolution fusion | flops 1207959552 | bytes 5505024 | tf_op jit(solution)/shard_map/dot_general | solution.py:45
  119.1 0.2 copy.28
  119.3 0.8 copy.40
  120.2 10.9 %psum.22 = f32[64,96]{0,1:T(8,128)S(1)} all-reduce(f32[64,96]{0,1:T(8,128)S(1)} %copy.40), channel_id=1, replica_groups=mesh['groups'=2,'dp'=4,'replica'=4] {'replica'}, use_global_device_ids=true, to_apply=%region_9.0 | all-reduce | flops 6144 | bytes 49152 | tf_op jit(solution)/shard_map/psum | solution.py:56
  131.2 1.9 copy.38
  133.1 86.4 %all-reduce.5.cloned.1.call-done = f32[768,768]{0,1:T(8,128)} async-done(((f32[768,768]{0,1:T(8,128)}), f32[768,768]{0,1:T(8,128)}) %all-reduce.5.cloned.1.call-update) | async-done | bytes 2359312 | tf_op jit(solution)/shard_map/psum | solution.py:44
  219.4 1.5 dynamic-slice_multiply_fusion
  221.0 1.1 copy.36
  222.1 30.9 %all-reduce.3.cloned.1.call-done = f32[64,768]{0,1:T(8,128)} async-done(((f32[64,768]{0,1:T(8,128)}), f32[64,768]{0,1:T(8,128)}) %all-reduce.3.cloned.1.call-update) | async-done | bytes 196624 | tf_op jit(solution)/shard_map/psum | solution.py:56
  252.9 1.1 bitcast_divide_fusion
  254.0 0.8 copy.35
  (27 shorter events, 0.9 us)
Async XLA Ops:
  8.0 19.9 %copy-start = (bf16[1024,768]{1,0:T(8,128)(2,1)S(1)}, bf16[1024,768]{1,0:T(8,128)(2,1)}, u32[]{:S(2)}) copy-start(bf16[1024,768]{1,0:T(8,128)(2,1)} %param.4) | copy-start | bytes 4718596
  8.0 111.3 %reduce-scatter.9.cloned.1.call-start = ((), (), s32[]{:S(2)}) async-start(), calls=%async_computation.5 | async-start | bytes 163840
  27.9 103.3 %reduce-scatter.7.cloned.1.call-start = ((), (), s32[]{:S(2)}) async-start(), calls=%async_computation.4 | async-start | bytes 983040
  63.9 1.3 copy-start.1
  65.1 154.3 %all-reduce.5.cloned.1.call-start = ((), (), s32[]{:S(2)}) async-start(), calls=%async_computation.3 | async-start | bytes 4718592 | tf_op jit(solution)/shard_map/psum | solution.py:44
  119.1 133.8 %all-reduce.3.cloned.1.call-start = ((), (), s32[]{:S(2)}) async-start(), calls=%async_computation.2 | async-start | bytes 786432 | tf_op jit(solution)/shard_map/psum | solution.py:56
Sparse Core Ops, SparseCore 0:
  28.0 21.9 reduce-scatter.8
  65.2 28.5 reduce-scatter.6
Sparse Core Ops, SparseCore 1:
  119.2 100.2 all-reduce.4
  221.8 31.1 all-reduce.2
where the time goes:
time: 263 us; the launch traced here: 262 us
  waiting for transfers between devices  117 us (44%)
  matrix products  69.6 us (26%)
  blocking collectives  30.4 us (12%)
  other arithmetic  20.4 us (8%)
  between operations  15.7 us (6%)
  local copies, waits for them, and re-layouts  8.57 us (3%)
    psum x1, waiting for transfers between devices, local(): lax.psum(lax.dot_general(embeddings, recon, (((0,), (0,)), ((), ())), pre...  86.4 us
    dot_general x6, matrix products, local(): jnp.einsum('rgk,rgd->kgd', onehot, rot_group, preferred_element_type=jnp....  33.2 us
    psum x1, waiting for transfers between devices, local(): word_sums, word_counts = lax.psum((part_sums, part_counts), 'replica')  30.9 us
    dot_general x6, matrix products, local(): jnp.einsum('rgk,kgd->rgd', onehot, book_group, preferred_element_type=jnp...  29.4 us
    all_gather x1, blocking collectives, local(): full_book = lax.all_gather(codebook, 'dp', axis=0, tiled=True)  19.5 us
    reduce_sum x3, other arithmetic, local(): count_parts.append(jnp.sum(onehot, axis=0, dtype=jnp.float32).T)  17.8 us
    psum x1, blocking collectives, local(): word_sums, word_counts = lax.psum((part_sums, part_counts), 'replica')  10.9 us
    unnamed x16, local copies, waits for them, and re-layouts  6.72 us
  transfers between devices with their start and end apart: 4, of which 2 were waited for; matrix products, arithmetic and copies ran while one was open for 29% of the time, Pallas kernels for 0%

commit v1 on v0

v1 whole, which is shorter than its diff:
```python
import jax
import jax.numpy as jnp
from jax import lax
from jax.experimental import pallas as pl
from jax.experimental.pallas import tpu as pltpu
from jax.sharding import PartitionSpec as P

prior_count = 4.0
lane = 128
fine = 64
pack = 4
level = 32000.0
octave = 8.0
pad = 16

f32, bf16, i32, i16 = jnp.float32, jnp.bfloat16, jnp.int32, jnp.int16
nt = (((1,), (1,)), ((), ()))


def call(kernel, outs, args, scratch, name):
    return pl.pallas_call(
        kernel,
        out_shape=outs,
        scratch_shapes=scratch,
        compiler_params=pltpu.CompilerParams(vmem_limit_bytes=48 << 20),
        name=name,
    )(*args)


def my_half(width):
    core = lax.axis_index("replica") % 2
    return core, pl.ds(pl.multiple_of(core * width, lane), width)


def quantize(x):
    top = jnp.maximum(jnp.max(jnp.abs(x), axis=0, keepdims=True), 1e-30)
    power = jnp.ceil(jnp.log2(top) * octave)
    terms = jnp.round(x * (level * jnp.exp2(power * (-1.0 / octave)))).astype(i32)
    powers = jnp.broadcast_to(power.astype(i32), (pad, x.shape[1]))
    return jnp.concatenate([terms, powers], axis=0).astype(i16)


def dequantize(q):
    rows = q.shape[0] - pad
    power = q[rows:].astype(f32)[:1]
    return q[:rows].astype(f32) * (jnp.exp2(power * (1.0 / octave)) * (1.0 / level))


def sums_kernel(shape, e0, e1, c0, c1, rot, *rest):
    rows, half, n_sub, n_words, n_out = shape
    outs, (codes_out, turned, rt, lhs, rhs, total) = rest[:n_out], rest[n_out:]
    core, cols = my_half(half)
    subs = n_sub // 2
    for i, c in enumerate((c0, c1)):
        turned[...] = c[...].T
        codes_out[:, i * rows : (i + 1) * rows] = turned[pl.ds(pl.multiple_of(core * subs, 16), subs), :]
    rot_t = rot[:, cols].T
    for i, e in enumerate((e0, e1)):
        rt[:, i * rows : (i + 1) * rows] = lax.dot_general(
            rot_t, e[...], nt, preferred_element_type=f32
        ).astype(bf16)
    width = 2 * rows
    coarse = n_words // fine
    groups = subs // pack
    block = groups * 8 + 16
    row8 = lax.broadcasted_iota(i32, (8, width), 0)
    rowf = lax.broadcasted_iota(i32, (fine, width), 0).astype(bf16)
    out_lane = lax.broadcasted_iota(i32, (8, pack * fine), 1)
    for g in range(groups):
        b = g % 2
        high = []
        for s in range(pack):
            code = jnp.broadcast_to(codes_out[g * pack + s : g * pack + s + 1, :], (8, width))
            high.append(code // fine)
            low = (code % fine).astype(f32)
            low = jnp.concatenate([low] * (fine // 8), axis=0).astype(bf16)
            rhs[b, s * fine : (s + 1) * fine, :] = jnp.where(low == rowf, 1.0, 0.0).astype(bf16)
        for p in range(pack // 2):
            pair = jnp.concatenate([high[2 * p], high[2 * p + 1]], axis=0).astype(f32).astype(bf16)
            r = rt[g * pack * 8 + p * 16 : g * pack * 8 + (p + 1) * 16, :]
            for h in range(coarse):
                at = h * pack * 8 + p * 16
                lhs[b, at : at + 16, :] = jnp.where(pair == h, r, 0.0).astype(bf16)
        ones = []
        for p in range(pack // 2):
            both = jnp.where(row8 < coarse, high[2 * p], high[2 * p + 1])
            ones.append(jnp.where(both == row8 % coarse, 1.0, 0.0))
        base = coarse * pack * 8
        lhs[b, base : base + 16, :] = jnp.concatenate(ones, axis=0).astype(bf16)
        got = lax.dot_general(lhs[b], rhs[b], nt, preferred_element_type=f32)
        for h in range(coarse):
            kept = got[h * 32 : h * 32 + 8]
            for s in range(1, pack):
                kept = jnp.where(out_lane // fine == s, got[h * 32 + s * 8 : h * 32 + s * 8 + 8], kept)
            total[h * block + g * 8 : h * block + g * 8 + 8, :] = kept
        row = lax.broadcasted_iota(i32, (16, pack * fine), 0)
        lanes = lax.broadcasted_iota(i32, (16, pack * fine), 1)
        counts = jnp.where(row // coarse == lanes // fine, got[base : base + 16], 0.0)
        counts = counts[:8] + counts[8:]
        counts = counts[:coarse] + counts[coarse:]
        for h in range(coarse):
            at = h * block + groups * 8 + g
            total[at : at + 1, :] = counts[h : h + 1]
    zero = jnp.zeros((16 - groups, pack * fine), f32)
    for h in range(coarse):
        total[h * block + groups * 8 + groups : (h + 1) * block, :] = zero
    if n_out == 1:
        outs[0][...] = total[...]
    else:
        me = lax.axis_index("dp")
        for k in range(n_out):
            to = lax.rem(me + k, n_out)
            outs[k][...] = total[pl.ds(pl.multiple_of(to * block, 16), block), :]


def cross_kernel(shape, e0, e1, codes, *rest):
    rows, half, n_words, n_book, n_out = shape
    books, outs, (book, recon, total) = rest[:n_book], rest[n_book : n_book + n_out], rest[n_book + n_out :]
    me = lax.axis_index("dp")
    owned = n_words // n_book
    for k in range(n_book):
        source = lax.rem(me + n_book - k, n_book) if n_book > 1 else 0
        book[pl.ds(pl.multiple_of(source * owned, owned), owned), :] = books[k][...].astype(f32)
    table = book[...].T
    width = 2 * rows
    for p in range(half // 16):
        made = []
        for s in (2 * p, 2 * p + 1):
            code = jnp.broadcast_to(codes[s : s + 1, :], (8, width))
            parts = []
            for at in range(0, width, lane):
                c = code[:, at : at + lane]
                index = c % lane
                value = None
                for t in range(0, n_words, lane):
                    found = jnp.take_along_axis(
                        table[s * 8 : s * 8 + 8, t : t + lane], index, axis=1, mode="promise_in_bounds"
                    )
                    value = found if value is None else jnp.where(c >= t, found, value)
                parts.append(value)
            made.append(jnp.concatenate(parts, axis=1))
        recon[p * 16 : (p + 1) * 16, :] = jnp.concatenate(made, axis=0).astype(bf16)
    turned = jnp.dot(recon[:, :rows], e0[...], preferred_element_type=f32)
    turned += jnp.dot(recon[:, rows:], e1[...], preferred_element_type=f32)
    if n_out == 1:
        outs[0][...] = turned.T
    else:
        total[...] = turned.T
        block = total.shape[0] // n_out
        for k in range(n_out):
            to = lax.rem(me + k, n_out)
            terms = total[pl.ds(pl.multiple_of(to * block, 16), block), :]
            outs[k][...] = quantize(terms) if k else terms


def add_cross_kernel(own, *rest):
    total = own[...]
    for q in rest[:-1]:
        total += dequantize(q[...])
    rest[-1][...] = quantize(total)


def add_sums_kernel(*refs):
    total = refs[0][...]
    for r in refs[1:-1]:
        total += r[...]
    refs[-1][...] = total


def finish_cross_kernel(scale, q0, q1, p0, p1, out):
    half = q0.shape[1]
    core, mine = my_half(half)
    other = pl.ds(pl.multiple_of((1 - core) * half, lane), half)
    out[:, mine] = (dequantize(q0[...]) + dequantize(q1[...])) * scale
    out[:, other] = (dequantize(p0[...]) + dequantize(p1[...])) * scale


def finish_book_kernel(q0, q1, p0, p1, codebook, out, turned):
    half = codebook.shape[1] // 2
    core, mine = my_half(half)
    other = pl.ds(pl.multiple_of((1 - core) * half, lane), half)
    groups = half // (8 * pack)
    for cols, a, b in ((mine, q0, q1), (other, p0, p1)):
        s = a[...] + b[...]
        for g in range(groups):
            sums = s[g * 8 : g * 8 + 8]
            counts = jnp.broadcast_to(s[groups * 8 + g : groups * 8 + g + 1], sums.shape)
            for j in range(pack):
                at = (g * pack + j) * 8
                cut = slice(j * fine, (j + 1) * fine)
                turned[at : at + 8, :] = jnp.concatenate([sums[:, cut], counts[:, cut]], axis=1)
        t = turned[...].T
        old = codebook[:, cols].astype(f32)
        out[:, cols] = (t[:fine] + prior_count * old) / (t[fine:] + prior_count)


def local(embeddings, codes, rotation, codebook):
    rows, width = embeddings.shape
    n_sub = codes.shape[1]
    half = width // 2
    n = lax.axis_size("dp")
    replicas = lax.axis_size("replica")
    n_words = codebook.shape[0] * n
    owned = codebook.shape[0]
    out_rows = width // n
    core = lax.axis_index("replica") % 2
    direct = owned == fine and replicas == 4

    def swap(x, bit):
        return lax.ppermute(x, "replica", [(i, i ^ bit) for i in range(replicas)])

    def send(x, k):
        return lax.ppermute(x, "dp", [(i, (i + k) % n) for i in range(n)])

    book = lax.dynamic_slice_in_dim(codebook, core * half, half, 1)
    if direct:
        books = [book] + [send(book, k) for k in range(1, n)]
    else:
        books = [lax.all_gather(book, "dp", axis=0, tiled=True)]
    e1 = swap(embeddings, 1)
    c1 = swap(codes, 1)
    n_out = n if direct else 1
    coarse = n_words // fine
    groups = n_sub // 2 // pack
    block = groups * 8 + 16
    lhs_rows = coarse * pack * 8 + 16
    *sums, codes_t = call(
        lambda *refs: sums_kernel((rows, half, n_sub, n_words, n_out), *refs),
        [jax.ShapeDtypeStruct((coarse * block // n_out, pack * fine), f32)] * n_out
        + [jax.ShapeDtypeStruct((n_sub // 2, 2 * rows), i32)],
        (embeddings, e1, codes, c1, rotation),
        [
            pltpu.VMEM((n_sub, rows), i32),
            pltpu.VMEM((half, 2 * rows), bf16),
            pltpu.VMEM((2, lhs_rows, 2 * rows), bf16),
            pltpu.VMEM((2, pack * fine, 2 * rows), bf16),
            pltpu.VMEM((coarse * block, pack * fine), f32),
        ],
        "codeword_sums",
    )
    if direct:
        cross_outs = [jax.ShapeDtypeStruct((out_rows, half), f32)]
        cross_outs += [jax.ShapeDtypeStruct((out_rows + pad, half), i16)] * (n - 1)
    else:
        cross_outs = [jax.ShapeDtypeStruct((width, half), f32)]
    cross = call(
        lambda *refs: cross_kernel((rows, half, n_words, len(books), n_out), *refs),
        cross_outs,
        (embeddings, e1, codes_t, *books),
        [
            pltpu.VMEM((n_words, half), f32),
            pltpu.VMEM((half, 2 * rows), bf16),
            pltpu.VMEM((width, half), f32),
        ],
        "cross_terms",
    )
    scale = 1.0 / (rows * n * replicas)
    if not direct:
        return plain_finish(sums[0], cross[0], codebook, n_words, scale, swap)

    sums = [sums[0]] + [send(sums[k], k) for k in range(1, n)]
    cross = [cross[0]] + [send(cross[k], k) for k in range(1, n)]
    q = call(add_sums_kernel, jax.ShapeDtypeStruct((block, pack * fine), f32), sums, [], "add_sums")
    q1 = swap(q, 2)
    p, p1 = swap(q, 1), swap(q1, 1)
    new_codebook = call(
        finish_book_kernel,
        jax.ShapeDtypeStruct(codebook.shape, f32),
        (q, q1, p, p1, codebook),
        [pltpu.VMEM((half, lane), f32)],
        "finish_book",
    )
    t = call(add_cross_kernel, jax.ShapeDtypeStruct((out_rows + pad, half), i16), cross, [], "add_cross")
    t1 = swap(t, 2)
    u, u1 = swap(t, 1), swap(t1, 1)
    cross_out = call(
        lambda *refs: finish_cross_kernel(scale, *refs),
        jax.ShapeDtypeStruct((out_rows, width), f32),
        (t, t1, u, u1),
        [],
        "finish_cross",
    )
    return new_codebook, cross_out


def plain_finish(sums, cross, codebook, n_words, scale, swap):
    half = cross.shape[1]
    coarse = n_words // fine
    groups = half // (8 * pack)
    sums = sums.reshape(coarse, groups * 8 + 16, pack * fine)
    counts = sums[:, groups * 8 : groups * 8 + groups].reshape(coarse, groups, pack, fine)
    counts = counts.transpose(0, 3, 1, 2).reshape(n_words, groups * pack)
    sums = sums[:, : groups * 8].reshape(coarse, groups, 8, pack, fine)
    sums = sums.transpose(0, 4, 1, 3, 2).reshape(n_words, half)
    parts = []
    for x in (sums, counts, cross):
        x = lax.psum_scatter(x, "dp", scatter_dimension=0, tiled=True)
        bit = 2
        while bit < lax.axis_size("replica"):
            x = x + swap(x, bit)
            bit *= 2
        y = swap(x, 1)
        first = lax.axis_index("replica") % 2 == 0
        parts.append(jnp.where(first, jnp.concatenate([x, y], 1), jnp.concatenate([y, x], 1)))
    sums, counts, cross = parts
    spread = jnp.repeat(counts, 8, axis=1)
    new_codebook = (sums + prior_count * codebook.astype(f32)) / (spread + prior_count)
    return new_codebook, cross * scale


def solution(mesh):
    in_specs = (
        P(("groups", "dp", "replica"), None),
        P(("groups", "dp", "replica"), None),
        P("groups", None),
        P(("groups", "dp"), None),
    )
    out_specs = (P(("groups", "dp"), None), P(("groups", "dp"), None))
    return jax.shard_map(local, mesh=mesh, in_specs=in_specs, out_specs=out_specs, check_vma=False)
```

time: 263 us -> 58.8 us (0.22)
  waiting for transfers between devices: 117 us -> 21.3 us
  matrix products: 69.6 us -> 0 us
  blocking collectives: 30.4 us -> 0 us
  other arithmetic: 20.4 us -> 0 us
  starting transfers between devices: 0.17 us -> 17.2 us
  between operations: 15.7 us -> 0.71 us
  Pallas kernels: 0 us -> 14.7 us
  local copies, waits for them, and re-layouts: 8.57 us -> 4.67 us
    psum x2 -> x0, waiting for transfers between devices: 117 us -> none  [the longest x1 86.4 us: local(): lax.psum(lax.dot_general(embeddings, recon, (((0,), (0,)), ((), ())), pre...]
    dot_general x14 -> x0, matrix products: 69.6 us -> none  [the longest x6 33.2 us: local(): jnp.einsum('rgk,rgd->kgd', onehot, rot_group, preferred_element_type=jnp....]
    ppermute x0 -> x17, waiting for transfers between devices: none -> 21.3 us  [the longest x9 17.2 us: send(): return lax.ppermute(x, 'dp', [(i, (i + k) % n) for i in range(n)])]
    all_gather x1 -> x0, blocking collectives: 19.5 us -> none  [local(): full_book = lax.all_gather(codebook, 'dp', axis=0, tiled=True)]
    reduce_sum x3 -> x0, other arithmetic: 17.8 us -> none  [local(): count_parts.append(jnp.sum(onehot, axis=0, dtype=jnp.float32).T)]
    ppermute x0 -> x17, starting transfers between devices: none -> 17.2 us  [the longest x9 12.9 us: send(): return lax.ppermute(x, 'dp', [(i, (i + k) % n) for i in range(n)])]
    pallas_call x0 -> x6, Pallas kernels: none -> 14.7 us  [call(): pl.pallas_call(kernel, out_shape=outs, scratch_shapes=scratch, compiler_p...]
    psum x1 -> x0, blocking collectives: 10.9 us -> none  [local(): word_sums, word_counts = lax.psum((part_sums, part_counts), 'replica')]
  transfers between devices with their start and end apart: 4 -> 17, of which waited for: 2 -> 5; matrix products, arithmetic and copies ran while one was open for 29% -> 3% of each run, Pallas kernels for 0% -> 17%
where the time goes in v1:
time: 58.8 us; the launch traced here: 58.6 us
  waiting for transfers between devices  21.3 us (36%)
  starting transfers between devices  17.2 us (29%)
  Pallas kernels  14.7 us (25%)
  local copies, waits for them, and re-layouts  4.67 us (8%)
  between operations  0.71 us (1%)
    ppermute x9, waiting for transfers between devices, send(): return lax.ppermute(x, 'dp', [(i, (i + k) % n) for i in range(n)])  17.2 us
    pallas_call x6, Pallas kernels, call(): pl.pallas_call(kernel, out_shape=outs, scratch_shapes=scratch, compiler_p...  14.7 us
    ppermute x9, starting transfers between devices, send(): return lax.ppermute(x, 'dp', [(i, (i + k) % n) for i in range(n)])  12.9 us
    ppermute x8, starting transfers between devices, swap(): return lax.ppermute(x, 'replica', [(i, i ^ bit) for i in range(replicas)])  4.29 us
    ppermute x8, waiting for transfers between devices, swap(): return lax.ppermute(x, 'replica', [(i, i ^ bit) for i in range(replicas)])  4.11 us
    unnamed x7, local copies, waits for them, and re-layouts  3.87 us
  transfers between devices with their start and end apart: 17, of which 5 were waited for; matrix products, arithmetic and copies ran while one was open for 3% of the time, Pallas kernels for 17%

profile of v1, /device:TPU:0, one launch (start us, length us, event | category | flops | bytes accessed | tf_op | source)
XLA Modules:
  0.0 58.6 jit_solution(13382874445287909395)
XLA Ops:
  0.6 0.5 collective-permute-start
  1.1 1.2 %copy.7.refs_2_ = s32[1024,96]{1,0:T(8,128)S(1)} copy(s32[1024,96]{0,1:T(8,128)} %param.5) | data formatting | bytes 786432 | tf_op args[1]
  2.3 0.1 collective-permute-start.1
  2.5 0.8 %constant_dynamic-slice_fusion.refs_3_ = bf16[64,384]{1,0:T(8,128)(2,1)S(1)} fusion(bf16[64,768]{1,0:T(8,128)(2,1)} %codebook.1, s32[]{:T(128)S(6)} %select_n.11), kind=kLoop, calls=%fused_computation | loop fusion | bytes 98308 | tf_op jit(solution)/shard_map/dynamic_slice | solution.py:215
  3.3 3.0 %collective-permute-start.8 = (bf16[64,384]{1,0:T(8,128)(2,1)S(1)}, bf16[64,384]{1,0:T(8,128)(2,1)S(1)}, u32[]{:S(2)}, u32[]{:S(2)}) collective-permute-start(bf16[64,384]{1,0:T(8,128)(2,1)S(1)} %constant_dynamic-slice_fusion.refs_3_), channel_id=1, source_target_pairs={{0,4},{4,8},{8,12},{12,0},{1,5},{5,9},{9,13},{13,1},{2,6},{6,10},{... | collective-permute-start | bytes 147464 | tf_op jit(solution)/shard_map/ppermute | solution.py:213
  6.3 2.6 %collective-permute-start.9 = (bf16[64,384]{1,0:T(8,128)(2,1)S(1)}, bf16[64,384]{1,0:T(8,128)(2,1)S(1)}, u32[]{:S(2)}, u32[]{:S(2)}) collective-permute-start(bf16[64,384]{1,0:T(8,128)(2,1)S(1)} %constant_dynamic-slice_fusion.refs_3_), channel_id=1, source_target_pairs={{0,8},{4,12},{8,0},{12,4},{1,9},{5,13},{9,1},{13,5},{2,10},{6,14},... | collective-permute-start | bytes 147464 | tf_op jit(solution)/shard_map/ppermute | solution.py:213
  8.9 1.3 %collective-permute-start.10 = (bf16[64,384]{1,0:T(8,128)(2,1)S(1)}, bf16[64,384]{1,0:T(8,128)(2,1)S(1)}, u32[]{:S(2)}, u32[]{:S(2)}) collective-permute-start(bf16[64,384]{1,0:T(8,128)(2,1)S(1)} %constant_dynamic-slice_fusion.refs_3_), channel_id=1, source_target_pairs={{0,12},{4,0},{8,4},{12,8},{1,13},{5,1},{9,5},{13,9},{2,14},{6,2},{... | collective-permute-start | bytes 147464 | tf_op jit(solution)/shard_map/ppermute | solution.py:213
  10.2 0.0 collective-permute-done.1.refs_3_
  10.2 0.0 collective-permute-done.refs_1_
  10.2 1.4 %copy-done = bf16[1024,768]{1,0:T(8,128)(2,1)S(1)} copy-done((bf16[1024,768]{1,0:T(8,128)(2,1)S(1)}, bf16[1024,768]{1,0:T(8,128)(2,1)}, u32[]{:S(2)}) %copy-start) | copy-done | bytes 1572888
  11.7 1.3 %copy-done.1 = bf16[768,768]{1,0:T(8,128)(2,1)S(1)} copy-done((bf16[768,768]{1,0:T(8,128)(2,1)S(1)}, bf16[768,768]{1,0:T(8,128)(2,1)}, u32[]{:S(2)}) %copy-start.1) | copy-done | bytes 1179672
  12.9 9.0 %codeword_sums.1 = (f32[112,256]{1,0:T(8,128)S(1)}, f32[112,256]{1,0:T(8,128)S(1)}, f32[112,256]{1,0:T(8,128)S(1)}, f32[112,256]{1,0:T(8,128)S(1)}, s32[48,2048]{1,0:T(8,128)S(1)}) custom-call(bf16[1024,768]{1,0:T(8,128)(2,1)S(1)} %copy-done, bf16[1024,768]{1,0:T(8,128)(2,1)S(1)} %collective-permute-done.refs_1_, s32[1024,96]{1,0:T(8,128)S(1)} %copy.7.refs_2_, ...), custom_call_target="tpu_custom_call" | custom-call | tf_op jit(solution)/shard_map/codeword_sums/pallas_call | solution.py:21
  22.0 0.0 collective-permute-done.8.refs_4_
  22.0 3.5 %cross_terms.1 = (f32[192,384]{1,0:T(8,128)S(1)}, s16[208,384]{1,0:T(8,128)(2,1)S(1)}, s16[208,384]{1,0:T(8,128)(2,1)S(1)}, s16[208,384]{1,0:T(8,128)(2,1)S(1)}) custom-call(bf16[1024,768]{1,0:T(8,128)(2,1)S(1)} %copy-done, bf16[1024,768]{1,0:T(8,128)(2,1)S(1)} %collective-permute-done.refs_1_, s32[48,2048]{1,0:T(8,128)S(1)} %get-tuple-element.15.refs_2_, ...), custom_call_target="tpu_custom_call" | custom-call | tf_op jit(solution)/shard_map/cross_terms/pallas_call | solution.py:21
  25.5 0.0 copy-start.2
  25.5 0.7 %collective-permute-start.11 = (s16[208,384]{1,0:T(8,128)(2,1)S(1)}, s16[208,384]{1,0:T(8,128)(2,1)S(1)}, u32[]{:S(2)}, u32[]{:S(2)}) collective-permute-start(s16[208,384]{1,0:T(8,128)(2,1)S(1)} %get-tuple-element.17), channel_id=1, source_target_pairs={{0,4},{4,8},{8,12},{12,0},{1,5},{5,9},{9,13},{13,1},{2,6},{6,10},{... | collective-permute-start | bytes 479240 | tf_op jit(solution)/shard_map/ppermute | solution.py:213
  26.2 0.3 collective-permute-start.12
  26.6 2.8 %collective-permute-start.13 = (s16[208,384]{1,0:T(8,128)(2,1)S(1)}, s16[208,384]{1,0:T(8,128)(2,1)S(1)}, u32[]{:S(2)}, u32[]{:S(2)}) collective-permute-start(s16[208,384]{1,0:T(8,128)(2,1)S(1)} %get-tuple-element.19), channel_id=1, source_target_pairs={{0,12},{4,0},{8,4},{12,8},{1,13},{5,1},{9,5},{13,9},{2,14},{6,2},{... | collective-permute-start | bytes 479240 | tf_op jit(solution)/shard_map/ppermute | solution.py:213
  29.4 0.6 collective-permute-start.2
  29.9 1.5 %collective-permute-start.3 = (f32[112,256]{1,0:T(8,128)S(1)}, f32[112,256]{1,0:T(8,128)S(1)}, u32[]{:S(2)}, u32[]{:S(2)}) collective-permute-start(f32[112,256]{1,0:T(8,128)S(1)} %get-tuple-element.13), channel_id=1, source_target_pairs={{0,8},{4,12},{8,0},{12,4},{1,9},{5,13},{9,1},{13,5},{2,10},{6,14},... | collective-permute-start | bytes 344072 | tf_op jit(solution)/shard_map/ppermute | solution.py:213
  31.4 3.0 %collective-permute-done.11.rest_0_ = s16[208,384]{1,0:T(8,128)(2,1)S(1)} collective-permute-done((s16[208,384]{1,0:T(8,128)(2,1)S(1)}, s16[208,384]{1,0:T(8,128)(2,1)S(1)}, u32[]{:S(2)}, u32[]{:S(2)}) %collective-permute-start.11) | collective-permute-done | bytes 159776 | tf_op jit(solution)/shard_map/ppermute | solution.py:213
  34.4 8.4 %collective-permute-done.12.rest_1_ = s16[208,384]{1,0:T(8,128)(2,1)S(1)} collective-permute-done((s16[208,384]{1,0:T(8,128)(2,1)S(1)}, s16[208,384]{1,0:T(8,128)(2,1)S(1)}, u32[]{:S(2)}, u32[]{:S(2)}) %collective-permute-start.12) | collective-permute-done | bytes 159776 | tf_op jit(solution)/shard_map/ppermute | solution.py:213
  42.8 0.2 add_cross.1.refs_0_
  43.0 1.6 %collective-permute-start.14 = (s16[208,384]{1,0:T(8,128)(2,1)S(1)}, s16[208,384]{1,0:T(8,128)(2,1)S(1)}, u32[]{:S(2)}, u32[]{:S(2)}) collective-permute-start(s16[208,384]{1,0:T(8,128)(2,1)S(1)} %add_cross.1.refs_0_), channel_id=1, source_target_pairs={{0,2},{1,3},{2,0},{3,1},{4,6},{5,7},{6,4},{7,5},{8,10},{9,11},{10,... | collective-permute-start | bytes 479240 | tf_op jit(solution)/shard_map/ppermute | solution.py:210
  44.6 5.8 %collective-permute-done.3.refs_2_ = f32[112,256]{1,0:T(8,128)S(1)} collective-permute-done((f32[112,256]{1,0:T(8,128)S(1)}, f32[112,256]{1,0:T(8,128)S(1)}, u32[]{:S(2)}, u32[]{:S(2)}) %collective-permute-start.3) | collective-permute-done | bytes 114720 | tf_op jit(solution)/shard_map/ppermute | solution.py:213
  50.4 1.6 %collective-permute-start.5 = (f32[112,256]{1,0:T(8,128)S(1)}, f32[112,256]{1,0:T(8,128)S(1)}, u32[]{:S(2)}, u32[]{:S(2)}) collective-permute-start(f32[112,256]{1,0:T(8,128)S(1)} %add_sums.1.q0), channel_id=1, source_target_pairs={{0,2},{1,3},{2,0},{3,1},{4,6},{5,7},{6,4},{7,5},{8,10},{9,11},{10,... | collective-permute-start | bytes 344072 | tf_op jit(solution)/shard_map/ppermute | solution.py:210
  52.0 0.5 collective-permute-start.16
  52.5 0.0 collective-permute-start.6
  52.5 2.8 %collective-permute-done.5.q1 = f32[112,256]{1,0:T(8,128)S(1)} collective-permute-done((f32[112,256]{1,0:T(8,128)S(1)}, f32[112,256]{1,0:T(8,128)S(1)}, u32[]{:S(2)}, u32[]{:S(2)}) %collective-permute-start.5) | collective-permute-done | bytes 114720 | tf_op jit(solution)/shard_map/ppermute | solution.py:210
  55.3 1.3 %collective-permute-done.7.p1 = f32[112,256]{1,0:T(8,128)S(1)} collective-permute-done((f32[112,256]{1,0:T(8,128)S(1)}, f32[112,256]{1,0:T(8,128)S(1)}, u32[]{:S(2)}, u32[]{:S(2)}) %collective-permute-start.7) | collective-permute-done | bytes 114720 | tf_op jit(solution)/shard_map/ppermute | solution.py:210
  56.6 1.0 %finish_book.1 = f32[64,768]{1,0:T(8,128)} custom-call(f32[112,256]{1,0:T(8,128)S(1)} %add_sums.1.q0, f32[112,256]{1,0:T(8,128)S(1)} %collective-permute-done.5.q1, f32[112,256]{1,0:T(8,128)S(1)} %collective-permute-done.6.p0, f32[112,256]{1,0:T(8,128)S(1)} %collective-permute-done.7.p1, bf16[64,768]{1,0:T(8,128)(2,1)S(1)} %copy-done.2), custom_call_target="tpu_custom_call" | custom-call | tf_op jit(solution)/shard_map/finish_book/pallas_call | solution.py:21
  57.6 1.0 %finish_cross.1 = f32[192,768]{1,0:T(8,128)} custom-call(s16[208,384]{1,0:T(8,128)(2,1)S(1)} %add_cross.1.refs_0_, s16[208,384]{1,0:T(8,128)(2,1)S(1)} %collective-permute-done.14.refs_1_, s16[208,384]{1,0:T(8,128)(2,1)S(1)} %collective-permute-done.15.refs_2_, s16[208,384]{1,0:T(8,128)(2,1)S(1)} %collective-permute-done.16.refs_3_), custom_call_target="tpu_custom_call" | custom-call | tf_op jit(solution)/shard_map/finish_cross/pallas_call | solution.py:21
  (16 shorter events, 0.1 us)
Async XLA Ops:
  0.6 9.6 %collective-permute-start = (bf16[1024,768]{1,0:T(8,128)(2,1)}, bf16[1024,768]{1,0:T(8,128)(2,1)S(1)}, u32[]{:S(2)}, u32[]{:S(2)}) collective-permute-start(bf16[1024,768]{1,0:T(8,128)(2,1)} %refs_0_.3), channel_id=1, source_target_pairs={{0,1},{1,0},{2,3},{3,2},{4,5},{5,4},{6,7},{7,6},{8,9},{9,8},{10,11... | collective-permute-start | bytes 4718600 | tf_op jit(solution)/shard_map/ppermute | solution.py:210
  2.3 7.9 %collective-permute-start.1 = (s32[1024,96]{1,0:T(8,128)S(1)}, s32[1024,96]{1,0:T(8,128)S(1)}, u32[]{:S(2)}, u32[]{:S(2)}) collective-permute-start(s32[1024,96]{1,0:T(8,128)S(1)} %copy.7.refs_2_), channel_id=1, source_target_pairs={{0,1},{1,0},{2,3},{3,2},{4,5},{5,4},{6,7},{7,6},{8,9},{9,8},{10,11... | collective-permute-start | bytes 1179656 | tf_op jit(solution)/shard_map/ppermute | solution.py:210
  3.3 18.7 %collective-permute-start.8 = (bf16[64,384]{1,0:T(8,128)(2,1)S(1)}, bf16[64,384]{1,0:T(8,128)(2,1)S(1)}, u32[]{:S(2)}, u32[]{:S(2)}) collective-permute-start(bf16[64,384]{1,0:T(8,128)(2,1)S(1)} %constant_dynamic-slice_fusion.refs_3_), channel_id=1, source_target_pairs={{0,4},{4,8},{8,12},{12,0},{1,5},{5,9},{9,13},{13,1},{2,6},{6,10},{... | collective-permute-start | bytes 147464 | tf_op jit(solution)/shard_map/ppermute | solution.py:213
  6.3 15.7 %collective-permute-start.9 = (bf16[64,384]{1,0:T(8,128)(2,1)S(1)}, bf16[64,384]{1,0:T(8,128)(2,1)S(1)}, u32[]{:S(2)}, u32[]{:S(2)}) collective-permute-start(bf16[64,384]{1,0:T(8,128)(2,1)S(1)} %constant_dynamic-slice_fusion.refs_3_), channel_id=1, source_target_pairs={{0,8},{4,12},{8,0},{12,4},{1,9},{5,13},{9,1},{13,5},{2,10},{6,14},... | collective-permute-start | bytes 147464 | tf_op jit(solution)/shard_map/ppermute | solution.py:213
  8.9 13.1 %collective-permute-start.10 = (bf16[64,384]{1,0:T(8,128)(2,1)S(1)}, bf16[64,384]{1,0:T(8,128)(2,1)S(1)}, u32[]{:S(2)}, u32[]{:S(2)}) collective-permute-start(bf16[64,384]{1,0:T(8,128)(2,1)S(1)} %constant_dynamic-slice_fusion.refs_3_), channel_id=1, source_target_pairs={{0,12},{4,0},{8,4},{12,8},{1,13},{5,1},{9,5},{13,9},{2,14},{6,2},{... | collective-permute-start | bytes 147464 | tf_op jit(solution)/shard_map/ppermute | solution.py:213
  10.2 1.4 %copy-start = (bf16[1024,768]{1,0:T(8,128)(2,1)S(1)}, bf16[1024,768]{1,0:T(8,128)(2,1)}, u32[]{:S(2)}) copy-start(bf16[1024,768]{1,0:T(8,128)(2,1)} %refs_0_.3) | copy-start | bytes 4718596
  11.6 1.3 %copy-start.1 = (bf16[768,768]{1,0:T(8,128)(2,1)S(1)}, bf16[768,768]{1,0:T(8,128)(2,1)}, u32[]{:S(2)}) copy-start(bf16[768,768]{1,0:T(8,128)(2,1)} %refs_4_.1) | copy-start | bytes 3538948
  25.5 31.1 %copy-start.2 = (bf16[64,768]{1,0:T(8,128)(2,1)S(1)}, bf16[64,768]{1,0:T(8,128)(2,1)}, u32[]{:S(2)}) copy-start(bf16[64,768]{1,0:T(8,128)(2,1)} %codebook.1) | copy-start | bytes 294916
  25.5 8.9 %collective-permute-start.11 = (s16[208,384]{1,0:T(8,128)(2,1)S(1)}, s16[208,384]{1,0:T(8,128)(2,1)S(1)}, u32[]{:S(2)}, u32[]{:S(2)}) collective-permute-start(s16[208,384]{1,0:T(8,128)(2,1)S(1)} %get-tuple-element.17), channel_id=1, source_target_pairs={{0,4},{4,8},{8,12},{12,0},{1,5},{5,9},{9,13},{13,1},{2,6},{6,10},{... | collective-permute-start | bytes 479240 | tf_op jit(solution)/shard_map/ppermute | solution.py:213
  26.2 16.6 %collective-permute-start.12 = (s16[208,384]{1,0:T(8,128)(2,1)S(1)}, s16[208,384]{1,0:T(8,128)(2,1)S(1)}, u32[]{:S(2)}, u32[]{:S(2)}) collective-permute-start(s16[208,384]{1,0:T(8,128)(2,1)S(1)} %get-tuple-element.18), channel_id=1, source_target_pairs={{0,8},{4,12},{8,0},{12,4},{1,9},{5,13},{9,1},{13,5},{2,10},{6,14},... | collective-permute-start | bytes 479240 | tf_op jit(solution)/shard_map/ppermute | solution.py:213
  26.6 16.2 %collective-permute-start.13 = (s16[208,384]{1,0:T(8,128)(2,1)S(1)}, s16[208,384]{1,0:T(8,128)(2,1)S(1)}, u32[]{:S(2)}, u32[]{:S(2)}) collective-permute-start(s16[208,384]{1,0:T(8,128)(2,1)S(1)} %get-tuple-element.19), channel_id=1, source_target_pairs={{0,12},{4,0},{8,4},{12,8},{1,13},{5,1},{9,5},{13,9},{2,14},{6,2},{... | collective-permute-start | bytes 479240 | tf_op jit(solution)/shard_map/ppermute | solution.py:213
  29.4 15.2 %collective-permute-start.2 = (f32[112,256]{1,0:T(8,128)S(1)}, f32[112,256]{1,0:T(8,128)S(1)}, u32[]{:S(2)}, u32[]{:S(2)}) collective-permute-start(f32[112,256]{1,0:T(8,128)S(1)} %get-tuple-element.12), channel_id=1, source_target_pairs={{0,4},{4,8},{8,12},{12,0},{1,5},{5,9},{9,13},{13,1},{2,6},{6,10},{... | collective-permute-start | bytes 344072 | tf_op jit(solution)/shard_map/ppermute | solution.py:213
  29.9 20.4 %collective-permute-start.3 = (f32[112,256]{1,0:T(8,128)S(1)}, f32[112,256]{1,0:T(8,128)S(1)}, u32[]{:S(2)}, u32[]{:S(2)}) collective-permute-start(f32[112,256]{1,0:T(8,128)S(1)} %get-tuple-element.13), channel_id=1, source_target_pairs={{0,8},{4,12},{8,0},{12,4},{1,9},{5,13},{9,1},{13,5},{2,10},{6,14},... | collective-permute-start | bytes 344072 | tf_op jit(solution)/shard_map/ppermute | solution.py:213
  34.4 16.0 %collective-permute-start.4 = (f32[112,256]{1,0:T(8,128)S(1)}, f32[112,256]{1,0:T(8,128)S(1)}, u32[]{:S(2)}, u32[]{:S(2)}) collective-permute-start(f32[112,256]{1,0:T(8,128)S(1)} %get-tuple-element.14), channel_id=1, source_target_pairs={{0,12},{4,0},{8,4},{12,8},{1,13},{5,1},{9,5},{13,9},{2,14},{6,2},{... | collective-permute-start | bytes 344072 | tf_op jit(solution)/shard_map/ppermute | solution.py:213
  43.0 9.0 %collective-permute-start.14 = (s16[208,384]{1,0:T(8,128)(2,1)S(1)}, s16[208,384]{1,0:T(8,128)(2,1)S(1)}, u32[]{:S(2)}, u32[]{:S(2)}) collective-permute-start(s16[208,384]{1,0:T(8,128)(2,1)S(1)} %add_cross.1.refs_0_), channel_id=1, source_target_pairs={{0,2},{1,3},{2,0},{3,1},{4,6},{5,7},{6,4},{7,5},{8,10},{9,11},{10,... | collective-permute-start | bytes 479240 | tf_op jit(solution)/shard_map/ppermute | solution.py:210
  50.4 4.9 %collective-permute-start.5 = (f32[112,256]{1,0:T(8,128)S(1)}, f32[112,256]{1,0:T(8,128)S(1)}, u32[]{:S(2)}, u32[]{:S(2)}) collective-permute-start(f32[112,256]{1,0:T(8,128)S(1)} %add_sums.1.q0), channel_id=1, source_target_pairs={{0,2},{1,3},{2,0},{3,1},{4,6},{5,7},{6,4},{7,5},{8,10},{9,11},{10,... | collective-permute-start | bytes 344072 | tf_op jit(solution)/shard_map/ppermute | solution.py:210
  52.0 5.6 %collective-permute-start.15 = (s16[208,384]{1,0:T(8,128)(2,1)S(1)}, s16[208,384]{1,0:T(8,128)(2,1)S(1)}, u32[]{:S(2)}, u32[]{:S(2)}) collective-permute-start(s16[208,384]{1,0:T(8,128)(2,1)S(1)} %add_cross.1.refs_0_), channel_id=1, source_target_pairs={{0,1},{1,0},{2,3},{3,2},{4,5},{5,4},{6,7},{7,6},{8,9},{9,8},{10,11... | collective-permute-start | bytes 479240 | tf_op jit(solution)/shard_map/ppermute | solution.py:210
  52.0 5.6 %collective-permute-start.16 = (s16[208,384]{1,0:T(8,128)(2,1)S(1)}, s16[208,384]{1,0:T(8,128)(2,1)S(1)}, u32[]{:S(2)}, u32[]{:S(2)}) collective-permute-start(s16[208,384]{1,0:T(8,128)(2,1)S(1)} %collective-permute-done.14.refs_1_), channel_id=1, source_target_pairs={{0,1},{1,0},{2,3},{3,2},{4,5},{5,4},{6,7},{7,6},{8,9},{9,8},{10,11... | collective-permute-start | bytes 479240 | tf_op jit(solution)/shard_map/ppermute | solution.py:210
  52.5 2.8 %collective-permute-start.6 = (f32[112,256]{1,0:T(8,128)S(1)}, f32[112,256]{1,0:T(8,128)S(1)}, u32[]{:S(2)}, u32[]{:S(2)}) collective-permute-start(f32[112,256]{1,0:T(8,128)S(1)} %add_sums.1.q0), channel_id=1, source_target_pairs={{0,1},{1,0},{2,3},{3,2},{4,5},{5,4},{6,7},{7,6},{8,9},{9,8},{10,11... | collective-permute-start | bytes 344072 | tf_op jit(solution)/shard_map/ppermute | solution.py:210
  55.3 1.3 %collective-permute-start.7 = (f32[112,256]{1,0:T(8,128)S(1)}, f32[112,256]{1,0:T(8,128)S(1)}, u32[]{:S(2)}, u32[]{:S(2)}) collective-permute-start(f32[112,256]{1,0:T(8,128)S(1)} %collective-permute-done.5.q1), channel_id=1, source_target_pairs={{0,1},{1,0},{2,3},{3,2},{4,5},{5,4},{6,7},{7,6},{8,9},{9,8},{10,11... | collective-permute-start | bytes 344072 | tf_op jit(solution)/shard_map/ppermute | solution.py:210

commit v2 on v0

v2 whole, which is shorter than its diff:
```python
import jax
import jax.numpy as jnp
from jax import lax
from jax.experimental import pallas as pl
from jax.experimental.pallas import tpu as pltpu
from jax.sharding import PartitionSpec as P

prior_count = 4.0
lane = 128
hops = (2, 1, 3)
fine = 64
pack = 4
level = 32000.0
octave = 8.0
pad = 16

f32, bf16, i32, i16 = jnp.float32, jnp.bfloat16, jnp.int32, jnp.int16
nt = (((1,), (1,)), ((), ()))


def call(kernel, outs, args, scratch, name, flops=0, unread=(), hbm=()):
    spaces = [pl.ANY if i in unread + hbm else pltpu.VMEM for i in range(len(args))]
    args = [pltpu.with_memory_space_constraint(x, pltpu.HBM) if i in hbm else x for i, x in enumerate(args)]
    shapes = jax.tree.leaves(outs) + list(args)
    bytes_accessed = sum(s.size * s.dtype.itemsize for s in shapes)
    return pl.pallas_call(
        kernel,
        out_shape=outs,
        in_specs=[pl.BlockSpec(memory_space=space) for space in spaces],
        scratch_shapes=scratch,
        compiler_params=pltpu.CompilerParams(vmem_limit_bytes=20 << 20),
        cost_estimate=pl.CostEstimate(flops=flops, bytes_accessed=bytes_accessed, transcendentals=0),
        name=name,
    )(*args)


def my_half(width):
    core = lax.axis_index("replica") % 2
    return core, pl.ds(pl.multiple_of(core * width, lane), width)


def powers_of(x):
    top = jnp.maximum(jnp.max(jnp.abs(x), axis=0, keepdims=True), 1e-30)
    return jnp.ceil(jnp.log2(top) * octave)


def units(power):
    return level * jnp.exp2(power * (-1.0 / octave))


def scales(power):
    return jnp.exp2(power * (1.0 / octave)) * (1.0 / level)


def quantize(x):
    power = powers_of(x)
    terms = jnp.round(x * units(power)).astype(i32)
    powers = jnp.broadcast_to(power.astype(i32), (pad, x.shape[1]))
    return jnp.concatenate([terms, powers], axis=0).astype(i16)


def dequantize(q):
    rows = q.shape[0] - pad
    return q[:rows].astype(f32) * scales(q[rows:].astype(f32)[:1])


def quantize_sums(x, groups):
    tail = groups * 8
    sums, powers = [], []
    for g in range(groups):
        s = x[g * 8 : g * 8 + 8]
        powers.append(powers_of(s))
        sums.append(jnp.round(s * units(powers[-1])))
    return jnp.concatenate(sums + powers + [x[tail + groups :]], axis=0).astype(i32).astype(i16)


def dequantize_sums(q, groups):
    x = q.astype(f32)
    tail = groups * 8
    sums = [x[g * 8 : g * 8 + 8] * scales(x[tail + g : tail + g + 1]) for g in range(groups)]
    return jnp.concatenate(sums + [x[tail:]], axis=0)


def block_rows(groups):
    return groups * 8 + -(-2 * groups // 16) * 16


def begin_kernel(shape, e0, e1, c0, c1, rot, out, codes, rt, v0, rot_half, lhs, rhs, total, sems):
    rows, half, n_words, n_out = shape
    subs = codes.shape[0]
    core, cols = my_half(half)
    mine = pl.ds(pl.multiple_of(core * subs, 16), subs)
    loads = [
        pltpu.make_async_copy(rot.at[:, cols], rot_half, sems.at[0]),
        pltpu.make_async_copy(c0.at[mine, :], codes.at[:, :rows], sems.at[1]),
        pltpu.make_async_copy(e0, v0, sems.at[2]),
    ]
    for load in loads:
        load.start()
    codes[:, rows:] = c1[mine, :]
    loads[0].wait()
    rot_t = rot_half[...].T
    rt[:, rows:] = lax.dot_general(rot_t, e1[...], nt, preferred_element_type=f32).astype(bf16)
    loads[1].wait()
    loads[2].wait()
    rt[:, :rows] = lax.dot_general(rot_t, v0[...], nt, preferred_element_type=f32).astype(bf16)
    x = lax.axis_index("replica") // 2
    half_sums(0 if n_out == 1 else 1 - x, n_words, codes, rt, lhs, rhs, total)
    if n_out == 1:
        out[...] = total[...]
        return
    me = lax.axis_index("dp")
    block = total.shape[0] // n_out
    for k in range(n_out):
        at = pl.ds(pl.multiple_of((me ^ k) * block, 16), block)
        out[k * block : (k + 1) * block, :] = quantize_sums(total[at, :], subs // pack // 2)


def cross_kernel(shape, e0, e1, codes, *rest):
    rows, half, n_words, n_book, n_out = shape
    books, outs, (book, recon, turned, total) = rest[:n_book], rest[n_book : n_book + n_out], rest[n_book + n_out :]
    me = lax.axis_index("dp")
    owned = n_words // n_book
    for k in range(n_book):
        book[pl.ds(pl.multiple_of((me ^ k) * owned if n_book > 1 else 0, owned), owned), :] = books[k][...].astype(f32)
    table = book[...].T
    for part in range(half // lane):
        for p in range(part * lane // 16, (part + 1) * lane // 16):
            made = []
            for s in (2 * p, 2 * p + 1):
                parts = []
                for at in range(0, 2 * rows, lane):
                    c = jnp.broadcast_to(codes[s : s + 1, at : at + lane], (8, lane))
                    index = c & (lane - 1)
                    value = None
                    for t in range(0, n_words, lane):
                        found = jnp.take_along_axis(
                            table[s * 8 : s * 8 + 8, t : t + lane], index, axis=1, mode="promise_in_bounds"
                        )
                        value = found if value is None else jnp.where(c >= t, found, value)
                    parts.append(value)
                made.append(jnp.concatenate(parts, axis=1))
            recon[p * 16 : (p + 1) * 16, :] = jnp.concatenate(made, axis=0).astype(bf16)
        cut = slice(part * lane, (part + 1) * lane)
        got = jnp.dot(recon[cut, :rows], e0[...], preferred_element_type=f32)
        turned[cut, :] = got + jnp.dot(recon[cut, rows:], e1[...], preferred_element_type=f32)
    if n_out == 1:
        outs[0][...] = turned[...].T
    else:
        total[...] = turned[...].T
        block = total.shape[0] // n_out
        for k in range(n_out):
            terms = total[pl.ds(pl.multiple_of((me ^ k) * block, 16), block), :]
            outs[k][...] = quantize(terms) if k else terms


def half_sums(part, n_words, codes, rt, lhs, rhs, total):
    width = codes.shape[1]
    coarse = n_words // fine
    shift = fine.bit_length() - 1
    low_mask, coarse_shift = fine - 1, coarse.bit_length() - 1
    groups = codes.shape[0] // pack // 2
    block = block_rows(groups)
    subs = groups * pack
    codes = codes[pl.ds(pl.multiple_of(part * subs, 8), subs), :]
    row8 = lax.broadcasted_iota(i32, (8, width), 0)
    row16 = lax.broadcasted_iota(i32, (16, width), 0)
    steps = [(row16 + 16 * t).astype(f32).astype(bf16) for t in range(fine // 16)]
    one, zero = jnp.ones((16, width), bf16), jnp.zeros((16, width), bf16)
    out_sub = lax.broadcasted_iota(i32, (8, pack * fine), 1) >> shift
    count_row = lax.broadcasted_iota(i32, (16, pack * fine), 0) >> coarse_shift
    count_sub = lax.broadcasted_iota(i32, (16, pack * fine), 1) >> shift
    total[...] = jnp.zeros_like(total)
    for g in range(groups):
        b = g % 2
        high = []
        for s in range(pack):
            code = jnp.broadcast_to(codes[g * pack + s : g * pack + s + 1, :], (8, width))
            high.append(code >> shift)
            low = (code & low_mask).astype(f32)
            low = jnp.concatenate([low, low], axis=0).astype(bf16)
            for t, step in enumerate(steps):
                at = s * fine + t * 16
                rhs[b, at : at + 16, :] = jnp.where(low == step, one, zero)
        for p in range(pack // 2):
            pair = jnp.concatenate([high[2 * p], high[2 * p + 1]], axis=0).astype(f32).astype(bf16)
            r = rt[pl.ds(pl.multiple_of((part * subs + g * pack + 2 * p) * 8, 16), 16), :]
            for h in range(coarse):
                at = h * pack * 8 + p * 16
                lhs[b, at : at + 16, :] = jnp.where(pair == h, r, zero)
        ones = []
        for p in range(pack // 2):
            both = jnp.where(row8 < coarse, high[2 * p], high[2 * p + 1])
            ones.append(jnp.where(both == (row8 & (coarse - 1)), 1.0, 0.0))
        base = coarse * pack * 8
        lhs[b, base : base + 16, :] = jnp.concatenate(ones, axis=0).astype(bf16)
        got = lax.dot_general(lhs[b], rhs[b], nt, preferred_element_type=f32)
        counts = jnp.where(count_row == count_sub, got[base : base + 16], 0.0)
        counts = counts[:8] + counts[8:]
        counts = counts[:coarse] + counts[coarse:]
        for h in range(coarse):
            kept = got[h * 32 : h * 32 + 8]
            for s in range(1, pack):
                kept = jnp.where(out_sub == s, got[h * 32 + s * 8 : h * 32 + s * 8 + 8], kept)
            at = h * block
            total[at + g * 8 : at + g * 8 + 8, :] = kept
            at += groups * 9 + g
            total[at : at + 1, :] = counts[h : h + 1]


def sums_kernel(shape, codes, rt, got, _, *rest):
    n_words, n_out = shape
    outs, (lhs, rhs, total) = rest[:-3], rest[-3:]
    half_sums(1 if n_out == 1 else lax.axis_index("replica") // 2, n_words, codes, rt, lhs, rhs, total)
    if n_out == 1:
        outs[0][...] = total[...]
        return
    me = lax.axis_index("dp")
    block = total.shape[0] // n_out
    groups = codes.shape[0] // pack // 2
    for k in range(n_out):
        at = pl.ds(pl.multiple_of((me ^ k) * block, 16), block)
        x = total[at, :] + dequantize_sums(got[k * block : (k + 1) * block, :], groups)
        outs[k][...] = quantize_sums(x, groups)


def tiles(x):
    return [x[:, at : at + lane] for at in range(0, x.shape[1], lane)]


def add_kernel(groups, n, *refs):
    cross, sums, out = refs[:n], refs[n : 2 * n], refs[-1]
    total = cross[0][...]
    for q in cross[1:]:
        total += dequantize(q[...])
    parts = tiles(quantize(total))
    total = dequantize_sums(sums[0][...], groups)
    for r in sums[1:]:
        total += dequantize_sums(r[...], groups)
    parts += tiles(quantize_sums(total, groups))
    out[...] = jnp.concatenate(parts, axis=0)


def finish_kernel(scale, shape, q0, q1, p0, p1, codebook, out, cross, turned):
    terms, block = shape
    width = codebook.shape[1]
    half = width // 2
    core = lax.axis_index("replica") % 2
    low = lax.axis_index("replica") < 2
    groups = half // (8 * pack) // 2
    for start, m0, m1 in ((core * half, q0, q1), (half - core * half, p0, p1)):
        start = pl.multiple_of(start, lane)
        across = half // lane
        for j in range(across):
            at = slice(j * terms, (j + 1) * terms)
            cross[:, pl.ds(start + j * lane, lane)] = (dequantize(m0[at, :]) + dequantize(m1[at, :])) * scale
        wide = pack * fine // lane
        subs = pack // wide
        for j in range(wide):
            at = slice(across * terms + j * block, across * terms + (j + 1) * block)
            a, b = dequantize_sums(m0[at, :], groups), dequantize_sums(m1[at, :], groups)
            for part, x in enumerate((jnp.where(low, a, b), jnp.where(low, b, a))):
                for g in range(groups):
                    sums = x[g * 8 : g * 8 + 8]
                    row = groups * 9 + g
                    counts = jnp.broadcast_to(x[row : row + 1], sums.shape)
                    for i in range(subs):
                        to = ((part * groups + g) * pack + j * subs + i) * 8
                        cut = slice(i * fine, (i + 1) * fine)
                        turned[to : to + 8, :] = jnp.concatenate([sums[:, cut], counts[:, cut]], axis=1)
        t = turned[...].T
        cols = pl.ds(start, half)
        old = codebook[:, cols].astype(f32)
        out[:, cols] = (t[:fine] + prior_count * old) / (t[fine:] + prior_count)


def local(embeddings, codes, rotation, codebook):
    rows, width = embeddings.shape
    n_sub = codes.shape[1]
    half = width // 2
    n = lax.axis_size("dp")
    replicas = lax.axis_size("replica")
    n_words = codebook.shape[0] * n
    owned = codebook.shape[0]
    out_rows = width // n
    core = lax.axis_index("replica") % 2
    direct = n == 4 and owned == fine and replicas == 4 and rows * n * replicas < 32768

    def swap(x, bit):
        return lax.ppermute(x, "replica", [(i, i ^ bit) for i in range(replicas)])

    def send(blocks):
        sent = {k: lax.ppermute(blocks[k], "dp", [(i, i ^ k) for i in range(n)]) for k in hops}
        return [blocks[0]] + [sent[k] for k in range(1, n)]

    e1 = swap(embeddings, 1)
    c0 = codes.T
    c1 = swap(c0, 1)
    book = lax.dynamic_slice_in_dim(codebook, core * half, half, 1)
    if direct:
        books = send([book] * n)
    else:
        books = [lax.all_gather(book, "dp", axis=0, tiled=True)]
    n_out = n if direct else 1
    coarse = n_words // fine
    groups = n_sub // 2 // pack // 2
    block = block_rows(groups)
    lhs_rows = coarse * pack * 8 + 16
    if direct:
        cross_outs = [jax.ShapeDtypeStruct((out_rows, half), f32)]
        cross_outs += [jax.ShapeDtypeStruct((out_rows + pad, half), i16)] * (n - 1)
    else:
        cross_outs = [jax.ShapeDtypeStruct((width, half), f32)]
    sums_shape = (coarse * block, pack * fine)
    buffers = [
        pltpu.VMEM((2, lhs_rows, 2 * rows), bf16),
        pltpu.VMEM((2, pack * fine, 2 * rows), bf16),
        pltpu.VMEM(sums_shape, f32),
    ]
    first, my_codes, rt, e0 = call(
        lambda *refs: begin_kernel((rows, half, n_words, n_out), *refs),
        [
            jax.ShapeDtypeStruct(sums_shape, i16 if direct else f32),
            jax.ShapeDtypeStruct((n_sub // 2, 2 * rows), i32),
            jax.ShapeDtypeStruct((half, 2 * rows), bf16),
            jax.ShapeDtypeStruct(embeddings.shape, bf16),
        ],
        (embeddings, e1, c0, c1, rotation),
        [pltpu.VMEM((width, half), bf16), *buffers, pltpu.SemaphoreType.DMA((3,))],
        "begin",
        flops=8 * rows * half * width,
        hbm=(0, 2, 4),
    )
    cross = call(
        lambda *refs: cross_kernel((rows, half, n_words, len(books), n_out), *refs),
        cross_outs,
        (e0, e1, my_codes, *books),
        [
            pltpu.VMEM((n_words, half), f32),
            pltpu.VMEM((half, 2 * rows), bf16),
            pltpu.VMEM((half, width), f32),
            pltpu.VMEM((width, half), f32),
        ],
        "cross_terms",
        flops=4 * rows * half * width,
    )
    scale = 1.0 / (rows * n * replicas)
    got = swap(first, 2) if direct else first
    sums = call(
        lambda *refs: sums_kernel((n_words, n_out), *refs),
        [jax.ShapeDtypeStruct((block, pack * fine), i16)] * n if direct else [jax.ShapeDtypeStruct(sums_shape, f32)],
        (my_codes, rt, got, cross[0]),
        buffers,
        "codeword_sums",
        flops=8 * rows * half * width,
        unread=(3,),
    )
    if not direct:
        return plain_finish((first, sums[0]), cross[0], codebook, n_words, scale, swap)

    cross, sums = send(cross), send(sums)
    size = (out_rows + pad) * half // lane + block * pack * fine // lane
    q = call(
        lambda *refs: add_kernel(groups, n, *refs),
        jax.ShapeDtypeStruct((size, lane), i16),
        (*cross, *sums),
        [],
        "add",
    )
    q1 = swap(q, 2)
    return call(
        lambda *refs: finish_kernel(scale, (out_rows + pad, block), *refs),
        [jax.ShapeDtypeStruct(codebook.shape, f32), jax.ShapeDtypeStruct((out_rows, width), f32)],
        (q, q1, swap(q, 1), swap(q1, 1), codebook),
        [pltpu.VMEM((half, lane), f32)],
        "finish",
    )


def plain_finish(sums, cross, codebook, n_words, scale, swap):
    half = cross.shape[1]
    coarse = n_words // fine
    groups = half // (8 * pack) // 2
    sums = jnp.stack([x.reshape(coarse, -1, pack * fine) for x in sums])
    counts = sums[:, :, groups * 9 : groups * 10].reshape(2, coarse, groups, pack, fine)
    counts = counts.transpose(1, 4, 0, 2, 3).reshape(n_words, half // 8)
    sums = sums[:, :, : groups * 8].reshape(2, coarse, groups, 8, pack, fine)
    sums = sums.transpose(1, 5, 0, 2, 4, 3).reshape(n_words, half)
    parts = []
    for x in (sums, counts, cross):
        x = lax.psum_scatter(x, "dp", scatter_dimension=0, tiled=True)
        bit = 2
        while bit < lax.axis_size("replica"):
            x = x + swap(x, bit)
            bit *= 2
        y = swap(x, 1)
        first = lax.axis_index("replica") % 2 == 0
        parts.append(jnp.where(first, jnp.concatenate([x, y], 1), jnp.concatenate([y, x], 1)))
    sums, counts, cross = parts
    spread = jnp.repeat(counts, 8, axis=1)
    new_codebook = (sums + prior_count * codebook.astype(f32)) / (spread + prior_count)
    return new_codebook, cross * scale


def solution(mesh):
    in_specs = (
        P(("groups", "dp", "replica"), None),
        P(("groups", "dp", "replica"), None),
        P("groups", None),
        P(("groups", "dp"), None),
    )
    out_specs = (P(("groups", "dp"), None), P(("groups", "dp"), None))
    return jax.shard_map(local, mesh=mesh, in_specs=in_specs, out_specs=out_specs, check_vma=False)
```

time: 263 us -> 46.5 us (0.18)
  waiting for transfers between devices: 117 us -> 15.2 us
  matrix products: 69.6 us -> 0 us
  blocking collectives: 30.4 us -> 0 us
  other arithmetic: 20.4 us -> 0 us
  starting transfers between devices: 0.17 us -> 17.5 us
  between operations: 15.7 us -> 0.68 us
  Pallas kernels: 0 us -> 12.1 us
  local copies, waits for them, and re-layouts: 8.57 us -> 0.81 us
    psum x2 -> x0, waiting for transfers between devices: 117 us -> none  [the longest x1 86.4 us: local(): lax.psum(lax.dot_general(embeddings, recon, (((0,), (0,)), ((), ())), pre...]
    dot_general x14 -> x0, matrix products: 69.6 us -> none  [the longest x6 33.2 us: local(): jnp.einsum('rgk,rgd->kgd', onehot, rot_group, preferred_element_type=jnp....]
    all_gather x1 -> x0, blocking collectives: 19.5 us -> none  [local(): full_book = lax.all_gather(codebook, 'dp', axis=0, tiled=True)]
    reduce_sum x3 -> x0, other arithmetic: 17.8 us -> none  [local(): count_parts.append(jnp.sum(onehot, axis=0, dtype=jnp.float32).T)]
    ppermute x0 -> x15, starting transfers between devices: none -> 17.5 us  [the longest x9 14.6 us: send(): lax.ppermute(blocks[k], 'dp', [(i, i ^ k) for i in range(n)])]
    ppermute x0 -> x15, waiting for transfers between devices: none -> 15.2 us  [the longest x9 8.7 us: send(): lax.ppermute(blocks[k], 'dp', [(i, i ^ k) for i in range(n)])]
    pallas_call x0 -> x5, Pallas kernels: none -> 12.1 us  [call(): pl.pallas_call(kernel, out_shape=outs, in_specs=[pl.BlockSpec(memory_spac...]
    psum x1 -> x0, blocking collectives: 10.9 us -> none  [local(): word_sums, word_counts = lax.psum((part_sums, part_counts), 'replica')]
  transfers between devices with their start and end apart: 4 -> 15, of which waited for: 2 -> 4; matrix products, arithmetic and copies ran while one was open for 29% -> 2% of each run, Pallas kernels for 0% -> 23%
where the time goes in v2:
time: 46.5 us; the launch traced here: 46.3 us
  starting transfers between devices  17.5 us (38%)
  waiting for transfers between devices  15.2 us (33%)
  Pallas kernels  12.1 us (26%)
  local copies, waits for them, and re-layouts  0.81 us (2%)
  between operations  0.68 us (1%)
    ppermute x9, starting transfers between devices, send(): lax.ppermute(blocks[k], 'dp', [(i, i ^ k) for i in range(n)])  14.6 us
    pallas_call x5, Pallas kernels, call(): pl.pallas_call(kernel, out_shape=outs, in_specs=[pl.BlockSpec(memory_spac...  12.1 us
    ppermute x9, waiting for transfers between devices, send(): lax.ppermute(blocks[k], 'dp', [(i, i ^ k) for i in range(n)])  8.7 us
    ppermute x6, waiting for transfers between devices, swap(): return lax.ppermute(x, 'replica', [(i, i ^ bit) for i in range(replicas)])  6.52 us
    ppermute x6, starting transfers between devices, swap(): return lax.ppermute(x, 'replica', [(i, i ^ bit) for i in range(replicas)])  2.91 us
  transfers between devices with their start and end apart: 15, of which 4 were waited for; matrix products, arithmetic and copies ran while one was open for 2% of the time, Pallas kernels for 23%

profile of v2, /device:TPU:0, one launch (start us, length us, event | category | flops | bytes accessed | tf_op | source)
XLA Modules:
  0.0 46.3 jit_solution(15430633050340551395)
XLA Ops:
  0.6 0.5 %collective-permute-start = (bf16[1024,768]{1,0:T(8,128)(2,1)}, bf16[1024,768]{1,0:T(8,128)(2,1)S(1)}, u32[]{:S(2)}, u32[]{:S(2)}) collective-permute-start(bf16[1024,768]{1,0:T(8,128)(2,1)} %refs_0_.1), channel_id=1, source_target_pairs={{0,1},{1,0},{2,3},{3,2},{4,5},{5,4},{6,7},{7,6},{8,9},{9,8},{10,11... | collective-permute-start | bytes 4718600 | tf_op jit(solution)/shard_map/ppermute | solution.py:290
  1.1 0.1 collective-permute-start.1
  1.2 0.8 %constant_dynamic-slice_fusion.refs_3_ = bf16[64,384]{1,0:T(8,128)(2,1)S(1)} fusion(bf16[64,768]{1,0:T(8,128)(2,1)} %refs_4_.3, s32[]{:T(128)S(6)} %select_n.11), kind=kLoop, calls=%fused_computation | loop fusion | bytes 98308 | tf_op jit(solution)/shard_map/dynamic_slice | solution.py:299
  2.0 5.0 %collective-permute-start.4 = (bf16[64,384]{1,0:T(8,128)(2,1)S(1)}, bf16[64,384]{1,0:T(8,128)(2,1)S(1)}, u32[]{:S(2)}, u32[]{:S(2)}) collective-permute-start(bf16[64,384]{1,0:T(8,128)(2,1)S(1)} %constant_dynamic-slice_fusion.refs_3_), channel_id=1, source_target_pairs={{0,12},{4,8},{8,4},{12,0},{1,13},{5,9},{9,5},{13,1},{2,14},{6,10},... | collective-permute-start | bytes 147464 | tf_op jit(solution)/shard_map/ppermute | solution.py:293
  7.1 0.0 collective-permute-start.3
  7.1 0.6 %collective-permute-start.2 = (bf16[64,384]{1,0:T(8,128)(2,1)S(1)}, bf16[64,384]{1,0:T(8,128)(2,1)S(1)}, u32[]{:S(2)}, u32[]{:S(2)}) collective-permute-start(bf16[64,384]{1,0:T(8,128)(2,1)S(1)} %constant_dynamic-slice_fusion.refs_3_), channel_id=1, source_target_pairs={{0,4},{4,0},{8,12},{12,8},{1,5},{5,1},{9,13},{13,9},{2,6},{6,2},{1... | collective-permute-start | bytes 147464 | tf_op jit(solution)/shard_map/ppermute | solution.py:293
  7.7 0.0 collective-permute-done.1.refs_3_
  7.7 0.0 collective-permute-done.refs_1_
  7.7 5.0 %begin.1 = (s16[256,256]{1,0:T(8,128)(2,1)S(1)}, s32[48,2048]{1,0:T(8,128)S(1)}, bf16[384,2048]{1,0:T(8,128)(2,1)S(1)}, bf16[1024,768]{1,0:T(8,128)(2,1)S(1)}) custom-call(bf16[1024,768]{1,0:T(8,128)(2,1)} %refs_0_.1, bf16[1024,768]{1,0:T(8,128)(2,1)S(1)} %collective-permute-done.refs_1_, s32[96,1024]{1,0:T(8,128)} %bitcast.2, ...), custom_call_target="tpu_custom_call" | custom-call | flops 2415919104 | bytes 8781824 | tf_op jit(solution)/shard_map/begin/pallas_call | solution.py:26
  12.7 1.7 %collective-permute-start.8 = (s16[256,256]{1,0:T(8,128)(2,1)S(1)}, s16[256,256]{1,0:T(8,128)(2,1)S(1)}, u32[]{:S(2)}, u32[]{:S(2)}) collective-permute-start(s16[256,256]{1,0:T(8,128)(2,1)S(1)} %get-tuple-element.21), channel_id=1, source_target_pairs={{0,2},{1,3},{2,0},{3,1},{4,6},{5,7},{6,4},{7,5},{8,10},{9,11},{10,... | collective-permute-start | bytes 393224 | tf_op jit(solution)/shard_map/ppermute | solution.py:290
  14.4 0.0 collective-permute-done.4.refs_6_
  14.4 0.0 collective-permute-done.3.refs_5_
  14.4 0.0 collective-permute-done.2.refs_4_
  14.4 3.2 %cross_terms.1 = (f32[192,384]{1,0:T(8,128)S(1)}, s16[208,384]{1,0:T(8,128)(2,1)S(1)}, s16[208,384]{1,0:T(8,128)(2,1)S(1)}, s16[208,384]{1,0:T(8,128)(2,1)S(1)}) custom-call(bf16[1024,768]{1,0:T(8,128)(2,1)S(1)} %get-tuple-element.14.refs_0_, bf16[1024,768]{1,0:T(8,128)(2,1)S(1)} %collective-permute-done.refs_1_, ...), custom_call_target="tpu_custom_call" | custom-call | flops 1207959552 | bytes 4509696 | tf_op jit(solution)/shard_map/cross_terms/pallas_call | solution.py:26
  17.7 1.3 %collective-permute-start.5 = (s16[208,384]{1,0:T(8,128)(2,1)S(1)}, s16[208,384]{1,0:T(8,128)(2,1)S(1)}, u32[]{:S(2)}, u32[]{:S(2)}) collective-permute-start(s16[208,384]{1,0:T(8,128)(2,1)S(1)} %get-tuple-element.17), channel_id=1, source_target_pairs={{0,4},{4,0},{8,12},{12,8},{1,5},{5,1},{9,13},{13,9},{2,6},{6,2},{1... | collective-permute-start | bytes 479240 | tf_op jit(solution)/shard_map/ppermute | solution.py:293
  19.0 2.9 %collective-permute-start.6 = (s16[208,384]{1,0:T(8,128)(2,1)S(1)}, s16[208,384]{1,0:T(8,128)(2,1)S(1)}, u32[]{:S(2)}, u32[]{:S(2)}) collective-permute-start(s16[208,384]{1,0:T(8,128)(2,1)S(1)} %get-tuple-element.18), channel_id=1, source_target_pairs={{0,8},{4,12},{8,0},{12,4},{1,9},{5,13},{9,1},{13,5},{2,10},{6,14},... | collective-permute-start | bytes 479240 | tf_op jit(solution)/shard_map/ppermute | solution.py:293
  21.9 0.2 collective-permute-start.7
  22.1 0.0 collective-permute-done.8.refs_2_
  22.2 2.4 %codeword_sums.1 = (s16[64,256]{1,0:T(8,128)(2,1)S(1)}, s16[64,256]{1,0:T(8,128)(2,1)S(1)}, s16[64,256]{1,0:T(8,128)(2,1)S(1)}, s16[64,256]{1,0:T(8,128)(2,1)S(1)}) custom-call(s32[48,2048]{1,0:T(8,128)S(1)} %get-tuple-element.15.refs_2_.refs_0_, bf16[384,2048]{1,0:T(8,128)(2,1)S(1)} %get-tuple-element.20.refs_1_, ...), custom_call_target="tpu_custom_call" | custom-call | flops 2415919104 | bytes 2523136 | tf_op jit(solution)/shard_map/codeword_sums/pallas_call | solution.py:26
  24.5 0.4 collective-permute-start.9
  25.0 3.8 %collective-permute-start.10 = (s16[64,256]{1,0:T(8,128)(2,1)S(1)}, s16[64,256]{1,0:T(8,128)(2,1)S(1)}, u32[]{:S(2)}, u32[]{:S(2)}) collective-permute-start(s16[64,256]{1,0:T(8,128)(2,1)S(1)} %get-tuple-element.24), channel_id=1, source_target_pairs={{0,8},{4,12},{8,0},{12,4},{1,9},{5,13},{9,1},{13,5},{2,10},{6,14},... | collective-permute-start | bytes 98312 | tf_op jit(solution)/shard_map/ppermute | solution.py:293
  28.8 0.0 collective-permute-done.5.refs_1_
  28.8 0.2 collective-permute-start.11
  29.0 5.9 %collective-permute-done.6.refs_2_ = s16[208,384]{1,0:T(8,128)(2,1)S(1)} collective-permute-done((s16[208,384]{1,0:T(8,128)(2,1)S(1)}, s16[208,384]{1,0:T(8,128)(2,1)S(1)}, u32[]{:S(2)}, u32[]{:S(2)}) %collective-permute-start.6) | collective-permute-done | bytes 159776 | tf_op jit(solution)/shard_map/ppermute | solution.py:293
  34.9 2.8 %collective-permute-done.10.refs_6_ = s16[64,256]{1,0:T(8,128)(2,1)S(1)} collective-permute-done((s16[64,256]{1,0:T(8,128)(2,1)S(1)}, s16[64,256]{1,0:T(8,128)(2,1)S(1)}, u32[]{:S(2)}, u32[]{:S(2)}) %collective-permute-start.10) | collective-permute-done | bytes 32800 | tf_op jit(solution)/shard_map/ppermute | solution.py:293
  37.7 0.0 collective-permute-done.11.refs_7_
  37.7 0.3 add.10.refs_0_
  37.9 0.6 %collective-permute-start.12 = (s16[752,128]{1,0:T(8,128)(2,1)S(1)}, s16[752,128]{1,0:T(8,128)(2,1)S(1)}, u32[]{:S(2)}, u32[]{:S(2)}) collective-permute-start(s16[752,128]{1,0:T(8,128)(2,1)S(1)} %add.10.refs_0_), channel_id=1, source_target_pairs={{0,2},{1,3},{2,0},{3,1},{4,6},{5,7},{6,4},{7,5},{8,10},{9,11},{10,... | collective-permute-start | bytes 577544 | tf_op jit(solution)/shard_map/ppermute | solution.py:290
  38.5 0.0 collective-permute-start.13
  38.5 5.1 %collective-permute-done.12.refs_1_ = s16[752,128]{1,0:T(8,128)(2,1)S(1)} collective-permute-done((s16[752,128]{1,0:T(8,128)(2,1)S(1)}, s16[752,128]{1,0:T(8,128)(2,1)S(1)}, u32[]{:S(2)}, u32[]{:S(2)}) %collective-permute-start.12) | collective-permute-done | bytes 192544 | tf_op jit(solution)/shard_map/ppermute | solution.py:290
  43.6 1.4 %collective-permute-done.14.refs_3_ = s16[752,128]{1,0:T(8,128)(2,1)S(1)} collective-permute-done((s16[752,128]{1,0:T(8,128)(2,1)S(1)}, s16[752,128]{1,0:T(8,128)(2,1)S(1)}, u32[]{:S(2)}, u32[]{:S(2)}) %collective-permute-start.14) | collective-permute-done | bytes 192544 | tf_op jit(solution)/shard_map/ppermute | solution.py:290
  45.1 1.2 %finish.1 = (f32[64,768]{1,0:T(8,128)}, f32[192,768]{1,0:T(8,128)}) custom-call(s16[752,128]{1,0:T(8,128)(2,1)S(1)} %add.10.refs_0_, s16[752,128]{1,0:T(8,128)(2,1)S(1)} %collective-permute-done.12.refs_1_, s16[752,128]{1,0:T(8,128)(2,1)S(1)} %collective-permute-done.13.refs_2_, s16[752,128]{1,0:T(8,128)(2,1)S(1)} %collective-permute-done.14.refs_3_, ...), custom_call_target="tpu_custom_call" | custom-call | bytes 1654784 | tf_op jit(solution)/shard_map/finish/pallas_call | solution.py:26
  (6 shorter events, 0.0 us)
Async XLA Ops:
  0.6 7.1 %collective-permute-start = (bf16[1024,768]{1,0:T(8,128)(2,1)}, bf16[1024,768]{1,0:T(8,128)(2,1)S(1)}, u32[]{:S(2)}, u32[]{:S(2)}) collective-permute-start(bf16[1024,768]{1,0:T(8,128)(2,1)} %refs_0_.1), channel_id=1, source_target_pairs={{0,1},{1,0},{2,3},{3,2},{4,5},{5,4},{6,7},{7,6},{8,9},{9,8},{10,11... | collective-permute-start | bytes 4718600 | tf_op jit(solution)/shard_map/ppermute | solution.py:290
  1.1 6.5 %collective-permute-start.1 = (s32[96,1024]{1,0:T(8,128)}, s32[96,1024]{1,0:T(8,128)S(1)}, u32[]{:S(2)}, u32[]{:S(2)}) collective-permute-start(s32[96,1024]{1,0:T(8,128)} %bitcast.1), channel_id=1, source_target_pairs={{0,1},{1,0},{2,3},{3,2},{4,5},{5,4},{6,7},{7,6},{8,9},{9,8},{10,11... | collective-permute-start | bytes 1179656 | tf_op jit(solution)/shard_map/ppermute | solution.py:290
  2.0 12.4 %collective-permute-start.4 = (bf16[64,384]{1,0:T(8,128)(2,1)S(1)}, bf16[64,384]{1,0:T(8,128)(2,1)S(1)}, u32[]{:S(2)}, u32[]{:S(2)}) collective-permute-start(bf16[64,384]{1,0:T(8,128)(2,1)S(1)} %constant_dynamic-slice_fusion.refs_3_), channel_id=1, source_target_pairs={{0,12},{4,8},{8,4},{12,0},{1,13},{5,9},{9,5},{13,1},{2,14},{6,10},... | collective-permute-start | bytes 147464 | tf_op jit(solution)/shard_map/ppermute | solution.py:293
  7.1 7.4 %collective-permute-start.3 = (bf16[64,384]{1,0:T(8,128)(2,1)S(1)}, bf16[64,384]{1,0:T(8,128)(2,1)S(1)}, u32[]{:S(2)}, u32[]{:S(2)}) collective-permute-start(bf16[64,384]{1,0:T(8,128)(2,1)S(1)} %constant_dynamic-slice_fusion.refs_3_), channel_id=1, source_target_pairs={{0,8},{4,12},{8,0},{12,4},{1,9},{5,13},{9,1},{13,5},{2,10},{6,14},... | collective-permute-start | bytes 147464 | tf_op jit(solution)/shard_map/ppermute | solution.py:293
  7.1 7.4 %collective-permute-start.2 = (bf16[64,384]{1,0:T(8,128)(2,1)S(1)}, bf16[64,384]{1,0:T(8,128)(2,1)S(1)}, u32[]{:S(2)}, u32[]{:S(2)}) collective-permute-start(bf16[64,384]{1,0:T(8,128)(2,1)S(1)} %constant_dynamic-slice_fusion.refs_3_), channel_id=1, source_target_pairs={{0,4},{4,0},{8,12},{12,8},{1,5},{5,1},{9,13},{13,9},{2,6},{6,2},{1... | collective-permute-start | bytes 147464 | tf_op jit(solution)/shard_map/ppermute | solution.py:293
  12.7 9.4 %collective-permute-start.8 = (s16[256,256]{1,0:T(8,128)(2,1)S(1)}, s16[256,256]{1,0:T(8,128)(2,1)S(1)}, u32[]{:S(2)}, u32[]{:S(2)}) collective-permute-start(s16[256,256]{1,0:T(8,128)(2,1)S(1)} %get-tuple-element.21), channel_id=1, source_target_pairs={{0,2},{1,3},{2,0},{3,1},{4,6},{5,7},{6,4},{7,5},{8,10},{9,11},{10,... | collective-permute-start | bytes 393224 | tf_op jit(solution)/shard_map/ppermute | solution.py:290
  17.7 11.1 %collective-permute-start.5 = (s16[208,384]{1,0:T(8,128)(2,1)S(1)}, s16[208,384]{1,0:T(8,128)(2,1)S(1)}, u32[]{:S(2)}, u32[]{:S(2)}) collective-permute-start(s16[208,384]{1,0:T(8,128)(2,1)S(1)} %get-tuple-element.17), channel_id=1, source_target_pairs={{0,4},{4,0},{8,12},{12,8},{1,5},{5,1},{9,13},{13,9},{2,6},{6,2},{1... | collective-permute-start | bytes 479240 | tf_op jit(solution)/shard_map/ppermute | solution.py:293
  19.0 15.9 %collective-permute-start.6 = (s16[208,384]{1,0:T(8,128)(2,1)S(1)}, s16[208,384]{1,0:T(8,128)(2,1)S(1)}, u32[]{:S(2)}, u32[]{:S(2)}) collective-permute-start(s16[208,384]{1,0:T(8,128)(2,1)S(1)} %get-tuple-element.18), channel_id=1, source_target_pairs={{0,8},{4,12},{8,0},{12,4},{1,9},{5,13},{9,1},{13,5},{2,10},{6,14},... | collective-permute-start | bytes 479240 | tf_op jit(solution)/shard_map/ppermute | solution.py:293
  21.9 13.0 %collective-permute-start.7 = (s16[208,384]{1,0:T(8,128)(2,1)S(1)}, s16[208,384]{1,0:T(8,128)(2,1)S(1)}, u32[]{:S(2)}, u32[]{:S(2)}) collective-permute-start(s16[208,384]{1,0:T(8,128)(2,1)S(1)} %get-tuple-element.19), channel_id=1, source_target_pairs={{0,12},{4,8},{8,4},{12,0},{1,13},{5,9},{9,5},{13,1},{2,14},{6,10},... | collective-permute-start | bytes 479240 | tf_op jit(solution)/shard_map/ppermute | solution.py:293
  22.1 22.9 %copy-start = (bf16[64,768]{1,0:T(8,128)(2,1)S(1)}, bf16[64,768]{1,0:T(8,128)(2,1)}, u32[]{:S(2)}) copy-start(bf16[64,768]{1,0:T(8,128)(2,1)} %refs_4_.3) | copy-start | bytes 294916
  24.5 10.4 %collective-permute-start.9 = (s16[64,256]{1,0:T(8,128)(2,1)S(1)}, s16[64,256]{1,0:T(8,128)(2,1)S(1)}, u32[]{:S(2)}, u32[]{:S(2)}) collective-permute-start(s16[64,256]{1,0:T(8,128)(2,1)S(1)} %get-tuple-element.23), channel_id=1, source_target_pairs={{0,4},{4,0},{8,12},{12,8},{1,5},{5,1},{9,13},{13,9},{2,6},{6,2},{1... | collective-permute-start | bytes 98312 | tf_op jit(solution)/shard_map/ppermute | solution.py:293
  25.0 12.7 %collective-permute-start.10 = (s16[64,256]{1,0:T(8,128)(2,1)S(1)}, s16[64,256]{1,0:T(8,128)(2,1)S(1)}, u32[]{:S(2)}, u32[]{:S(2)}) collective-permute-start(s16[64,256]{1,0:T(8,128)(2,1)S(1)} %get-tuple-element.24), channel_id=1, source_target_pairs={{0,8},{4,12},{8,0},{12,4},{1,9},{5,13},{9,1},{13,5},{2,10},{6,14},... | collective-permute-start | bytes 98312 | tf_op jit(solution)/shard_map/ppermute | solution.py:293
  28.8 8.9 %collective-permute-start.11 = (s16[64,256]{1,0:T(8,128)(2,1)S(1)}, s16[64,256]{1,0:T(8,128)(2,1)S(1)}, u32[]{:S(2)}, u32[]{:S(2)}) collective-permute-start(s16[64,256]{1,0:T(8,128)(2,1)S(1)} %get-tuple-element.25), channel_id=1, source_target_pairs={{0,12},{4,8},{8,4},{12,0},{1,13},{5,9},{9,5},{13,1},{2,14},{6,10},... | collective-permute-start | bytes 98312 | tf_op jit(solution)/shard_map/ppermute | solution.py:293
  37.9 5.7 %collective-permute-start.12 = (s16[752,128]{1,0:T(8,128)(2,1)S(1)}, s16[752,128]{1,0:T(8,128)(2,1)S(1)}, u32[]{:S(2)}, u32[]{:S(2)}) collective-permute-start(s16[752,128]{1,0:T(8,128)(2,1)S(1)} %add.10.refs_0_), channel_id=1, source_target_pairs={{0,2},{1,3},{2,0},{3,1},{4,6},{5,7},{6,4},{7,5},{8,10},{9,11},{10,... | collective-permute-start | bytes 577544 | tf_op jit(solution)/shard_map/ppermute | solution.py:290
  38.5 5.1 %collective-permute-start.13 = (s16[752,128]{1,0:T(8,128)(2,1)S(1)}, s16[752,128]{1,0:T(8,128)(2,1)S(1)}, u32[]{:S(2)}, u32[]{:S(2)}) collective-permute-start(s16[752,128]{1,0:T(8,128)(2,1)S(1)} %add.10.refs_0_), channel_id=1, source_target_pairs={{0,1},{1,0},{2,3},{3,2},{4,5},{5,4},{6,7},{7,6},{8,9},{9,8},{10,11... | collective-permute-start | bytes 577544 | tf_op jit(solution)/shard_map/ppermute | solution.py:290
  43.6 1.4 %collective-permute-start.14 = (s16[752,128]{1,0:T(8,128)(2,1)S(1)}, s16[752,128]{1,0:T(8,128)(2,1)S(1)}, u32[]{:S(2)}, u32[]{:S(2)}) collective-permute-start(s16[752,128]{1,0:T(8,128)(2,1)S(1)} %collective-permute-done.12.refs_1_), channel_id=1, source_target_pairs={{0,1},{1,0},{2,3},{3,2},{4,5},{5,4},{6,7},{7,6},{8,9},{9,8},{10,11... | collective-permute-start | bytes 577544 | tf_op jit(solution)/shard_map/ppermute | solution.py:290

commit v3 on v2

--- a/solution.py
+++ b/solution.py
@@ -7,7 +7,7 @@
 
 prior_count = 4.0
 lane = 128
-hops = (2, 1, 3)
+hops = (2, 3, 1)
 fine = 64
 pack = 4
 level = 32000.0
@@ -52,33 +52,43 @@
     return jnp.exp2(power * (1.0 / octave)) * (1.0 / level)
 
 
-def quantize(x):
+def tiles(x):
+    return [x[:, at : at + lane] for at in range(0, x.shape[1], lane)]
+
+
+def whole(x):
+    return x.astype(i32).astype(i16)
+
+
+def encode(x):
     power = powers_of(x)
-    terms = jnp.round(x * units(power)).astype(i32)
-    powers = jnp.broadcast_to(power.astype(i32), (pad, x.shape[1]))
-    return jnp.concatenate([terms, powers], axis=0).astype(i16)
-
-
-def dequantize(q):
-    rows = q.shape[0] - pad
-    return q[:rows].astype(f32) * scales(q[rows:].astype(f32)[:1])
-
-
-def quantize_sums(x, groups):
+    return tiles(jnp.round(x * units(power))), tiles(power)
+
+
+def decode(x, rows, powers):
+    parts = [x[j * rows : (j + 1) * rows] * scales(powers[j : j + 1]) for j in range(powers.shape[0])]
+    return jnp.concatenate(parts, axis=1)
+
+
+def encode_sums(x, groups):
     tail = groups * 8
     sums, powers = [], []
     for g in range(groups):
         s = x[g * 8 : g * 8 + 8]
         powers.append(powers_of(s))
         sums.append(jnp.round(s * units(powers[-1])))
-    return jnp.concatenate(sums + powers + [x[tail + groups :]], axis=0).astype(i32).astype(i16)
-
-
-def dequantize_sums(q, groups):
-    x = q.astype(f32)
+    return jnp.concatenate(sums + powers + [x[tail + groups :]], axis=0)
+
+
+def decode_sums(x, groups):
     tail = groups * 8
     sums = [x[g * 8 : g * 8 + 8] * scales(x[tail + g : tail + g + 1]) for g in range(groups)]
     return jnp.concatenate(sums + [x[tail:]], axis=0)
+
+
+def with_rows(tile, rows, groups):
+    at = groups * 10
+    return jnp.concatenate([tile[:at], *rows, tile[at + len(rows) :]], axis=0)
 
 
 def block_rows(groups):
@@ -113,16 +123,16 @@
     block = total.shape[0] // n_out
     for k in range(n_out):
         at = pl.ds(pl.multiple_of((me ^ k) * block, 16), block)
-        out[k * block : (k + 1) * block, :] = quantize_sums(total[at, :], subs // pack // 2)
-
-
-def cross_kernel(shape, e0, e1, codes, *rest):
+        out[k * block : (k + 1) * block, :] = encode_sums(total[at, :], subs // pack // 2)
+
+
+def cross_kernel(shape, e0, e1, codes, first, *rest):
     rows, half, n_words, n_book, n_out = shape
-    books, outs, (book, recon, turned, total) = rest[:n_book], rest[n_book : n_book + n_out], rest[n_book + n_out :]
+    books, outs, (book, recon, turned, total) = rest[:n_book], rest[n_book:-4], rest[-4:]
     me = lax.axis_index("dp")
     owned = n_words // n_book
-    for k in range(n_book):
-        book[pl.ds(pl.multiple_of((me ^ k) * owned if n_book > 1 else 0, owned), owned), :] = books[k][...].astype(f32)
+    for i, k in enumerate((0,) + hops if n_book > 1 else (0,)):
+        book[pl.ds(pl.multiple_of((me ^ k) * owned if n_book > 1 else 0, owned), owned), :] = books[i][...].astype(f32)
     table = book[...].T
     for part in range(half // lane):
         for p in range(part * lane // 16, (part + 1) * lane // 16):
@@ -146,12 +156,32 @@
         turned[cut, :] = got + jnp.dot(recon[cut, rows:], e1[...], preferred_element_type=f32)
     if n_out == 1:
         outs[0][...] = turned[...].T
-    else:
-        total[...] = turned[...].T
-        block = total.shape[0] // n_out
-        for k in range(n_out):
-            terms = total[pl.ds(pl.multiple_of((me ^ k) * block, 16), block), :]
-            outs[k][...] = quantize(terms) if k else terms
+        outs[1][...] = first[...]
+        return
+    total[...] = turned[...].T
+    own, own_late, message, *sent = outs
+    block, sums = total.shape[0] // n_out, first.shape[0] // n_out
+    early, late = block // 2, block // 4
+    groups = codes.shape[0] // pack // 2
+    x = lax.axis_index("replica") // 2
+    for k in range(n_out):
+        at = (me ^ k) * block
+        terms = total[pl.ds(pl.multiple_of(at, 16), early), :]
+        if k:
+            parts, powers = encode(terms)
+            powers.append(jnp.zeros((pad - len(powers), lane), f32))
+            sent[hops.index(k)][...] = whole(jnp.concatenate(parts + powers, axis=0))
+        else:
+            own[...] = terms
+        mine = pl.ds(pl.multiple_of(at + early + x * late, 16), late)
+        other = pl.ds(pl.multiple_of(at + early + (1 - x) * late, 16), late)
+        own_late[k * late : (k + 1) * late, :] = total[mine, :]
+        parts, powers = encode(total[other, :])
+        low, high = tiles(first[k * sums : (k + 1) * sums, :])
+        size = message.shape[0] // n_out
+        message[k * size : (k + 1) * size, :] = whole(
+            jnp.concatenate(parts + [with_rows(low, powers, groups), high], axis=0)
+        )
 
 
 def half_sums(part, n_words, codes, rt, lhs, rhs, total):
@@ -208,68 +238,81 @@
             total[at : at + 1, :] = counts[h : h + 1]
 
 
-def sums_kernel(shape, codes, rt, got, _, *rest):
-    n_words, n_out = shape
-    outs, (lhs, rhs, total) = rest[:-3], rest[-3:]
-    half_sums(1 if n_out == 1 else lax.axis_index("replica") // 2, n_words, codes, rt, lhs, rhs, total)
-    if n_out == 1:
-        outs[0][...] = total[...]
-        return
+def sums_kernel(fixed, codes, rt, _, out, lhs, rhs, total):
+    n_words, direct = fixed
+    half_sums(lax.axis_index("replica") // 2 if direct else 1, n_words, codes, rt, lhs, rhs, total)
+    out[...] = total[...]
+
+
+def open_late(x, rows, across, groups):
+    at = rows * across
+    low, high = x[at : at + (x.shape[0] - at) // 2], x[at + (x.shape[0] - at) // 2 :]
+    powers = low[groups * 10 : groups * 10 + across]
+    return decode(x, rows, powers), jnp.concatenate([decode_sums(low, groups), decode_sums(high, groups)], axis=1)
+
+
+def add_half_kernel(groups, own_late, own_sums, got, *outs):
     me = lax.axis_index("dp")
-    block = total.shape[0] // n_out
-    groups = codes.shape[0] // pack // 2
-    for k in range(n_out):
-        at = pl.ds(pl.multiple_of((me ^ k) * block, 16), block)
-        x = total[at, :] + dequantize_sums(got[k * block : (k + 1) * block, :], groups)
-        outs[k][...] = quantize_sums(x, groups)
-
-
-def tiles(x):
-    return [x[:, at : at + lane] for at in range(0, x.shape[1], lane)]
+    n = len(outs)
+    late, block, size = own_late.shape[0] // n, own_sums.shape[0] // n, got.shape[0] // n
+    across = own_late.shape[1] // lane
+    for i, k in enumerate((0,) + hops):
+        cross, sums = open_late(got[k * size : (k + 1) * size, :].astype(f32), late, across, groups)
+        parts, powers = encode(own_late[k * late : (k + 1) * late, :] + cross)
+        sums += own_sums[pl.ds(pl.multiple_of((me ^ k) * block, 16), block), :]
+        low, high = tiles(encode_sums(sums, groups))
+        outs[i][...] = whole(jnp.concatenate(parts + [with_rows(low, powers, groups), high], axis=0))
 
 
 def add_kernel(groups, n, *refs):
-    cross, sums, out = refs[:n], refs[n : 2 * n], refs[-1]
-    total = cross[0][...]
-    for q in cross[1:]:
-        total += dequantize(q[...])
-    parts = tiles(quantize(total))
-    total = dequantize_sums(sums[0][...], groups)
-    for r in sums[1:]:
-        total += dequantize_sums(r[...], groups)
-    parts += tiles(quantize_sums(total, groups))
-    out[...] = jnp.concatenate(parts, axis=0)
-
-
-def finish_kernel(scale, shape, q0, q1, p0, p1, codebook, out, cross, turned):
-    terms, block = shape
+    (own, *early), late, out = refs[:n], refs[n : 2 * n], refs[-1]
+    total = own[...]
+    rows, across = total.shape[0], total.shape[1] // lane
+    for q in early:
+        x = q[...].astype(f32)
+        total += decode(x, rows, x[rows * across : rows * across + across])
+    parts, powers = encode(total)
+    cross = sums = None
+    for q in late:
+        c, s = open_late(q[...].astype(f32), rows // 2, across, groups)
+        cross, sums = (c, s) if cross is None else (cross + c, sums + s)
+    late_parts, late_powers = encode(cross)
+    low, high = tiles(encode_sums(sums, groups))
+    low, high = with_rows(low, late_powers, groups), with_rows(high, powers, groups)
+    out[...] = whole(jnp.concatenate(parts + late_parts + [low, high], axis=0))
+
+
+def finish_kernel(scale, early, q0, q1, p0, p1, codebook, out, cross, turned):
+    late = early // 2
     width = codebook.shape[1]
     half = width // 2
+    across = half // lane
     core = lax.axis_index("replica") % 2
     low = lax.axis_index("replica") < 2
     groups = half // (8 * pack) // 2
     for start, m0, m1 in ((core * half, q0, q1), (half - core * half, p0, p1)):
-        start = pl.multiple_of(start, lane)
-        across = half // lane
-        for j in range(across):
-            at = slice(j * terms, (j + 1) * terms)
-            cross[:, pl.ds(start + j * lane, lane)] = (dequantize(m0[at, :]) + dequantize(m1[at, :])) * scale
-        wide = pack * fine // lane
-        subs = pack // wide
-        for j in range(wide):
-            at = slice(across * terms + j * block, across * terms + (j + 1) * block)
-            a, b = dequantize_sums(m0[at, :], groups), dequantize_sums(m1[at, :], groups)
-            for part, x in enumerate((jnp.where(low, a, b), jnp.where(low, b, a))):
-                for g in range(groups):
-                    sums = x[g * 8 : g * 8 + 8]
-                    row = groups * 9 + g
-                    counts = jnp.broadcast_to(x[row : row + 1], sums.shape)
-                    for i in range(subs):
-                        to = ((part * groups + g) * pack + j * subs + i) * 8
-                        cut = slice(i * fine, (i + 1) * fine)
-                        turned[to : to + 8, :] = jnp.concatenate([sums[:, cut], counts[:, cut]], axis=1)
+        cols = pl.ds(pl.multiple_of(start, lane), half)
+        opened = []
+        for m in (m0, m1):
+            x = m[...].astype(f32)
+            late_cross, sums = open_late(x[early * across :], late, across, groups)
+            at = x.shape[0] - sums.shape[0] + groups * 10
+            opened.append((decode(x, early, x[at : at + across]), late_cross, sums))
+        (a, b), lates, halves = zip(*opened)
+        cross[:early, cols] = (a + b) * scale
+        for part, (a, b) in enumerate((lates, lates[::-1])):
+            cross[early + part * late : early + (part + 1) * late, cols] = jnp.where(low, a, b) * scale
+        for part, (a, b) in enumerate((halves, halves[::-1])):
+            x = jnp.where(low, a, b)
+            for g in range(groups):
+                sums = x[g * 8 : g * 8 + 8]
+                row = groups * 9 + g
+                counts = jnp.broadcast_to(x[row : row + 1], sums.shape)
+                for i in range(pack):
+                    to = ((part * groups + g) * pack + i) * 8
+                    cut = slice(i * fine, (i + 1) * fine)
+                    turned[to : to + 8, :] = jnp.concatenate([sums[:, cut], counts[:, cut]], axis=1)
         t = turned[...].T
-        cols = pl.ds(start, half)
         old = codebook[:, cols].astype(f32)
         out[:, cols] = (t[:fine] + prior_count * old) / (t[fine:] + prior_count)
 
@@ -289,16 +332,15 @@
     def swap(x, bit):
         return lax.ppermute(x, "replica", [(i, i ^ bit) for i in range(replicas)])
 
-    def send(blocks):
-        sent = {k: lax.ppermute(blocks[k], "dp", [(i, i ^ k) for i in range(n)]) for k in hops}
-        return [blocks[0]] + [sent[k] for k in range(1, n)]
+    def exchange(blocks):
+        return [lax.ppermute(x, "dp", [(i, i ^ k) for i in range(n)]) for k, x in zip(hops, blocks)]
 
     e1 = swap(embeddings, 1)
     c0 = codes.T
     c1 = swap(c0, 1)
     book = lax.dynamic_slice_in_dim(codebook, core * half, half, 1)
     if direct:
-        books = send([book] * n)
+        books = [book] + exchange([book] * len(hops))
     else:
         books = [lax.all_gather(book, "dp", axis=0, tiled=True)]
     n_out = n if direct else 1
@@ -306,11 +348,6 @@
     groups = n_sub // 2 // pack // 2
     block = block_rows(groups)
     lhs_rows = coarse * pack * 8 + 16
-    if direct:
-        cross_outs = [jax.ShapeDtypeStruct((out_rows, half), f32)]
-        cross_outs += [jax.ShapeDtypeStruct((out_rows + pad, half), i16)] * (n - 1)
-    else:
-        cross_outs = [jax.ShapeDtypeStruct((width, half), f32)]
     sums_shape = (coarse * block, pack * fine)
     buffers = [
         pltpu.VMEM((2, lhs_rows, 2 * rows), bf16),
@@ -320,7 +357,7 @@
     first, my_codes, rt, e0 = call(
         lambda *refs: begin_kernel((rows, half, n_words, n_out), *refs),
         [
-            jax.ShapeDtypeStruct(sums_shape, i16 if direct else f32),
+            jax.ShapeDtypeStruct(sums_shape, f32),
             jax.ShapeDtypeStruct((n_sub // 2, 2 * rows), i32),
             jax.ShapeDtypeStruct((half, 2 * rows), bf16),
             jax.ShapeDtypeStruct(embeddings.shape, bf16),
@@ -331,10 +368,21 @@
         flops=8 * rows * half * width,
         hbm=(0, 2, 4),
     )
+    early, late = out_rows // 2, out_rows // 4
+    across = half // lane
+    late_size = late * across + block * pack * fine // lane
+    if direct:
+        cross_outs = [
+            jax.ShapeDtypeStruct((early, half), f32),
+            jax.ShapeDtypeStruct((n * late, half), f32),
+            jax.ShapeDtypeStruct((n * late_size, lane), i16),
+        ] + [jax.ShapeDtypeStruct((early * across + pad, lane), i16)] * (n - 1)
+    else:
+        cross_outs = [jax.ShapeDtypeStruct((width, half), f32), jax.ShapeDtypeStruct(first.shape, f32)]
     cross = call(
         lambda *refs: cross_kernel((rows, half, n_words, len(books), n_out), *refs),
         cross_outs,
-        (e0, e1, my_codes, *books),
+        (e0, e1, my_codes, first, *books),
         [
             pltpu.VMEM((n_words, half), f32),
             pltpu.VMEM((half, 2 * rows), bf16),
@@ -345,31 +393,36 @@
         flops=4 * rows * half * width,
     )
     scale = 1.0 / (rows * n * replicas)
-    got = swap(first, 2) if direct else first
-    sums = call(
-        lambda *refs: sums_kernel((n_words, n_out), *refs),
-        [jax.ShapeDtypeStruct((block, pack * fine), i16)] * n if direct else [jax.ShapeDtypeStruct(sums_shape, f32)],
-        (my_codes, rt, got, cross[0]),
+    own = call(
+        lambda *refs: sums_kernel((n_words, direct), *refs),
+        jax.ShapeDtypeStruct(sums_shape, f32),
+        (my_codes, rt, cross[0]),
         buffers,
         "codeword_sums",
         flops=8 * rows * half * width,
-        unread=(3,),
+        unread=(2,),
     )
     if not direct:
-        return plain_finish((first, sums[0]), cross[0], codebook, n_words, scale, swap)
-
-    cross, sums = send(cross), send(sums)
-    size = (out_rows + pad) * half // lane + block * pack * fine // lane
+        return plain_finish((cross[1], own), cross[0], codebook, n_words, scale, swap)
+
+    own_early, own_late, message, *early_sent = cross
+    late_blocks = call(
+        lambda *refs: add_half_kernel(groups, *refs),
+        [jax.ShapeDtypeStruct((late_size, lane), i16)] * n,
+        (own_late, own, swap(message, 2)),
+        [],
+        "add_half",
+    )
     q = call(
         lambda *refs: add_kernel(groups, n, *refs),
-        jax.ShapeDtypeStruct((size, lane), i16),
-        (*cross, *sums),
+        jax.ShapeDtypeStruct((early * across + late_size, lane), i16),
+        (own_early, *exchange(early_sent), late_blocks[0], *exchange(late_blocks[1:])),
         [],
         "add",
     )
     q1 = swap(q, 2)
     return call(
-        lambda *refs: finish_kernel(scale, (out_rows + pad, block), *refs),
+        lambda *refs: finish_kernel(scale, early, *refs),
         [jax.ShapeDtypeStruct(codebook.shape, f32), jax.ShapeDtypeStruct((out_rows, width), f32)],
         (q, q1, swap(q, 1), swap(q1, 1), codebook),
         [pltpu.VMEM((half, lane), f32)],

time: 46.5 us -> 41.8 us (0.90)
  waiting for transfers between devices: 15.2 us -> 10.9 us
    ppermute x9, waiting for transfers between devices: 8.7 us -> 5.41 us  [exchange(): lax.ppermute(x, 'dp', [(i, i ^ k) for i in range(n)])]
    ppermute x6, waiting for transfers between devices: 6.52 us -> 5.5 us  [swap(): return lax.ppermute(x, 'replica', [(i, i ^ bit) for i in range(replicas)])]
    ppermute x9, starting transfers between devices: 14.6 us -> 13.7 us  [exchange(): lax.ppermute(x, 'dp', [(i, i ^ k) for i in range(n)])]
    pallas_call x5 -> x6, Pallas kernels: 12.1 us -> 12.1 us  [call(): pl.pallas_call(kernel, out_shape=outs, in_specs=[pl.BlockSpec(memory_spac...]
  transfers between devices with their start and end apart: 15 -> 15, of which waited for: 4 -> 7; matrix products, arithmetic and copies ran while one was open for 2% -> 2% of each run, Pallas kernels for 23% -> 18%
where the time goes in v3:
time: 41.8 us; the launch traced here: 41.6 us
  starting transfers between devices  17.1 us (41%)
  Pallas kernels  12.1 us (29%)
  waiting for transfers between devices  10.9 us (26%)
  local copies, waits for them, and re-layouts  0.81 us (2%)
  between operations  0.71 us (2%)
    ppermute x9, starting transfers between devices, exchange(): lax.ppermute(x, 'dp', [(i, i ^ k) for i in range(n)])  13.7 us
    pallas_call x6, Pallas kernels, call(): pl.pallas_call(kernel, out_shape=outs, in_specs=[pl.BlockSpec(memory_spac...  12.1 us
    ppermute x6, waiting for transfers between devices, swap(): return lax.ppermute(x, 'replica', [(i, i ^ bit) for i in range(replicas)])  5.5 us
    ppermute x9, waiting for transfers between devices, exchange(): lax.ppermute(x, 'dp', [(i, i ^ k) for i in range(n)])  5.41 us
    ppermute x6, starting transfers between devices, swap(): return lax.ppermute(x, 'replica', [(i, i ^ bit) for i in range(replicas)])  3.33 us
  transfers between devices with their start and end apart: 15, of which 7 were waited for; matrix products, arithmetic and copies ran while one was open for 2% of the time, Pallas kernels for 18%

profile of v3, /device:TPU:0, one launch (start us, length us, event | category | flops | bytes accessed | tf_op | source)
XLA Modules:
  0.0 41.6 jit_solution(17717800905744559108)
XLA Ops:
  0.6 0.5 %collective-permute-start = (bf16[1024,768]{1,0:T(8,128)(2,1)}, bf16[1024,768]{1,0:T(8,128)(2,1)S(1)}, u32[]{:S(2)}, u32[]{:S(2)}) collective-permute-start(bf16[1024,768]{1,0:T(8,128)(2,1)} %refs_0_.1), channel_id=1, source_target_pairs={{0,1},{1,0},{2,3},{3,2},{4,5},{5,4},{6,7},{7,6},{8,9},{9,8},{10,11... | collective-permute-start | bytes 4718600 | tf_op jit(solution)/shard_map/ppermute | solution.py:333
  1.1 0.1 collective-permute-start.1
  1.2 0.8 %constant_dynamic-slice_fusion.refs_4_ = bf16[64,384]{1,0:T(8,128)(2,1)S(1)} fusion(bf16[64,768]{1,0:T(8,128)(2,1)} %refs_4_.3, s32[]{:T(128)S(6)} %select_n.11), kind=kLoop, calls=%fused_computation | loop fusion | bytes 98308 | tf_op jit(solution)/shard_map/dynamic_slice | solution.py:341
  2.0 3.0 %collective-permute-start.4 = (bf16[64,384]{1,0:T(8,128)(2,1)S(1)}, bf16[64,384]{1,0:T(8,128)(2,1)S(1)}, u32[]{:S(2)}, u32[]{:S(2)}) collective-permute-start(bf16[64,384]{1,0:T(8,128)(2,1)S(1)} %constant_dynamic-slice_fusion.refs_4_), channel_id=1, source_target_pairs={{0,4},{4,0},{8,12},{12,8},{1,5},{5,1},{9,13},{13,9},{2,6},{6,2},{1... | collective-permute-start | bytes 147464 | tf_op jit(solution)/shard_map/ppermute | solution.py:336
  5.0 2.5 %collective-permute-start.3 = (bf16[64,384]{1,0:T(8,128)(2,1)S(1)}, bf16[64,384]{1,0:T(8,128)(2,1)S(1)}, u32[]{:S(2)}, u32[]{:S(2)}) collective-permute-start(bf16[64,384]{1,0:T(8,128)(2,1)S(1)} %constant_dynamic-slice_fusion.refs_4_), channel_id=1, source_target_pairs={{0,12},{4,8},{8,4},{12,0},{1,13},{5,9},{9,5},{13,1},{2,14},{6,10},... | collective-permute-start | bytes 147464 | tf_op jit(solution)/shard_map/ppermute | solution.py:336
  7.5 0.1 collective-permute-start.2
  7.6 0.0 collective-permute-done.1.refs_3_
  7.6 0.0 collective-permute-done.refs_1_
  7.6 5.0 %begin.1 = (f32[256,256]{1,0:T(8,128)S(1)}, s32[48,2048]{1,0:T(8,128)S(1)}, bf16[384,2048]{1,0:T(8,128)(2,1)S(1)}, bf16[1024,768]{1,0:T(8,128)(2,1)S(1)}) custom-call(bf16[1024,768]{1,0:T(8,128)(2,1)} %refs_0_.1, bf16[1024,768]{1,0:T(8,128)(2,1)S(1)} %collective-permute-done.refs_1_, s32[96,1024]{1,0:T(8,128)} %bitcast.2, ...), custom_call_target="tpu_custom_call" | custom-call | flops 2415919104 | bytes 8912896 | tf_op jit(solution)/shard_map/begin/pallas_call | solution.py:26
  12.6 0.0 collective-permute-done.4.refs_7_
  12.7 0.0 collective-permute-done.3.refs_6_
  12.7 0.4 collective-permute-done.2.refs_5_
  13.0 3.2 %cross_terms.1 = (f32[96,384]{1,0:T(8,128)S(1)}, f32[192,384]{1,0:T(8,128)S(1)}, s16[1088,128]{1,0:T(8,128)(2,1)S(1)}, s16[304,128]{1,0:T(8,128)(2,1)S(1)}, s16[...) custom-call(bf16[1024,768]{1,0:T(8,128)(2,1)S(1)} %get-tuple-element.16.refs_0_, ...), custom_call_target="tpu_custom_call" | custom-call | flops 1207959552 | bytes 4952064 | tf_op jit(solution)/shard_map/cross_terms/pallas_call | solution.py:26
  16.2 1.5 %collective-permute-start.8 = (s16[1088,128]{1,0:T(8,128)(2,1)S(1)}, s16[1088,128]{1,0:T(8,128)(2,1)S(1)}, u32[]{:S(2)}, u32[]{:S(2)}) collective-permute-start(s16[1088,128]{1,0:T(8,128)(2,1)S(1)} %get-tuple-element.25), channel_id=1, source_target_pairs={{0,2},{1,3},{2,0},{3,1},{4,6},{5,7},{6,4},{7,5},{8,10},{9,11},{10,... | collective-permute-start | bytes 835592 | tf_op jit(solution)/shard_map/ppermute | solution.py:333
  17.8 2.5 %collective-permute-start.5 = (s16[304,128]{1,0:T(8,128)(2,1)S(1)}, s16[304,128]{1,0:T(8,128)(2,1)S(1)}, u32[]{:S(2)}, u32[]{:S(2)}) collective-permute-start(s16[304,128]{1,0:T(8,128)(2,1)S(1)} %get-tuple-element.20), channel_id=1, source_target_pairs={{0,8},{4,12},{8,0},{12,4},{1,9},{5,13},{9,1},{13,5},{2,10},{6,14},... | collective-permute-start | bytes 233480 | tf_op jit(solution)/shard_map/ppermute | solution.py:336
  20.2 1.4 %collective-permute-start.6 = (s16[304,128]{1,0:T(8,128)(2,1)S(1)}, s16[304,128]{1,0:T(8,128)(2,1)S(1)}, u32[]{:S(2)}, u32[]{:S(2)}) collective-permute-start(s16[304,128]{1,0:T(8,128)(2,1)S(1)} %get-tuple-element.21), channel_id=1, source_target_pairs={{0,12},{4,8},{8,4},{12,0},{1,13},{5,9},{9,5},{13,1},{2,14},{6,10},... | collective-permute-start | bytes 233480 | tf_op jit(solution)/shard_map/ppermute | solution.py:336
  21.6 0.0 collective-permute-start.7
  21.6 2.2 %codeword_sums.1.refs_1_ = f32[256,256]{1,0:T(8,128)S(1)} custom-call(s32[48,2048]{1,0:T(8,128)S(1)} %get-tuple-element.17.refs_2_.refs_0_, bf16[384,2048]{1,0:T(8,128)(2,1)S(1)} %get-tuple-element.24.refs_1_, f32[96,384]{1,0:T(8,128)S(1)} %get-tuple-element.19.refs_2_.refs_0_), custom_call_target="tpu_custom_call" | custom-call | flops 2415919104 | bytes 2375680 | tf_op jit(solution)/shard_map/codeword_sums/pallas_call | solution.py:26
  23.9 0.0 copy-start
  23.9 0.2 collective-permute-done.8.refs_2_
  24.0 0.3 add_half.1
  24.3 2.9 %collective-permute-start.9 = (s16[272,128]{1,0:T(8,128)(2,1)S(1)}, s16[272,128]{1,0:T(8,128)(2,1)S(1)}, u32[]{:S(2)}, u32[]{:S(2)}) collective-permute-start(s16[272,128]{1,0:T(8,128)(2,1)S(1)} %get-tuple-element.27), channel_id=1, source_target_pairs={{0,8},{4,12},{8,0},{12,4},{1,9},{5,13},{9,1},{13,5},{2,10},{6,14},... | collective-permute-start | bytes 208904 | tf_op jit(solution)/shard_map/ppermute | solution.py:336
  27.2 1.4 %collective-permute-start.10 = (s16[272,128]{1,0:T(8,128)(2,1)S(1)}, s16[272,128]{1,0:T(8,128)(2,1)S(1)}, u32[]{:S(2)}, u32[]{:S(2)}) collective-permute-start(s16[272,128]{1,0:T(8,128)(2,1)S(1)} %get-tuple-element.28), channel_id=1, source_target_pairs={{0,12},{4,8},{8,4},{12,0},{1,13},{5,9},{9,5},{13,1},{2,14},{6,10},... | collective-permute-start | bytes 208904 | tf_op jit(solution)/shard_map/ppermute | solution.py:336
  28.6 0.0 collective-permute-done.7.refs_3_
  28.6 2.6 %collective-permute-done.9.refs_5_ = s16[272,128]{1,0:T(8,128)(2,1)S(1)} collective-permute-done((s16[272,128]{1,0:T(8,128)(2,1)S(1)}, s16[272,128]{1,0:T(8,128)(2,1)S(1)}, u32[]{:S(2)}, u32[]{:S(2)}) %collective-permute-start.9) | collective-permute-done | bytes 69664 | tf_op jit(solution)/shard_map/ppermute | solution.py:336
  31.3 2.2 %collective-permute-done.10.refs_6_ = s16[272,128]{1,0:T(8,128)(2,1)S(1)} collective-permute-done((s16[272,128]{1,0:T(8,128)(2,1)S(1)}, s16[272,128]{1,0:T(8,128)(2,1)S(1)}, u32[]{:S(2)}, u32[]{:S(2)}) %collective-permute-start.10) | collective-permute-done | bytes 69664 | tf_op jit(solution)/shard_map/ppermute | solution.py:336
  33.5 0.2 collective-permute-done.11.refs_7_
  33.7 0.2 add.10.refs_0_
  33.9 1.2 %collective-permute-start.12 = (s16[560,128]{1,0:T(8,128)(2,1)S(1)}, s16[560,128]{1,0:T(8,128)(2,1)S(1)}, u32[]{:S(2)}, u32[]{:S(2)}) collective-permute-start(s16[560,128]{1,0:T(8,128)(2,1)S(1)} %add.10.refs_0_), channel_id=1, source_target_pairs={{0,2},{1,3},{2,0},{3,1},{4,6},{5,7},{6,4},{7,5},{8,10},{9,11},{10,... | collective-permute-start | bytes 430088 | tf_op jit(solution)/shard_map/ppermute | solution.py:333
  35.1 4.0 %collective-permute-done.12.refs_1_ = s16[560,128]{1,0:T(8,128)(2,1)S(1)} collective-permute-done((s16[560,128]{1,0:T(8,128)(2,1)S(1)}, s16[560,128]{1,0:T(8,128)(2,1)S(1)}, u32[]{:S(2)}, u32[]{:S(2)}) %collective-permute-start.12) | collective-permute-done | bytes 143392 | tf_op jit(solution)/shard_map/ppermute | solution.py:333
  39.1 1.4 %collective-permute-done.14.refs_3_ = s16[560,128]{1,0:T(8,128)(2,1)S(1)} collective-permute-done((s16[560,128]{1,0:T(8,128)(2,1)S(1)}, s16[560,128]{1,0:T(8,128)(2,1)S(1)}, u32[]{:S(2)}, u32[]{:S(2)}) %collective-permute-start.14) | collective-permute-done | bytes 143392 | tf_op jit(solution)/shard_map/ppermute | solution.py:333
  40.4 1.1 %finish.1 = (f32[64,768]{1,0:T(8,128)}, f32[192,768]{1,0:T(8,128)}) custom-call(s16[560,128]{1,0:T(8,128)(2,1)S(1)} %add.10.refs_0_, s16[560,128]{1,0:T(8,128)(2,1)S(1)} %collective-permute-done.12.refs_1_, s16[560,128]{1,0:T(8,128)(2,1)S(1)} %collective-permute-done.13.refs_2_, s16[560,128]{1,0:T(8,128)(2,1)S(1)} %collective-permute-done.14.refs_3_, ...), custom_call_target="tpu_custom_call" | custom-call | bytes 1458176 | tf_op jit(solution)/shard_map/finish/pallas_call | solution.py:26
  (7 shorter events, 0.0 us)
Async XLA Ops:
  0.6 7.0 %collective-permute-start = (bf16[1024,768]{1,0:T(8,128)(2,1)}, bf16[1024,768]{1,0:T(8,128)(2,1)S(1)}, u32[]{:S(2)}, u32[]{:S(2)}) collective-permute-start(bf16[1024,768]{1,0:T(8,128)(2,1)} %refs_0_.1), channel_id=1, source_target_pairs={{0,1},{1,0},{2,3},{3,2},{4,5},{5,4},{6,7},{7,6},{8,9},{9,8},{10,11... | collective-permute-start | bytes 4718600 | tf_op jit(solution)/shard_map/ppermute | solution.py:333
  1.1 6.5 %collective-permute-start.1 = (s32[96,1024]{1,0:T(8,128)}, s32[96,1024]{1,0:T(8,128)S(1)}, u32[]{:S(2)}, u32[]{:S(2)}) collective-permute-start(s32[96,1024]{1,0:T(8,128)} %bitcast.1), channel_id=1, source_target_pairs={{0,1},{1,0},{2,3},{3,2},{4,5},{5,4},{6,7},{7,6},{8,9},{9,8},{10,11... | collective-permute-start | bytes 1179656 | tf_op jit(solution)/shard_map/ppermute | solution.py:333
  2.0 10.6 %collective-permute-start.4 = (bf16[64,384]{1,0:T(8,128)(2,1)S(1)}, bf16[64,384]{1,0:T(8,128)(2,1)S(1)}, u32[]{:S(2)}, u32[]{:S(2)}) collective-permute-start(bf16[64,384]{1,0:T(8,128)(2,1)S(1)} %constant_dynamic-slice_fusion.refs_4_), channel_id=1, source_target_pairs={{0,4},{4,0},{8,12},{12,8},{1,5},{5,1},{9,13},{13,9},{2,6},{6,2},{1... | collective-permute-start | bytes 147464 | tf_op jit(solution)/shard_map/ppermute | solution.py:336
  5.0 7.6 %collective-permute-start.3 = (bf16[64,384]{1,0:T(8,128)(2,1)S(1)}, bf16[64,384]{1,0:T(8,128)(2,1)S(1)}, u32[]{:S(2)}, u32[]{:S(2)}) collective-permute-start(bf16[64,384]{1,0:T(8,128)(2,1)S(1)} %constant_dynamic-slice_fusion.refs_4_), channel_id=1, source_target_pairs={{0,12},{4,8},{8,4},{12,0},{1,13},{5,9},{9,5},{13,1},{2,14},{6,10},... | collective-permute-start | bytes 147464 | tf_op jit(solution)/shard_map/ppermute | solution.py:336
  7.5 5.5 %collective-permute-start.2 = (bf16[64,384]{1,0:T(8,128)(2,1)S(1)}, bf16[64,384]{1,0:T(8,128)(2,1)S(1)}, u32[]{:S(2)}, u32[]{:S(2)}) collective-permute-start(bf16[64,384]{1,0:T(8,128)(2,1)S(1)} %constant_dynamic-slice_fusion.refs_4_), channel_id=1, source_target_pairs={{0,8},{4,12},{8,0},{12,4},{1,9},{5,13},{9,1},{13,5},{2,10},{6,14},... | collective-permute-start | bytes 147464 | tf_op jit(solution)/shard_map/ppermute | solution.py:336
  16.2 7.8 %collective-permute-start.8 = (s16[1088,128]{1,0:T(8,128)(2,1)S(1)}, s16[1088,128]{1,0:T(8,128)(2,1)S(1)}, u32[]{:S(2)}, u32[]{:S(2)}) collective-permute-start(s16[1088,128]{1,0:T(8,128)(2,1)S(1)} %get-tuple-element.25), channel_id=1, source_target_pairs={{0,2},{1,3},{2,0},{3,1},{4,6},{5,7},{6,4},{7,5},{8,10},{9,11},{10,... | collective-permute-start | bytes 835592 | tf_op jit(solution)/shard_map/ppermute | solution.py:333
  17.8 10.8 %collective-permute-start.5 = (s16[304,128]{1,0:T(8,128)(2,1)S(1)}, s16[304,128]{1,0:T(8,128)(2,1)S(1)}, u32[]{:S(2)}, u32[]{:S(2)}) collective-permute-start(s16[304,128]{1,0:T(8,128)(2,1)S(1)} %get-tuple-element.20), channel_id=1, source_target_pairs={{0,8},{4,12},{8,0},{12,4},{1,9},{5,13},{9,1},{13,5},{2,10},{6,14},... | collective-permute-start | bytes 233480 | tf_op jit(solution)/shard_map/ppermute | solution.py:336
  20.2 8.4 %collective-permute-start.6 = (s16[304,128]{1,0:T(8,128)(2,1)S(1)}, s16[304,128]{1,0:T(8,128)(2,1)S(1)}, u32[]{:S(2)}, u32[]{:S(2)}) collective-permute-start(s16[304,128]{1,0:T(8,128)(2,1)S(1)} %get-tuple-element.21), channel_id=1, source_target_pairs={{0,12},{4,8},{8,4},{12,0},{1,13},{5,9},{9,5},{13,1},{2,14},{6,10},... | collective-permute-start | bytes 233480 | tf_op jit(solution)/shard_map/ppermute | solution.py:336
  21.6 7.0 %collective-permute-start.7 = (s16[304,128]{1,0:T(8,128)(2,1)S(1)}, s16[304,128]{1,0:T(8,128)(2,1)S(1)}, u32[]{:S(2)}, u32[]{:S(2)}) collective-permute-start(s16[304,128]{1,0:T(8,128)(2,1)S(1)} %get-tuple-element.22), channel_id=1, source_target_pairs={{0,4},{4,0},{8,12},{12,8},{1,5},{5,1},{9,13},{13,9},{2,6},{6,2},{1... | collective-permute-start | bytes 233480 | tf_op jit(solution)/shard_map/ppermute | solution.py:336
  23.9 16.6 %copy-start = (bf16[64,768]{1,0:T(8,128)(2,1)S(1)}, bf16[64,768]{1,0:T(8,128)(2,1)}, u32[]{:S(2)}) copy-start(bf16[64,768]{1,0:T(8,128)(2,1)} %refs_4_.3) | copy-start | bytes 294916
  24.3 7.0 %collective-permute-start.9 = (s16[272,128]{1,0:T(8,128)(2,1)S(1)}, s16[272,128]{1,0:T(8,128)(2,1)S(1)}, u32[]{:S(2)}, u32[]{:S(2)}) collective-permute-start(s16[272,128]{1,0:T(8,128)(2,1)S(1)} %get-tuple-element.27), channel_id=1, source_target_pairs={{0,8},{4,12},{8,0},{12,4},{1,9},{5,13},{9,1},{13,5},{2,10},{6,14},... | collective-permute-start | bytes 208904 | tf_op jit(solution)/shard_map/ppermute | solution.py:336
  27.2 6.2 %collective-permute-start.10 = (s16[272,128]{1,0:T(8,128)(2,1)S(1)}, s16[272,128]{1,0:T(8,128)(2,1)S(1)}, u32[]{:S(2)}, u32[]{:S(2)}) collective-permute-start(s16[272,128]{1,0:T(8,128)(2,1)S(1)} %get-tuple-element.28), channel_id=1, source_target_pairs={{0,12},{4,8},{8,4},{12,0},{1,13},{5,9},{9,5},{13,1},{2,14},{6,10},... | collective-permute-start | bytes 208904 | tf_op jit(solution)/shard_map/ppermute | solution.py:336
  28.6 5.1 %collective-permute-start.11 = (s16[272,128]{1,0:T(8,128)(2,1)S(1)}, s16[272,128]{1,0:T(8,128)(2,1)S(1)}, u32[]{:S(2)}, u32[]{:S(2)}) collective-permute-start(s16[272,128]{1,0:T(8,128)(2,1)S(1)} %get-tuple-element.29), channel_id=1, source_target_pairs={{0,4},{4,0},{8,12},{12,8},{1,5},{5,1},{9,13},{13,9},{2,6},{6,2},{1... | collective-permute-start | bytes 208904 | tf_op jit(solution)/shard_map/ppermute | solution.py:336
  33.9 5.2 %collective-permute-start.12 = (s16[560,128]{1,0:T(8,128)(2,1)S(1)}, s16[560,128]{1,0:T(8,128)(2,1)S(1)}, u32[]{:S(2)}, u32[]{:S(2)}) collective-permute-start(s16[560,128]{1,0:T(8,128)(2,1)S(1)} %add.10.refs_0_), channel_id=1, source_target_pairs={{0,2},{1,3},{2,0},{3,1},{4,6},{5,7},{6,4},{7,5},{8,10},{9,11},{10,... | collective-permute-start | bytes 430088 | tf_op jit(solution)/shard_map/ppermute | solution.py:333
  35.1 4.0 %collective-permute-start.13 = (s16[560,128]{1,0:T(8,128)(2,1)S(1)}, s16[560,128]{1,0:T(8,128)(2,1)S(1)}, u32[]{:S(2)}, u32[]{:S(2)}) collective-permute-start(s16[560,128]{1,0:T(8,128)(2,1)S(1)} %add.10.refs_0_), channel_id=1, source_target_pairs={{0,1},{1,0},{2,3},{3,2},{4,5},{5,4},{6,7},{7,6},{8,9},{9,8},{10,11... | collective-permute-start | bytes 430088 | tf_op jit(solution)/shard_map/ppermute | solution.py:333
  39.1 1.4 %collective-permute-start.14 = (s16[560,128]{1,0:T(8,128)(2,1)S(1)}, s16[560,128]{1,0:T(8,128)(2,1)S(1)}, u32[]{:S(2)}, u32[]{:S(2)}) collective-permute-start(s16[560,128]{1,0:T(8,128)(2,1)S(1)} %collective-permute-done.12.refs_1_), channel_id=1, source_target_pairs={{0,1},{1,0},{2,3},{3,2},{4,5},{5,4},{6,7},{7,6},{8,9},{9,8},{10,11... | collective-permute-start | bytes 430088 | tf_op jit(solution)/shard_map/ppermute | solution.py:333

commit v4 on v3

--- a/solution.py
+++ b/solution.py
@@ -95,25 +95,24 @@
     return groups * 8 + -(-2 * groups // 16) * 16
 
 
-def begin_kernel(shape, e0, e1, c0, c1, rot, out, codes, rt, v0, rot_half, lhs, rhs, total, sems):
+def take_half_kernel(codebook, out, sem):
+    _, cols = my_half(out.shape[1])
+    copy = pltpu.make_async_copy(codebook.at[:, cols], out, sem)
+    copy.start()
+    copy.wait()
+
+
+def begin_kernel(shape, e0, e1, c0, c1, rot, out, codes, rt, v0, lhs, rhs, total):
     rows, half, n_words, n_out = shape
     subs = codes.shape[0]
     core, cols = my_half(half)
     mine = pl.ds(pl.multiple_of(core * subs, 16), subs)
-    loads = [
-        pltpu.make_async_copy(rot.at[:, cols], rot_half, sems.at[0]),
-        pltpu.make_async_copy(c0.at[mine, :], codes.at[:, :rows], sems.at[1]),
-        pltpu.make_async_copy(e0, v0, sems.at[2]),
-    ]
-    for load in loads:
-        load.start()
-    codes[:, rows:] = c1[mine, :]
-    loads[0].wait()
-    rot_t = rot_half[...].T
-    rt[:, rows:] = lax.dot_general(rot_t, e1[...], nt, preferred_element_type=f32).astype(bf16)
-    loads[1].wait()
-    loads[2].wait()
-    rt[:, :rows] = lax.dot_general(rot_t, v0[...], nt, preferred_element_type=f32).astype(bf16)
+    rot_t = rot[:, cols].T
+    for i, (e, c) in enumerate(((e0, c0), (e1, c1))):
+        at = slice(i * rows, (i + 1) * rows)
+        codes[:, at] = c[mine, :]
+        rt[:, at] = lax.dot_general(rot_t, e[...], nt, preferred_element_type=f32).astype(bf16)
+    v0[...] = e0[...]
     x = lax.axis_index("replica") // 2
     half_sums(0 if n_out == 1 else 1 - x, n_words, codes, rt, lhs, rhs, total)
     if n_out == 1:
@@ -168,9 +167,7 @@
         at = (me ^ k) * block
         terms = total[pl.ds(pl.multiple_of(at, 16), early), :]
         if k:
-            parts, powers = encode(terms)
-            powers.append(jnp.zeros((pad - len(powers), lane), f32))
-            sent[hops.index(k)][...] = whole(jnp.concatenate(parts + powers, axis=0))
+            sent[hops.index(k)][...] = close_early(terms)
         else:
             own[...] = terms
         mine = pl.ds(pl.multiple_of(at + early + x * late, 16), late)
@@ -244,6 +241,17 @@
     out[...] = total[...]
 
 
+def close_early(x):
+    parts, powers = encode(x)
+    powers.append(jnp.zeros((pad - len(powers), lane), f32))
+    return whole(jnp.concatenate(parts + powers, axis=0))
+
+
+def open_early(x, rows, across):
+    at = rows * across
+    return decode(x, rows, x[at : at + across])
+
+
 def open_late(x, rows, across, groups):
     at = rows * across
     low, high = x[at : at + (x.shape[0] - at) // 2], x[at + (x.shape[0] - at) // 2 :]
@@ -264,42 +272,39 @@
         outs[i][...] = whole(jnp.concatenate(parts + [with_rows(low, powers, groups), high], axis=0))
 
 
-def add_kernel(groups, n, *refs):
-    (own, *early), late, out = refs[:n], refs[n : 2 * n], refs[-1]
+def add_early_kernel(own, *rest):
     total = own[...]
-    rows, across = total.shape[0], total.shape[1] // lane
-    for q in early:
-        x = q[...].astype(f32)
-        total += decode(x, rows, x[rows * across : rows * across + across])
-    parts, powers = encode(total)
+    rows = total.shape[0]
+    for q in rest[:-1]:
+        total += open_early(q[...].astype(f32), rows, total.shape[1] // lane)
+    rest[-1][...] = close_early(total)
+
+
+def add_late_kernel(groups, late, across, *refs):
     cross = sums = None
-    for q in late:
-        c, s = open_late(q[...].astype(f32), rows // 2, across, groups)
+    for q in refs[:-1]:
+        c, s = open_late(q[...].astype(f32), late, across, groups)
         cross, sums = (c, s) if cross is None else (cross + c, sums + s)
-    late_parts, late_powers = encode(cross)
+    parts, powers = encode(cross)
     low, high = tiles(encode_sums(sums, groups))
-    low, high = with_rows(low, late_powers, groups), with_rows(high, powers, groups)
-    out[...] = whole(jnp.concatenate(parts + late_parts + [low, high], axis=0))
-
-
-def finish_kernel(scale, early, q0, q1, p0, p1, codebook, out, cross, turned):
-    late = early // 2
+    refs[-1][...] = whole(jnp.concatenate(parts + [with_rows(low, powers, groups), high], axis=0))
+
+
+def finish_kernel(scale, *refs):
+    mine, other, (codebook, out, cross, turned) = refs[:4], refs[4:8], refs[8:]
     width = codebook.shape[1]
     half = width // 2
     across = half // lane
+    early = cross.shape[0] // 2
+    late = early // 2
     core = lax.axis_index("replica") % 2
     low = lax.axis_index("replica") < 2
     groups = half // (8 * pack) // 2
-    for start, m0, m1 in ((core * half, q0, q1), (half - core * half, p0, p1)):
+    for start, (a0, a1, b0, b1) in ((core * half, mine), (half - core * half, other)):
         cols = pl.ds(pl.multiple_of(start, lane), half)
-        opened = []
-        for m in (m0, m1):
-            x = m[...].astype(f32)
-            late_cross, sums = open_late(x[early * across :], late, across, groups)
-            at = x.shape[0] - sums.shape[0] + groups * 10
-            opened.append((decode(x, early, x[at : at + across]), late_cross, sums))
-        (a, b), lates, halves = zip(*opened)
-        cross[:early, cols] = (a + b) * scale
+        total = open_early(a0[...].astype(f32), early, across) + open_early(a1[...].astype(f32), early, across)
+        cross[:early, cols] = total * scale
+        lates, halves = zip(*(open_late(b[...].astype(f32), late, across, groups) for b in (b0, b1)))
         for part, (a, b) in enumerate((lates, lates[::-1])):
             cross[early + part * late : early + (part + 1) * late, cols] = jnp.where(low, a, b) * scale
         for part, (a, b) in enumerate((halves, halves[::-1])):
@@ -326,7 +331,6 @@
     n_words = codebook.shape[0] * n
     owned = codebook.shape[0]
     out_rows = width // n
-    core = lax.axis_index("replica") % 2
     direct = n == 4 and owned == fine and replicas == 4 and rows * n * replicas < 32768
 
     def swap(x, bit):
@@ -338,7 +342,15 @@
     e1 = swap(embeddings, 1)
     c0 = codes.T
     c1 = swap(c0, 1)
-    book = lax.dynamic_slice_in_dim(codebook, core * half, half, 1)
+    book = call(
+        take_half_kernel,
+        jax.ShapeDtypeStruct((owned, half), bf16),
+        (codebook,),
+        [pltpu.SemaphoreType.DMA(())],
+        "take_half",
+        flops=1 << 34,
+        hbm=(0,),
+    )
     if direct:
         books = [book] + exchange([book] * len(hops))
     else:
@@ -363,10 +375,9 @@
             jax.ShapeDtypeStruct(embeddings.shape, bf16),
         ],
         (embeddings, e1, c0, c1, rotation),
-        [pltpu.VMEM((width, half), bf16), *buffers, pltpu.SemaphoreType.DMA((3,))],
+        buffers,
         "begin",
         flops=8 * rows * half * width,
-        hbm=(0, 2, 4),
     )
     early, late = out_rows // 2, out_rows // 4
     across = half // lane
@@ -413,18 +424,25 @@
         [],
         "add_half",
     )
-    q = call(
-        lambda *refs: add_kernel(groups, n, *refs),
-        jax.ShapeDtypeStruct((early * across + late_size, lane), i16),
-        (own_early, *exchange(early_sent), late_blocks[0], *exchange(late_blocks[1:])),
+    a = call(
+        add_early_kernel,
+        jax.ShapeDtypeStruct((early * across + pad, lane), i16),
+        (own_early, *exchange(early_sent)),
         [],
-        "add",
-    )
-    q1 = swap(q, 2)
+        "add_early",
+    )
+    b = call(
+        lambda *refs: add_late_kernel(groups, late, across, *refs),
+        jax.ShapeDtypeStruct((late_size, lane), i16),
+        (late_blocks[0], *exchange(late_blocks[1:])),
+        [],
+        "add_late",
+    )
+    mine = (a, swap(a, 2), b, swap(b, 2))
     return call(
-        lambda *refs: finish_kernel(scale, early, *refs),
+        lambda *refs: finish_kernel(scale, *refs),
         [jax.ShapeDtypeStruct(codebook.shape, f32), jax.ShapeDtypeStruct((out_rows, width), f32)],
-        (q, q1, swap(q, 1), swap(q1, 1), codebook),
+        (*mine, *(swap(x, 1) for x in mine), codebook),
         [pltpu.VMEM((half, lane), f32)],
         "finish",
     )

time: 41.8 us -> 39.8 us (0.952)
  waiting for transfers between devices: 10.9 us -> 9.25 us
  local copies, waits for them, and re-layouts: 0.81 us -> 0.02 us
  starting transfers between devices: 17.1 us -> 17.8 us
    ppermute x6 -> x9, starting transfers between devices: 3.33 us -> 5.14 us  [swap(): return lax.ppermute(x, 'replica', [(i, i ^ bit) for i in range(replicas)])]
    ppermute x6 -> x9, waiting for transfers between devices: 5.5 us -> 4.2 us  [swap(): return lax.ppermute(x, 'replica', [(i, i ^ bit) for i in range(replicas)])]
    ppermute x9, starting transfers between devices: 13.7 us -> 12.7 us  [exchange(): lax.ppermute(x, 'dp', [(i, i ^ k) for i in range(n)])]
    dynamic_slice x1 -> x0, local copies, waits for them, and re-layouts: 0.8 us -> none  [local(): book = lax.dynamic_slice_in_dim(codebook, core * half, half, 1)]
    pallas_call x6 -> x8, Pallas kernels: 12.1 us -> 11.8 us  [call(): pl.pallas_call(kernel, out_shape=outs, in_specs=[pl.BlockSpec(memory_spac...]
  transfers between devices with their start and end apart: 15 -> 18, of which waited for: 7 -> 7; matrix products, arithmetic and copies ran while one was open for 2% -> 0% of each run, Pallas kernels for 18% -> 19%
where the time goes in v4:
time: 39.8 us; the launch traced here: 39.7 us
  starting transfers between devices  17.8 us (45%)
  Pallas kernels  11.8 us (30%)
  waiting for transfers between devices  9.25 us (23%)
  between operations  0.76 us (2%)
    ppermute x9, starting transfers between devices, exchange(): lax.ppermute(x, 'dp', [(i, i ^ k) for i in range(n)])  12.7 us
    pallas_call x8, Pallas kernels, call(): pl.pallas_call(kernel, out_shape=outs, in_specs=[pl.BlockSpec(memory_spac...  11.8 us
    ppermute x9, starting transfers between devices, swap(): return lax.ppermute(x, 'replica', [(i, i ^ bit) for i in range(replicas)])  5.14 us
    ppermute x9, waiting for transfers between devices, exchange(): lax.ppermute(x, 'dp', [(i, i ^ k) for i in range(n)])  5.05 us
    ppermute x9, waiting for transfers between devices, swap(): return lax.ppermute(x, 'replica', [(i, i ^ bit) for i in range(replicas)])  4.2 us
  transfers between devices with their start and end apart: 18, of which 7 were waited for; matrix products, arithmetic and copies ran while one was open for 0% of the time, Pallas kernels for 19%

profile of v4, /device:TPU:0, one launch (start us, length us, event | category | flops | bytes accessed | tf_op | source)
XLA Modules:
  0.0 39.7 jit_solution(9682489706103905359)
XLA Ops:
  0.7 0.5 %collective-permute-start.1 = (s32[96,1024]{1,0:T(8,128)}, s32[96,1024]{1,0:T(8,128)S(1)}, u32[]{:S(2)}, u32[]{:S(2)}) collective-permute-start(s32[96,1024]{1,0:T(8,128)} %bitcast.1), channel_id=1, source_target_pairs={{0,1},{1,0},{2,3},{3,2},{4,5},{5,4},{6,7},{7,6},{8,9},{9,8},{10,11... | collective-permute-start | bytes 1179656 | tf_op jit(solution)/shard_map/ppermute | solution.py:337
  1.2 0.1 collective-permute-start
  1.3 1.1 %take_half.1.refs_4_ = bf16[64,384]{1,0:T(8,128)(2,1)S(1)} custom-call(bf16[64,768]{1,0:T(8,128)(2,1)} %refs_8_.1), custom_call_target="tpu_custom_call" | custom-call | flops 17179869184 | bytes 147456 | tf_op jit(solution)/shard_map/take_half/pallas_call | solution.py:26
  2.4 3.1 %collective-permute-start.4 = (bf16[64,384]{1,0:T(8,128)(2,1)S(1)}, bf16[64,384]{1,0:T(8,128)(2,1)S(1)}, u32[]{:S(2)}, u32[]{:S(2)}) collective-permute-start(bf16[64,384]{1,0:T(8,128)(2,1)S(1)} %take_half.1.refs_4_), channel_id=1, source_target_pairs={{0,4},{4,0},{8,12},{12,8},{1,5},{5,1},{9,13},{13,9},{2,6},{6,2},{1... | collective-permute-start | bytes 147464 | tf_op jit(solution)/shard_map/ppermute | solution.py:340
  5.4 2.5 %collective-permute-start.3 = (bf16[64,384]{1,0:T(8,128)(2,1)S(1)}, bf16[64,384]{1,0:T(8,128)(2,1)S(1)}, u32[]{:S(2)}, u32[]{:S(2)}) collective-permute-start(bf16[64,384]{1,0:T(8,128)(2,1)S(1)} %take_half.1.refs_4_), channel_id=1, source_target_pairs={{0,12},{4,8},{8,4},{12,0},{1,13},{5,9},{9,5},{13,1},{2,14},{6,10},... | collective-permute-start | bytes 147464 | tf_op jit(solution)/shard_map/ppermute | solution.py:340
  7.9 0.1 collective-permute-start.2
  8.1 3.7 %begin.1 = (f32[256,256]{1,0:T(8,128)S(1)}, s32[48,2048]{1,0:T(8,128)S(1)}, bf16[384,2048]{1,0:T(8,128)(2,1)S(1)}, bf16[1024,768]{1,0:T(8,128)(2,1)S(1)}) custom-call(bf16[1024,768]{1,0:T(8,128)(2,1)S(1)} %copy-done.1, bf16[1024,768]{1,0:T(8,128)(2,1)S(1)} %collective-permute-done.refs_1_, s32[96,1024]{1,0:T(8,128)S(1)} %bitcast.2, ...), custom_call_target="tpu_custom_call" | custom-call | flops 2415919104 | bytes 8912896 | tf_op jit(solution)/shard_map/begin/pallas_call | solution.py:26
  11.8 0.1 collective-permute-done.3.refs_6_
  11.9 1.5 %collective-permute-done.2.refs_5_ = bf16[64,384]{1,0:T(8,128)(2,1)S(1)} collective-permute-done((bf16[64,384]{1,0:T(8,128)(2,1)S(1)}, bf16[64,384]{1,0:T(8,128)(2,1)S(1)}, u32[]{:S(2)}, u32[]{:S(2)}) %collective-permute-start.2) | collective-permute-done | bytes 49184 | tf_op jit(solution)/shard_map/ppermute | solution.py:340
  13.4 3.1 %cross_terms.1 = (f32[96,384]{1,0:T(8,128)S(1)}, f32[192,384]{1,0:T(8,128)S(1)}, s16[1088,128]{1,0:T(8,128)(2,1)S(1)}, s16[304,128]{1,0:T(8,128)(2,1)S(1)}, s16[...) custom-call(bf16[1024,768]{1,0:T(8,128)(2,1)S(1)} %get-tuple-element.16.refs_0_, ...), custom_call_target="tpu_custom_call" | custom-call | flops 1207959552 | bytes 4952064 | tf_op jit(solution)/shard_map/cross_terms/pallas_call | solution.py:26
  16.6 1.5 %collective-permute-start.9 = (s16[1088,128]{1,0:T(8,128)(2,1)S(1)}, s16[1088,128]{1,0:T(8,128)(2,1)S(1)}, u32[]{:S(2)}, u32[]{:S(2)}) collective-permute-start(s16[1088,128]{1,0:T(8,128)(2,1)S(1)} %get-tuple-element.25), channel_id=1, source_target_pairs={{0,2},{1,3},{2,0},{3,1},{4,6},{5,7},{6,4},{7,5},{8,10},{9,11},{10,... | collective-permute-start | bytes 835592 | tf_op jit(solution)/shard_map/ppermute | solution.py:337
  18.1 1.2 %collective-permute-start.5 = (s16[304,128]{1,0:T(8,128)(2,1)S(1)}, s16[304,128]{1,0:T(8,128)(2,1)S(1)}, u32[]{:S(2)}, u32[]{:S(2)}) collective-permute-start(s16[304,128]{1,0:T(8,128)(2,1)S(1)} %get-tuple-element.20), channel_id=1, source_target_pairs={{0,8},{4,12},{8,0},{12,4},{1,9},{5,13},{9,1},{13,5},{2,10},{6,14},... | collective-permute-start | bytes 233480 | tf_op jit(solution)/shard_map/ppermute | solution.py:340
  19.3 1.4 %collective-permute-start.6 = (s16[304,128]{1,0:T(8,128)(2,1)S(1)}, s16[304,128]{1,0:T(8,128)(2,1)S(1)}, u32[]{:S(2)}, u32[]{:S(2)}) collective-permute-start(s16[304,128]{1,0:T(8,128)(2,1)S(1)} %get-tuple-element.21), channel_id=1, source_target_pairs={{0,12},{4,8},{8,4},{12,0},{1,13},{5,9},{9,5},{13,1},{2,14},{6,10},... | collective-permute-start | bytes 233480 | tf_op jit(solution)/shard_map/ppermute | solution.py:340
  20.7 0.9 %collective-permute-start.7 = (s16[304,128]{1,0:T(8,128)(2,1)S(1)}, s16[304,128]{1,0:T(8,128)(2,1)S(1)}, u32[]{:S(2)}, u32[]{:S(2)}) collective-permute-start(s16[304,128]{1,0:T(8,128)(2,1)S(1)} %get-tuple-element.22), channel_id=1, source_target_pairs={{0,4},{4,0},{8,12},{12,8},{1,5},{5,1},{9,13},{13,9},{2,6},{6,2},{1... | collective-permute-start | bytes 233480 | tf_op jit(solution)/shard_map/ppermute | solution.py:340
  21.6 2.2 %codeword_sums.1.refs_1_ = f32[256,256]{1,0:T(8,128)S(1)} custom-call(s32[48,2048]{1,0:T(8,128)S(1)} %get-tuple-element.17.refs_2_.refs_0_, bf16[384,2048]{1,0:T(8,128)(2,1)S(1)} %get-tuple-element.24.refs_1_, f32[96,384]{1,0:T(8,128)S(1)} %get-tuple-element.19.own.refs_2_), custom_call_target="tpu_custom_call" | custom-call | flops 2415919104 | bytes 2375680 | tf_op jit(solution)/shard_map/codeword_sums/pallas_call | solution.py:26
  23.8 0.0 copy-start
  23.8 0.0 collective-permute-done.9.refs_2_
  23.9 0.3 add_half.1
  24.1 2.1 %collective-permute-start.10 = (s16[272,128]{1,0:T(8,128)(2,1)S(1)}, s16[272,128]{1,0:T(8,128)(2,1)S(1)}, u32[]{:S(2)}, u32[]{:S(2)}) collective-permute-start(s16[272,128]{1,0:T(8,128)(2,1)S(1)} %get-tuple-element.27), channel_id=1, source_target_pairs={{0,8},{4,12},{8,0},{12,4},{1,9},{5,13},{9,1},{13,5},{2,10},{6,14},... | collective-permute-start | bytes 208904 | tf_op jit(solution)/shard_map/ppermute | solution.py:340
  26.3 1.4 %collective-permute-start.11 = (s16[272,128]{1,0:T(8,128)(2,1)S(1)}, s16[272,128]{1,0:T(8,128)(2,1)S(1)}, u32[]{:S(2)}, u32[]{:S(2)}) collective-permute-start(s16[272,128]{1,0:T(8,128)(2,1)S(1)} %get-tuple-element.28), channel_id=1, source_target_pairs={{0,12},{4,8},{8,4},{12,0},{1,13},{5,9},{9,5},{13,1},{2,14},{6,10},... | collective-permute-start | bytes 208904 | tf_op jit(solution)/shard_map/ppermute | solution.py:340
  27.7 0.1 add_early.1.refs_0_
  27.8 1.5 %collective-permute-start.8 = (s16[304,128]{1,0:T(8,128)(2,1)S(1)}, s16[304,128]{1,0:T(8,128)(2,1)S(1)}, u32[]{:S(2)}, u32[]{:S(2)}) collective-permute-start(s16[304,128]{1,0:T(8,128)(2,1)S(1)} %add_early.1.refs_0_), channel_id=1, source_target_pairs={{0,2},{1,3},{2,0},{3,1},{4,6},{5,7},{6,4},{7,5},{8,10},{9,11},{10,... | collective-permute-start | bytes 233480 | tf_op jit(solution)/shard_map/ppermute | solution.py:337
  29.4 1.8 %collective-permute-done.10.refs_1_ = s16[272,128]{1,0:T(8,128)(2,1)S(1)} collective-permute-done((s16[272,128]{1,0:T(8,128)(2,1)S(1)}, s16[272,128]{1,0:T(8,128)(2,1)S(1)}, u32[]{:S(2)}, u32[]{:S(2)}) %collective-permute-start.10) | collective-permute-done | bytes 69664 | tf_op jit(solution)/shard_map/ppermute | solution.py:340
  31.2 1.4 %collective-permute-done.11.refs_2_ = s16[272,128]{1,0:T(8,128)(2,1)S(1)} collective-permute-done((s16[272,128]{1,0:T(8,128)(2,1)S(1)}, s16[272,128]{1,0:T(8,128)(2,1)S(1)}, u32[]{:S(2)}, u32[]{:S(2)}) %collective-permute-start.11) | collective-permute-done | bytes 69664 | tf_op jit(solution)/shard_map/ppermute | solution.py:340
  32.6 0.2 collective-permute-done.12.refs_3_
  32.8 0.1 add_late.1.refs_2_
  32.9 0.9 %collective-permute-start.13 = (s16[272,128]{1,0:T(8,128)(2,1)S(1)}, s16[272,128]{1,0:T(8,128)(2,1)S(1)}, u32[]{:S(2)}, u32[]{:S(2)}) collective-permute-start(s16[272,128]{1,0:T(8,128)(2,1)S(1)} %add_late.1.refs_2_), channel_id=1, source_target_pairs={{0,2},{1,3},{2,0},{3,1},{4,6},{5,7},{6,4},{7,5},{8,10},{9,11},{10,... | collective-permute-start | bytes 208904 | tf_op jit(solution)/shard_map/ppermute | solution.py:337
  33.8 0.5 %collective-permute-start.15 = (s16[304,128]{1,0:T(8,128)(2,1)S(1)}, s16[304,128]{1,0:T(8,128)(2,1)S(1)}, u32[]{:S(2)}, u32[]{:S(2)}) collective-permute-start(s16[304,128]{1,0:T(8,128)(2,1)S(1)} %collective-permute-done.8.refs_1_), channel_id=1, source_target_pairs={{0,1},{1,0},{2,3},{3,2},{4,5},{5,4},{6,7},{7,6},{8,9},{9,8},{10,11... | collective-permute-start | bytes 233480 | tf_op jit(solution)/shard_map/ppermute | solution.py:337
  34.4 0.0 collective-permute-start.16
  34.4 2.9 %collective-permute-done.13.refs_3_ = s16[272,128]{1,0:T(8,128)(2,1)S(1)} collective-permute-done((s16[272,128]{1,0:T(8,128)(2,1)S(1)}, s16[272,128]{1,0:T(8,128)(2,1)S(1)}, u32[]{:S(2)}, u32[]{:S(2)}) %collective-permute-start.13) | collective-permute-done | bytes 69664 | tf_op jit(solution)/shard_map/ppermute | solution.py:337
  37.3 1.2 %collective-permute-done.17.refs_7_ = s16[272,128]{1,0:T(8,128)(2,1)S(1)} collective-permute-done((s16[272,128]{1,0:T(8,128)(2,1)S(1)}, s16[272,128]{1,0:T(8,128)(2,1)S(1)}, u32[]{:S(2)}, u32[]{:S(2)}) %collective-permute-start.17) | collective-permute-done | bytes 69664 | tf_op jit(solution)/shard_map/ppermute | solution.py:337
  38.5 1.1 %finish.1 = (f32[64,768]{1,0:T(8,128)}, f32[192,768]{1,0:T(8,128)}) custom-call(s16[304,128]{1,0:T(8,128)(2,1)S(1)} %add_early.1.refs_0_, s16[304,128]{1,0:T(8,128)(2,1)S(1)} %collective-permute-done.8.refs_1_, s16[272,128]{1,0:T(8,128)(2,1)S(1)} %add_late.1.refs_2_, s16[272,128]{1,0:T(8,128)(2,1)S(1)} %collective-permute-done.13.refs_3_, ...), custom_call_target="tpu_custom_call" | custom-call | bytes 1474560 | tf_op jit(solution)/shard_map/finish/pallas_call | solution.py:26
  (20 shorter events, 0.0 us)
Async XLA Ops:
  0.6 7.4 %copy-start.1 = (bf16[1024,768]{1,0:T(8,128)(2,1)S(1)}, bf16[1024,768]{1,0:T(8,128)(2,1)}, u32[]{:S(2)}) copy-start(bf16[1024,768]{1,0:T(8,128)(2,1)} %refs_0_.1) | copy-start | bytes 4718596
  0.6 7.4 %copy-start.2 = (bf16[768,768]{1,0:T(8,128)(2,1)S(1)}, bf16[768,768]{1,0:T(8,128)(2,1)}, u32[]{:S(2)}) copy-start(bf16[768,768]{1,0:T(8,128)(2,1)} %refs_4_.1) | copy-start | bytes 3538948
  0.6 7.4 %copy-start.3 = (s32[1024,96]{0,1:T(8,128)S(1)}, s32[1024,96]{0,1:T(8,128)}, u32[]{:S(2)}) copy-start(s32[1024,96]{0,1:T(8,128)} %param.5) | copy-start | bytes 1179652
  0.7 7.4 %collective-permute-start.1 = (s32[96,1024]{1,0:T(8,128)}, s32[96,1024]{1,0:T(8,128)S(1)}, u32[]{:S(2)}, u32[]{:S(2)}) collective-permute-start(s32[96,1024]{1,0:T(8,128)} %bitcast.1), channel_id=1, source_target_pairs={{0,1},{1,0},{2,3},{3,2},{4,5},{5,4},{6,7},{7,6},{8,9},{9,8},{10,11... | collective-permute-start | bytes 1179656 | tf_op jit(solution)/shard_map/ppermute | solution.py:337
  1.2 6.9 %collective-permute-start = (bf16[1024,768]{1,0:T(8,128)(2,1)}, bf16[1024,768]{1,0:T(8,128)(2,1)S(1)}, u32[]{:S(2)}, u32[]{:S(2)}) collective-permute-start(bf16[1024,768]{1,0:T(8,128)(2,1)} %refs_0_.1), channel_id=1, source_target_pairs={{0,1},{1,0},{2,3},{3,2},{4,5},{5,4},{6,7},{7,6},{8,9},{9,8},{10,11... | collective-permute-start | bytes 4718600 | tf_op jit(solution)/shard_map/ppermute | solution.py:337
  2.4 9.4 %collective-permute-start.4 = (bf16[64,384]{1,0:T(8,128)(2,1)S(1)}, bf16[64,384]{1,0:T(8,128)(2,1)S(1)}, u32[]{:S(2)}, u32[]{:S(2)}) collective-permute-start(bf16[64,384]{1,0:T(8,128)(2,1)S(1)} %take_half.1.refs_4_), channel_id=1, source_target_pairs={{0,4},{4,0},{8,12},{12,8},{1,5},{5,1},{9,13},{13,9},{2,6},{6,2},{1... | collective-permute-start | bytes 147464 | tf_op jit(solution)/shard_map/ppermute | solution.py:340
  5.4 6.5 %collective-permute-start.3 = (bf16[64,384]{1,0:T(8,128)(2,1)S(1)}, bf16[64,384]{1,0:T(8,128)(2,1)S(1)}, u32[]{:S(2)}, u32[]{:S(2)}) collective-permute-start(bf16[64,384]{1,0:T(8,128)(2,1)S(1)} %take_half.1.refs_4_), channel_id=1, source_target_pairs={{0,12},{4,8},{8,4},{12,0},{1,13},{5,9},{9,5},{13,1},{2,14},{6,10},... | collective-permute-start | bytes 147464 | tf_op jit(solution)/shard_map/ppermute | solution.py:340
  7.9 5.5 %collective-permute-start.2 = (bf16[64,384]{1,0:T(8,128)(2,1)S(1)}, bf16[64,384]{1,0:T(8,128)(2,1)S(1)}, u32[]{:S(2)}, u32[]{:S(2)}) collective-permute-start(bf16[64,384]{1,0:T(8,128)(2,1)S(1)} %take_half.1.refs_4_), channel_id=1, source_target_pairs={{0,8},{4,12},{8,0},{12,4},{1,9},{5,13},{9,1},{13,5},{2,10},{6,14},... | collective-permute-start | bytes 147464 | tf_op jit(solution)/shard_map/ppermute | solution.py:340
  16.6 7.3 %collective-permute-start.9 = (s16[1088,128]{1,0:T(8,128)(2,1)S(1)}, s16[1088,128]{1,0:T(8,128)(2,1)S(1)}, u32[]{:S(2)}, u32[]{:S(2)}) collective-permute-start(s16[1088,128]{1,0:T(8,128)(2,1)S(1)} %get-tuple-element.25), channel_id=1, source_target_pairs={{0,2},{1,3},{2,0},{3,1},{4,6},{5,7},{6,4},{7,5},{8,10},{9,11},{10,... | collective-permute-start | bytes 835592 | tf_op jit(solution)/shard_map/ppermute | solution.py:337
  18.1 9.6 %collective-permute-start.5 = (s16[304,128]{1,0:T(8,128)(2,1)S(1)}, s16[304,128]{1,0:T(8,128)(2,1)S(1)}, u32[]{:S(2)}, u32[]{:S(2)}) collective-permute-start(s16[304,128]{1,0:T(8,128)(2,1)S(1)} %get-tuple-element.20), channel_id=1, source_target_pairs={{0,8},{4,12},{8,0},{12,4},{1,9},{5,13},{9,1},{13,5},{2,10},{6,14},... | collective-permute-start | bytes 233480 | tf_op jit(solution)/shard_map/ppermute | solution.py:340
  19.3 8.4 %collective-permute-start.6 = (s16[304,128]{1,0:T(8,128)(2,1)S(1)}, s16[304,128]{1,0:T(8,128)(2,1)S(1)}, u32[]{:S(2)}, u32[]{:S(2)}) collective-permute-start(s16[304,128]{1,0:T(8,128)(2,1)S(1)} %get-tuple-element.21), channel_id=1, source_target_pairs={{0,12},{4,8},{8,4},{12,0},{1,13},{5,9},{9,5},{13,1},{2,14},{6,10},... | collective-permute-start | bytes 233480 | tf_op jit(solution)/shard_map/ppermute | solution.py:340
  20.7 7.0 %collective-permute-start.7 = (s16[304,128]{1,0:T(8,128)(2,1)S(1)}, s16[304,128]{1,0:T(8,128)(2,1)S(1)}, u32[]{:S(2)}, u32[]{:S(2)}) collective-permute-start(s16[304,128]{1,0:T(8,128)(2,1)S(1)} %get-tuple-element.22), channel_id=1, source_target_pairs={{0,4},{4,0},{8,12},{12,8},{1,5},{5,1},{9,13},{13,9},{2,6},{6,2},{1... | collective-permute-start | bytes 233480 | tf_op jit(solution)/shard_map/ppermute | solution.py:340
  23.8 14.7 %copy-start = (bf16[64,768]{1,0:T(8,128)(2,1)S(1)}, bf16[64,768]{1,0:T(8,128)(2,1)}, u32[]{:S(2)}) copy-start(bf16[64,768]{1,0:T(8,128)(2,1)} %refs_8_.1) | copy-start | bytes 294916
  24.1 7.0 %collective-permute-start.10 = (s16[272,128]{1,0:T(8,128)(2,1)S(1)}, s16[272,128]{1,0:T(8,128)(2,1)S(1)}, u32[]{:S(2)}, u32[]{:S(2)}) collective-permute-start(s16[272,128]{1,0:T(8,128)(2,1)S(1)} %get-tuple-element.27), channel_id=1, source_target_pairs={{0,8},{4,12},{8,0},{12,4},{1,9},{5,13},{9,1},{13,5},{2,10},{6,14},... | collective-permute-start | bytes 208904 | tf_op jit(solution)/shard_map/ppermute | solution.py:340
  26.3 6.3 %collective-permute-start.11 = (s16[272,128]{1,0:T(8,128)(2,1)S(1)}, s16[272,128]{1,0:T(8,128)(2,1)S(1)}, u32[]{:S(2)}, u32[]{:S(2)}) collective-permute-start(s16[272,128]{1,0:T(8,128)(2,1)S(1)} %get-tuple-element.28), channel_id=1, source_target_pairs={{0,12},{4,8},{8,4},{12,0},{1,13},{5,9},{9,5},{13,1},{2,14},{6,10},... | collective-permute-start | bytes 208904 | tf_op jit(solution)/shard_map/ppermute | solution.py:340
  27.7 5.1 %collective-permute-start.12 = (s16[272,128]{1,0:T(8,128)(2,1)S(1)}, s16[272,128]{1,0:T(8,128)(2,1)S(1)}, u32[]{:S(2)}, u32[]{:S(2)}) collective-permute-start(s16[272,128]{1,0:T(8,128)(2,1)S(1)} %get-tuple-element.29), channel_id=1, source_target_pairs={{0,4},{4,0},{8,12},{12,8},{1,5},{5,1},{9,13},{13,9},{2,6},{6,2},{1... | collective-permute-start | bytes 208904 | tf_op jit(solution)/shard_map/ppermute | solution.py:340
  27.8 6.0 %collective-permute-start.8 = (s16[304,128]{1,0:T(8,128)(2,1)S(1)}, s16[304,128]{1,0:T(8,128)(2,1)S(1)}, u32[]{:S(2)}, u32[]{:S(2)}) collective-permute-start(s16[304,128]{1,0:T(8,128)(2,1)S(1)} %add_early.1.refs_0_), channel_id=1, source_target_pairs={{0,2},{1,3},{2,0},{3,1},{4,6},{5,7},{6,4},{7,5},{8,10},{9,11},{10,... | collective-permute-start | bytes 233480 | tf_op jit(solution)/shard_map/ppermute | solution.py:337
  32.9 4.4 %collective-permute-start.13 = (s16[272,128]{1,0:T(8,128)(2,1)S(1)}, s16[272,128]{1,0:T(8,128)(2,1)S(1)}, u32[]{:S(2)}, u32[]{:S(2)}) collective-permute-start(s16[272,128]{1,0:T(8,128)(2,1)S(1)} %add_late.1.refs_2_), channel_id=1, source_target_pairs={{0,2},{1,3},{2,0},{3,1},{4,6},{5,7},{6,4},{7,5},{8,10},{9,11},{10,... | collective-permute-start | bytes 208904 | tf_op jit(solution)/shard_map/ppermute | solution.py:337
  33.8 3.4 %collective-permute-start.14 = (s16[304,128]{1,0:T(8,128)(2,1)S(1)}, s16[304,128]{1,0:T(8,128)(2,1)S(1)}, u32[]{:S(2)}, u32[]{:S(2)}) collective-permute-start(s16[304,128]{1,0:T(8,128)(2,1)S(1)} %add_early.1.refs_0_), channel_id=1, source_target_pairs={{0,1},{1,0},{2,3},{3,2},{4,5},{5,4},{6,7},{7,6},{8,9},{9,8},{10,11... | collective-permute-start | bytes 233480 | tf_op jit(solution)/shard_map/ppermute | solution.py:337
  33.8 3.4 %collective-permute-start.15 = (s16[304,128]{1,0:T(8,128)(2,1)S(1)}, s16[304,128]{1,0:T(8,128)(2,1)S(1)}, u32[]{:S(2)}, u32[]{:S(2)}) collective-permute-start(s16[304,128]{1,0:T(8,128)(2,1)S(1)} %collective-permute-done.8.refs_1_), channel_id=1, source_target_pairs={{0,1},{1,0},{2,3},{3,2},{4,5},{5,4},{6,7},{7,6},{8,9},{9,8},{10,11... | collective-permute-start | bytes 233480 | tf_op jit(solution)/shard_map/ppermute | solution.py:337
  34.4 2.9 %collective-permute-start.16 = (s16[272,128]{1,0:T(8,128)(2,1)S(1)}, s16[272,128]{1,0:T(8,128)(2,1)S(1)}, u32[]{:S(2)}, u32[]{:S(2)}) collective-permute-start(s16[272,128]{1,0:T(8,128)(2,1)S(1)} %add_late.1.refs_2_), channel_id=1, source_target_pairs={{0,1},{1,0},{2,3},{3,2},{4,5},{5,4},{6,7},{7,6},{8,9},{9,8},{10,11... | collective-permute-start | bytes 208904 | tf_op jit(solution)/shard_map/ppermute | solution.py:337
  37.3 1.3 %collective-permute-start.17 = (s16[272,128]{1,0:T(8,128)(2,1)S(1)}, s16[272,128]{1,0:T(8,128)(2,1)S(1)}, u32[]{:S(2)}, u32[]{:S(2)}) collective-permute-start(s16[272,128]{1,0:T(8,128)(2,1)S(1)} %collective-permute-done.13.refs_3_), channel_id=1, source_target_pairs={{0,1},{1,0},{2,3},{3,2},{4,5},{5,4},{6,7},{7,6},{8,9},{9,8},{10,11... | collective-permute-start | bytes 208904 | tf_op jit(solution)/shard_map/ppermute | solution.py:337

commit v5 on v4

--- a/solution.py
+++ b/solution.py
@@ -7,6 +7,7 @@
 
 prior_count = 4.0
 lane = 128
+book_order, early_order, late_order = (1, 2, 3), (3, 2, 1), (2, 3, 1)
 hops = (2, 3, 1)
 fine = 64
 pack = 4
@@ -95,11 +96,9 @@
     return groups * 8 + -(-2 * groups // 16) * 16
 
 
-def take_half_kernel(codebook, out, sem):
+def take_half_kernel(codebook, out):
     _, cols = my_half(out.shape[1])
-    copy = pltpu.make_async_copy(codebook.at[:, cols], out, sem)
-    copy.start()
-    copy.wait()
+    out[...] = codebook[:, cols]
 
 
 def begin_kernel(shape, e0, e1, c0, c1, rot, out, codes, rt, v0, lhs, rhs, total):
@@ -130,7 +129,7 @@
     books, outs, (book, recon, turned, total) = rest[:n_book], rest[n_book:-4], rest[-4:]
     me = lax.axis_index("dp")
     owned = n_words // n_book
-    for i, k in enumerate((0,) + hops if n_book > 1 else (0,)):
+    for i, k in enumerate((0,) + book_order if n_book > 1 else (0,)):
         book[pl.ds(pl.multiple_of((me ^ k) * owned if n_book > 1 else 0, owned), owned), :] = books[i][...].astype(f32)
     table = book[...].T
     for part in range(half // lane):
@@ -336,8 +335,8 @@
     def swap(x, bit):
         return lax.ppermute(x, "replica", [(i, i ^ bit) for i in range(replicas)])
 
-    def exchange(blocks):
-        return [lax.ppermute(x, "dp", [(i, i ^ k) for i in range(n)]) for k, x in zip(hops, blocks)]
+    def exchange(blocks, order):
+        return [lax.ppermute(blocks[hops.index(k)], "dp", [(i, i ^ k) for i in range(n)]) for k in order]
 
     e1 = swap(embeddings, 1)
     c0 = codes.T
@@ -346,13 +345,12 @@
         take_half_kernel,
         jax.ShapeDtypeStruct((owned, half), bf16),
         (codebook,),
-        [pltpu.SemaphoreType.DMA(())],
+        [],
         "take_half",
         flops=1 << 34,
-        hbm=(0,),
     )
     if direct:
-        books = [book] + exchange([book] * len(hops))
+        books = [book] + exchange([book] * len(hops), book_order)
     else:
         books = [lax.all_gather(book, "dp", axis=0, tiled=True)]
     n_out = n if direct else 1
@@ -427,14 +425,14 @@
     a = call(
         add_early_kernel,
         jax.ShapeDtypeStruct((early * across + pad, lane), i16),
-        (own_early, *exchange(early_sent)),
+        (own_early, *exchange(early_sent, early_order)),
         [],
         "add_early",
     )
     b = call(
         lambda *refs: add_late_kernel(groups, late, across, *refs),
         jax.ShapeDtypeStruct((late_size, lane), i16),
-        (late_blocks[0], *exchange(late_blocks[1:])),
+        (late_blocks[0], *exchange(late_blocks[1:], late_order)),
         [],
         "add_late",
     )

time: 39.8 us -> 39.3 us (0.987)
  waiting for transfers between devices: 9.25 us -> 7.59 us
  starting transfers between devices: 17.8 us -> 19.2 us
  Pallas kernels: 11.8 us -> 10.7 us
  local copies, waits for them, and re-layouts: 0.02 us -> 0.91 us
    ppermute x9, starting transfers between devices: 12.7 us -> 13.9 us  [exchange(): lax.ppermute(blocks[hops.index(k)], 'dp', [(i, i ^ k) for i in range(n)])]
    ppermute x9, waiting for transfers between devices: 5.05 us -> 3.87 us  [exchange(): lax.ppermute(blocks[hops.index(k)], 'dp', [(i, i ^ k) for i in range(n)])]
    pallas_call x8, Pallas kernels: 11.8 us -> 10.7 us  [call(): pl.pallas_call(kernel, out_shape=outs, in_specs=[pl.BlockSpec(memory_spac...]
    unnamed x8 -> x10, local copies, waits for them, and re-layouts: 0.02 us -> 0.91 us
    ppermute x9, waiting for transfers between devices: 4.2 us -> 3.72 us  [swap(): return lax.ppermute(x, 'replica', [(i, i ^ bit) for i in range(replicas)])]
  transfers between devices with their start and end apart: 18 -> 18, of which waited for: 7 -> 6; matrix products, arithmetic and copies ran while one was open for 0% -> 0% of each run, Pallas kernels for 19% -> 16%
where the time goes in v5:
time: 39.3 us; the launch traced here: 39.1 us
  starting transfers between devices  19.2 us (49%)
  Pallas kernels  10.7 us (27%)
  waiting for transfers between devices  7.59 us (19%)
  local copies, waits for them, and re-layouts  0.91 us (2%)
  between operations  0.74 us (2%)
    ppermute x9, starting transfers between devices, exchange(): lax.ppermute(blocks[hops.index(k)], 'dp', [(i, i ^ k) for i in range(n)])  13.9 us
    pallas_call x8, Pallas kernels, call(): pl.pallas_call(kernel, out_shape=outs, in_specs=[pl.BlockSpec(memory_spac...  10.7 us
    ppermute x9, starting transfers between devices, swap(): return lax.ppermute(x, 'replica', [(i, i ^ bit) for i in range(replicas)])  5.23 us
    ppermute x9, waiting for transfers between devices, exchange(): lax.ppermute(blocks[hops.index(k)], 'dp', [(i, i ^ k) for i in range(n)])  3.87 us
    ppermute x9, waiting for transfers between devices, swap(): return lax.ppermute(x, 'replica', [(i, i ^ bit) for i in range(replicas)])  3.72 us
    unnamed x10, local copies, waits for them, and re-layouts  0.91 us
  transfers between devices with their start and end apart: 18, of which 6 were waited for; matrix products, arithmetic and copies ran while one was open for 0% of the time, Pallas kernels for 16%

profile of v5, /device:TPU:0, one launch (start us, length us, event | category | flops | bytes accessed | tf_op | source)
XLA Modules:
  0.0 39.1 jit_solution(810534238767553153)
XLA Ops:
  0.6 0.5 %collective-permute-start.1 = (s32[96,1024]{1,0:T(8,128)}, s32[96,1024]{1,0:T(8,128)S(1)}, u32[]{:S(2)}, u32[]{:S(2)}) collective-permute-start(s32[96,1024]{1,0:T(8,128)} %bitcast.1), channel_id=1, source_target_pairs={{0,1},{1,0},{2,3},{3,2},{4,5},{5,4},{6,7},{7,6},{8,9},{9,8},{10,11... | collective-permute-start | bytes 1179656 | tf_op jit(solution)/shard_map/ppermute | solution.py:336
  1.1 0.1 collective-permute-start
  1.2 0.9 %copy-done = bf16[64,768]{1,0:T(8,128)(2,1)S(1)} copy-done((bf16[64,768]{1,0:T(8,128)(2,1)S(1)}, bf16[64,768]{1,0:T(8,128)(2,1)}, u32[]{:S(2)}) %copy-start) | copy-done | bytes 98328
  2.1 5.1 %collective-permute-start.4 = (bf16[64,384]{1,0:T(8,128)(2,1)S(1)}, bf16[64,384]{1,0:T(8,128)(2,1)S(1)}, u32[]{:S(2)}, u32[]{:S(2)}) collective-permute-start(bf16[64,384]{1,0:T(8,128)(2,1)S(1)} %take_half.1.refs_4_), channel_id=1, source_target_pairs={{0,12},{4,8},{8,4},{12,0},{1,13},{5,9},{9,5},{13,1},{2,14},{6,10},... | collective-permute-start | bytes 147464 | tf_op jit(solution)/shard_map/ppermute | solution.py:339
  7.2 0.6 %collective-permute-start.2 = (bf16[64,384]{1,0:T(8,128)(2,1)S(1)}, bf16[64,384]{1,0:T(8,128)(2,1)S(1)}, u32[]{:S(2)}, u32[]{:S(2)}) collective-permute-start(bf16[64,384]{1,0:T(8,128)(2,1)S(1)} %take_half.1.refs_4_), channel_id=1, source_target_pairs={{0,4},{4,0},{8,12},{12,8},{1,5},{5,1},{9,13},{13,9},{2,6},{6,2},{1... | collective-permute-start | bytes 147464 | tf_op jit(solution)/shard_map/ppermute | solution.py:339
  7.9 0.0 collective-permute-done.refs_1_
  7.9 3.7 %begin.1 = (f32[256,256]{1,0:T(8,128)S(1)}, s32[48,2048]{1,0:T(8,128)S(1)}, bf16[384,2048]{1,0:T(8,128)(2,1)S(1)}, bf16[1024,768]{1,0:T(8,128)(2,1)S(1)}) custom-call(bf16[1024,768]{1,0:T(8,128)(2,1)S(1)} %copy-done.2, bf16[1024,768]{1,0:T(8,128)(2,1)S(1)} %collective-permute-done.refs_1_, s32[96,1024]{1,0:T(8,128)S(1)} %bitcast.2, ...), custom_call_target="tpu_custom_call" | custom-call | flops 2415919104 | bytes 8912896 | tf_op jit(solution)/shard_map/begin/pallas_call | solution.py:27
  11.6 0.0 collective-permute-done.4.refs_7_
  11.6 0.6 %collective-permute-done.3.refs_6_ = bf16[64,384]{1,0:T(8,128)(2,1)S(1)} collective-permute-done((bf16[64,384]{1,0:T(8,128)(2,1)S(1)}, bf16[64,384]{1,0:T(8,128)(2,1)S(1)}, u32[]{:S(2)}, u32[]{:S(2)}) %collective-permute-start.3) | collective-permute-done | bytes 49184 | tf_op jit(solution)/shard_map/ppermute | solution.py:339
  12.2 0.0 collective-permute-done.2.refs_5_
  12.2 3.1 %cross_terms.1 = (f32[96,384]{1,0:T(8,128)S(1)}, f32[192,384]{1,0:T(8,128)S(1)}, s16[1088,128]{1,0:T(8,128)(2,1)S(1)}, s16[304,128]{1,0:T(8,128)(2,1)S(1)}, s16[...) custom-call(bf16[1024,768]{1,0:T(8,128)(2,1)S(1)} %get-tuple-element.16.refs_0_, ...), custom_call_target="tpu_custom_call" | custom-call | flops 1207959552 | bytes 4952064 | tf_op jit(solution)/shard_map/cross_terms/pallas_call | solution.py:27
  15.4 1.5 %collective-permute-start.9 = (s16[1088,128]{1,0:T(8,128)(2,1)S(1)}, s16[1088,128]{1,0:T(8,128)(2,1)S(1)}, u32[]{:S(2)}, u32[]{:S(2)}) collective-permute-start(s16[1088,128]{1,0:T(8,128)(2,1)S(1)} %get-tuple-element.25), channel_id=1, source_target_pairs={{0,2},{1,3},{2,0},{3,1},{4,6},{5,7},{6,4},{7,5},{8,10},{9,11},{10,... | collective-permute-start | bytes 835592 | tf_op jit(solution)/shard_map/ppermute | solution.py:336
  16.9 3.2 %collective-permute-start.5 = (s16[304,128]{1,0:T(8,128)(2,1)S(1)}, s16[304,128]{1,0:T(8,128)(2,1)S(1)}, u32[]{:S(2)}, u32[]{:S(2)}) collective-permute-start(s16[304,128]{1,0:T(8,128)(2,1)S(1)} %get-tuple-element.20), channel_id=1, source_target_pairs={{0,12},{4,8},{8,4},{12,0},{1,13},{5,9},{9,5},{13,1},{2,14},{6,10},... | collective-permute-start | bytes 233480 | tf_op jit(solution)/shard_map/ppermute | solution.py:339
  20.1 1.2 %collective-permute-start.7 = (s16[304,128]{1,0:T(8,128)(2,1)S(1)}, s16[304,128]{1,0:T(8,128)(2,1)S(1)}, u32[]{:S(2)}, u32[]{:S(2)}) collective-permute-start(s16[304,128]{1,0:T(8,128)(2,1)S(1)} %get-tuple-element.22), channel_id=1, source_target_pairs={{0,4},{4,0},{8,12},{12,8},{1,5},{5,1},{9,13},{13,9},{2,6},{6,2},{1... | collective-permute-start | bytes 233480 | tf_op jit(solution)/shard_map/ppermute | solution.py:339
  21.3 2.2 %codeword_sums.1.refs_1_ = f32[256,256]{1,0:T(8,128)S(1)} custom-call(s32[48,2048]{1,0:T(8,128)S(1)} %get-tuple-element.17.refs_2_.refs_0_, bf16[384,2048]{1,0:T(8,128)(2,1)S(1)} %get-tuple-element.24.refs_1_, f32[96,384]{1,0:T(8,128)S(1)} %get-tuple-element.19.own.refs_2_), custom_call_target="tpu_custom_call" | custom-call | flops 2415919104 | bytes 2375680 | tf_op jit(solution)/shard_map/codeword_sums/pallas_call | solution.py:27
  23.5 0.0 copy-start.1
  23.6 0.3 add_half.1
  23.8 1.8 %collective-permute-start.10 = (s16[272,128]{1,0:T(8,128)(2,1)S(1)}, s16[272,128]{1,0:T(8,128)(2,1)S(1)}, u32[]{:S(2)}, u32[]{:S(2)}) collective-permute-start(s16[272,128]{1,0:T(8,128)(2,1)S(1)} %get-tuple-element.27), channel_id=1, source_target_pairs={{0,8},{4,12},{8,0},{12,4},{1,9},{5,13},{9,1},{13,5},{2,10},{6,14},... | collective-permute-start | bytes 208904 | tf_op jit(solution)/shard_map/ppermute | solution.py:339
  25.6 1.5 %collective-permute-start.11 = (s16[272,128]{1,0:T(8,128)(2,1)S(1)}, s16[272,128]{1,0:T(8,128)(2,1)S(1)}, u32[]{:S(2)}, u32[]{:S(2)}) collective-permute-start(s16[272,128]{1,0:T(8,128)(2,1)S(1)} %get-tuple-element.28), channel_id=1, source_target_pairs={{0,12},{4,8},{8,4},{12,0},{1,13},{5,9},{9,5},{13,1},{2,14},{6,10},... | collective-permute-start | bytes 208904 | tf_op jit(solution)/shard_map/ppermute | solution.py:339
  27.2 0.5 %collective-permute-start.12 = (s16[272,128]{1,0:T(8,128)(2,1)S(1)}, s16[272,128]{1,0:T(8,128)(2,1)S(1)}, u32[]{:S(2)}, u32[]{:S(2)}) collective-permute-start(s16[272,128]{1,0:T(8,128)(2,1)S(1)} %get-tuple-element.29), channel_id=1, source_target_pairs={{0,4},{4,0},{8,12},{12,8},{1,5},{5,1},{9,13},{13,9},{2,6},{6,2},{1... | collective-permute-start | bytes 208904 | tf_op jit(solution)/shard_map/ppermute | solution.py:339
  27.7 0.1 add_early.1.refs_0_
  27.8 1.2 %collective-permute-start.8 = (s16[304,128]{1,0:T(8,128)(2,1)S(1)}, s16[304,128]{1,0:T(8,128)(2,1)S(1)}, u32[]{:S(2)}, u32[]{:S(2)}) collective-permute-start(s16[304,128]{1,0:T(8,128)(2,1)S(1)} %add_early.1.refs_0_), channel_id=1, source_target_pairs={{0,2},{1,3},{2,0},{3,1},{4,6},{5,7},{6,4},{7,5},{8,10},{9,11},{10,... | collective-permute-start | bytes 233480 | tf_op jit(solution)/shard_map/ppermute | solution.py:336
  29.0 1.6 %collective-permute-done.10.refs_1_ = s16[272,128]{1,0:T(8,128)(2,1)S(1)} collective-permute-done((s16[272,128]{1,0:T(8,128)(2,1)S(1)}, s16[272,128]{1,0:T(8,128)(2,1)S(1)}, u32[]{:S(2)}, u32[]{:S(2)}) %collective-permute-start.10) | collective-permute-done | bytes 69664 | tf_op jit(solution)/shard_map/ppermute | solution.py:339
  30.6 1.3 %collective-permute-done.11.refs_2_ = s16[272,128]{1,0:T(8,128)(2,1)S(1)} collective-permute-done((s16[272,128]{1,0:T(8,128)(2,1)S(1)}, s16[272,128]{1,0:T(8,128)(2,1)S(1)}, u32[]{:S(2)}, u32[]{:S(2)}) %collective-permute-start.11) | collective-permute-done | bytes 69664 | tf_op jit(solution)/shard_map/ppermute | solution.py:339
  31.9 0.3 collective-permute-done.12.refs_3_
  32.2 0.1 add_late.1.refs_2_
  32.4 1.4 %collective-permute-start.13 = (s16[272,128]{1,0:T(8,128)(2,1)S(1)}, s16[272,128]{1,0:T(8,128)(2,1)S(1)}, u32[]{:S(2)}, u32[]{:S(2)}) collective-permute-start(s16[272,128]{1,0:T(8,128)(2,1)S(1)} %add_late.1.refs_2_), channel_id=1, source_target_pairs={{0,2},{1,3},{2,0},{3,1},{4,6},{5,7},{6,4},{7,5},{8,10},{9,11},{10,... | collective-permute-start | bytes 208904 | tf_op jit(solution)/shard_map/ppermute | solution.py:336
  33.8 0.5 %collective-permute-start.15 = (s16[304,128]{1,0:T(8,128)(2,1)S(1)}, s16[304,128]{1,0:T(8,128)(2,1)S(1)}, u32[]{:S(2)}, u32[]{:S(2)}) collective-permute-start(s16[304,128]{1,0:T(8,128)(2,1)S(1)} %collective-permute-done.8.refs_1_), channel_id=1, source_target_pairs={{0,1},{1,0},{2,3},{3,2},{4,5},{5,4},{6,7},{7,6},{8,9},{9,8},{10,11... | collective-permute-start | bytes 233480 | tf_op jit(solution)/shard_map/ppermute | solution.py:336
  34.3 0.0 collective-permute-start.16
  34.3 2.5 %collective-permute-done.13.refs_3_ = s16[272,128]{1,0:T(8,128)(2,1)S(1)} collective-permute-done((s16[272,128]{1,0:T(8,128)(2,1)S(1)}, s16[272,128]{1,0:T(8,128)(2,1)S(1)}, u32[]{:S(2)}, u32[]{:S(2)}) %collective-permute-start.13) | collective-permute-done | bytes 69664 | tf_op jit(solution)/shard_map/ppermute | solution.py:336
  36.8 1.2 %collective-permute-done.17.refs_7_ = s16[272,128]{1,0:T(8,128)(2,1)S(1)} collective-permute-done((s16[272,128]{1,0:T(8,128)(2,1)S(1)}, s16[272,128]{1,0:T(8,128)(2,1)S(1)}, u32[]{:S(2)}, u32[]{:S(2)}) %collective-permute-start.17) | collective-permute-done | bytes 69664 | tf_op jit(solution)/shard_map/ppermute | solution.py:336
  38.0 1.1 %finish.1 = (f32[64,768]{1,0:T(8,128)}, f32[192,768]{1,0:T(8,128)}) custom-call(s16[304,128]{1,0:T(8,128)(2,1)S(1)} %add_early.1.refs_0_, s16[304,128]{1,0:T(8,128)(2,1)S(1)} %collective-permute-done.8.refs_1_, s16[272,128]{1,0:T(8,128)(2,1)S(1)} %add_late.1.refs_2_, s16[272,128]{1,0:T(8,128)(2,1)S(1)} %collective-permute-done.13.refs_3_, ...), custom_call_target="tpu_custom_call" | custom-call | bytes 1474560 | tf_op jit(solution)/shard_map/finish/pallas_call | solution.py:27
  (22 shorter events, 0.1 us)
Async XLA Ops:
  0.6 7.2 %collective-permute-start.1 = (s32[96,1024]{1,0:T(8,128)}, s32[96,1024]{1,0:T(8,128)S(1)}, u32[]{:S(2)}, u32[]{:S(2)}) collective-permute-start(s32[96,1024]{1,0:T(8,128)} %bitcast.1), channel_id=1, source_target_pairs={{0,1},{1,0},{2,3},{3,2},{4,5},{5,4},{6,7},{7,6},{8,9},{9,8},{10,11... | collective-permute-start | bytes 1179656 | tf_op jit(solution)/shard_map/ppermute | solution.py:336
  1.1 6.7 %collective-permute-start = (bf16[1024,768]{1,0:T(8,128)(2,1)}, bf16[1024,768]{1,0:T(8,128)(2,1)S(1)}, u32[]{:S(2)}, u32[]{:S(2)}) collective-permute-start(bf16[1024,768]{1,0:T(8,128)(2,1)} %refs_0_.1), channel_id=1, source_target_pairs={{0,1},{1,0},{2,3},{3,2},{4,5},{5,4},{6,7},{7,6},{8,9},{9,8},{10,11... | collective-permute-start | bytes 4718600 | tf_op jit(solution)/shard_map/ppermute | solution.py:336
  1.2 0.9 %copy-start = (bf16[64,768]{1,0:T(8,128)(2,1)S(1)}, bf16[64,768]{1,0:T(8,128)(2,1)}, u32[]{:S(2)}) copy-start(bf16[64,768]{1,0:T(8,128)(2,1)} %refs_8_.1) | copy-start | bytes 294916
  2.1 5.8 %copy-start.2 = (bf16[1024,768]{1,0:T(8,128)(2,1)S(1)}, bf16[1024,768]{1,0:T(8,128)(2,1)}, u32[]{:S(2)}) copy-start(bf16[1024,768]{1,0:T(8,128)(2,1)} %refs_0_.1) | copy-start | bytes 4718596
  2.1 5.8 %copy-start.3 = (bf16[768,768]{1,0:T(8,128)(2,1)S(1)}, bf16[768,768]{1,0:T(8,128)(2,1)}, u32[]{:S(2)}) copy-start(bf16[768,768]{1,0:T(8,128)(2,1)} %refs_4_.1) | copy-start | bytes 3538948
  2.1 5.8 %copy-start.4 = (s32[1024,96]{0,1:T(8,128)S(1)}, s32[1024,96]{0,1:T(8,128)}, u32[]{:S(2)}) copy-start(s32[1024,96]{0,1:T(8,128)} %param.5) | copy-start | bytes 1179652
  2.1 9.5 %collective-permute-start.4 = (bf16[64,384]{1,0:T(8,128)(2,1)S(1)}, bf16[64,384]{1,0:T(8,128)(2,1)S(1)}, u32[]{:S(2)}, u32[]{:S(2)}) collective-permute-start(bf16[64,384]{1,0:T(8,128)(2,1)S(1)} %take_half.1.refs_4_), channel_id=1, source_target_pairs={{0,12},{4,8},{8,4},{12,0},{1,13},{5,9},{9,5},{13,1},{2,14},{6,10},... | collective-permute-start | bytes 147464 | tf_op jit(solution)/shard_map/ppermute | solution.py:339
  7.2 5.0 %collective-permute-start.3 = (bf16[64,384]{1,0:T(8,128)(2,1)S(1)}, bf16[64,384]{1,0:T(8,128)(2,1)S(1)}, u32[]{:S(2)}, u32[]{:S(2)}) collective-permute-start(bf16[64,384]{1,0:T(8,128)(2,1)S(1)} %take_half.1.refs_4_), channel_id=1, source_target_pairs={{0,8},{4,12},{8,0},{12,4},{1,9},{5,13},{9,1},{13,5},{2,10},{6,14},... | collective-permute-start | bytes 147464 | tf_op jit(solution)/shard_map/ppermute | solution.py:339
  7.2 5.0 %collective-permute-start.2 = (bf16[64,384]{1,0:T(8,128)(2,1)S(1)}, bf16[64,384]{1,0:T(8,128)(2,1)S(1)}, u32[]{:S(2)}, u32[]{:S(2)}) collective-permute-start(bf16[64,384]{1,0:T(8,128)(2,1)S(1)} %take_half.1.refs_4_), channel_id=1, source_target_pairs={{0,4},{4,0},{8,12},{12,8},{1,5},{5,1},{9,13},{13,9},{2,6},{6,2},{1... | collective-permute-start | bytes 147464 | tf_op jit(solution)/shard_map/ppermute | solution.py:339
  15.4 8.2 %collective-permute-start.9 = (s16[1088,128]{1,0:T(8,128)(2,1)S(1)}, s16[1088,128]{1,0:T(8,128)(2,1)S(1)}, u32[]{:S(2)}, u32[]{:S(2)}) collective-permute-start(s16[1088,128]{1,0:T(8,128)(2,1)S(1)} %get-tuple-element.25), channel_id=1, source_target_pairs={{0,2},{1,3},{2,0},{3,1},{4,6},{5,7},{6,4},{7,5},{8,10},{9,11},{10,... | collective-permute-start | bytes 835592 | tf_op jit(solution)/shard_map/ppermute | solution.py:336
  16.9 10.3 %collective-permute-start.5 = (s16[304,128]{1,0:T(8,128)(2,1)S(1)}, s16[304,128]{1,0:T(8,128)(2,1)S(1)}, u32[]{:S(2)}, u32[]{:S(2)}) collective-permute-start(s16[304,128]{1,0:T(8,128)(2,1)S(1)} %get-tuple-element.20), channel_id=1, source_target_pairs={{0,12},{4,8},{8,4},{12,0},{1,13},{5,9},{9,5},{13,1},{2,14},{6,10},... | collective-permute-start | bytes 233480 | tf_op jit(solution)/shard_map/ppermute | solution.py:339
  20.1 7.6 %collective-permute-start.6 = (s16[304,128]{1,0:T(8,128)(2,1)S(1)}, s16[304,128]{1,0:T(8,128)(2,1)S(1)}, u32[]{:S(2)}, u32[]{:S(2)}) collective-permute-start(s16[304,128]{1,0:T(8,128)(2,1)S(1)} %get-tuple-element.21), channel_id=1, source_target_pairs={{0,8},{4,12},{8,0},{12,4},{1,9},{5,13},{9,1},{13,5},{2,10},{6,14},... | collective-permute-start | bytes 233480 | tf_op jit(solution)/shard_map/ppermute | solution.py:339
  20.1 7.6 %collective-permute-start.7 = (s16[304,128]{1,0:T(8,128)(2,1)S(1)}, s16[304,128]{1,0:T(8,128)(2,1)S(1)}, u32[]{:S(2)}, u32[]{:S(2)}) collective-permute-start(s16[304,128]{1,0:T(8,128)(2,1)S(1)} %get-tuple-element.22), channel_id=1, source_target_pairs={{0,4},{4,0},{8,12},{12,8},{1,5},{5,1},{9,13},{13,9},{2,6},{6,2},{1... | collective-permute-start | bytes 233480 | tf_op jit(solution)/shard_map/ppermute | solution.py:339
  23.5 14.5 %copy-start.1 = (bf16[64,768]{1,0:T(8,128)(2,1)S(1)}, bf16[64,768]{1,0:T(8,128)(2,1)}, u32[]{:S(2)}) copy-start(bf16[64,768]{1,0:T(8,128)(2,1)} %refs_8_.1) | copy-start | bytes 294916
  23.8 6.7 %collective-permute-start.10 = (s16[272,128]{1,0:T(8,128)(2,1)S(1)}, s16[272,128]{1,0:T(8,128)(2,1)S(1)}, u32[]{:S(2)}, u32[]{:S(2)}) collective-permute-start(s16[272,128]{1,0:T(8,128)(2,1)S(1)} %get-tuple-element.27), channel_id=1, source_target_pairs={{0,8},{4,12},{8,0},{12,4},{1,9},{5,13},{9,1},{13,5},{2,10},{6,14},... | collective-permute-start | bytes 208904 | tf_op jit(solution)/shard_map/ppermute | solution.py:339
  25.6 6.3 %collective-permute-start.11 = (s16[272,128]{1,0:T(8,128)(2,1)S(1)}, s16[272,128]{1,0:T(8,128)(2,1)S(1)}, u32[]{:S(2)}, u32[]{:S(2)}) collective-permute-start(s16[272,128]{1,0:T(8,128)(2,1)S(1)} %get-tuple-element.28), channel_id=1, source_target_pairs={{0,12},{4,8},{8,4},{12,0},{1,13},{5,9},{9,5},{13,1},{2,14},{6,10},... | collective-permute-start | bytes 208904 | tf_op jit(solution)/shard_map/ppermute | solution.py:339
  27.2 5.1 %collective-permute-start.12 = (s16[272,128]{1,0:T(8,128)(2,1)S(1)}, s16[272,128]{1,0:T(8,128)(2,1)S(1)}, u32[]{:S(2)}, u32[]{:S(2)}) collective-permute-start(s16[272,128]{1,0:T(8,128)(2,1)S(1)} %get-tuple-element.29), channel_id=1, source_target_pairs={{0,4},{4,0},{8,12},{12,8},{1,5},{5,1},{9,13},{13,9},{2,6},{6,2},{1... | collective-permute-start | bytes 208904 | tf_op jit(solution)/shard_map/ppermute | solution.py:339
  27.8 6.0 %collective-permute-start.8 = (s16[304,128]{1,0:T(8,128)(2,1)S(1)}, s16[304,128]{1,0:T(8,128)(2,1)S(1)}, u32[]{:S(2)}, u32[]{:S(2)}) collective-permute-start(s16[304,128]{1,0:T(8,128)(2,1)S(1)} %add_early.1.refs_0_), channel_id=1, source_target_pairs={{0,2},{1,3},{2,0},{3,1},{4,6},{5,7},{6,4},{7,5},{8,10},{9,11},{10,... | collective-permute-start | bytes 233480 | tf_op jit(solution)/shard_map/ppermute | solution.py:336
  32.4 4.4 %collective-permute-start.13 = (s16[272,128]{1,0:T(8,128)(2,1)S(1)}, s16[272,128]{1,0:T(8,128)(2,1)S(1)}, u32[]{:S(2)}, u32[]{:S(2)}) collective-permute-start(s16[272,128]{1,0:T(8,128)(2,1)S(1)} %add_late.1.refs_2_), channel_id=1, source_target_pairs={{0,2},{1,3},{2,0},{3,1},{4,6},{5,7},{6,4},{7,5},{8,10},{9,11},{10,... | collective-permute-start | bytes 208904 | tf_op jit(solution)/shard_map/ppermute | solution.py:336
  33.7 3.0 %collective-permute-start.14 = (s16[304,128]{1,0:T(8,128)(2,1)S(1)}, s16[304,128]{1,0:T(8,128)(2,1)S(1)}, u32[]{:S(2)}, u32[]{:S(2)}) collective-permute-start(s16[304,128]{1,0:T(8,128)(2,1)S(1)} %add_early.1.refs_0_), channel_id=1, source_target_pairs={{0,1},{1,0},{2,3},{3,2},{4,5},{5,4},{6,7},{7,6},{8,9},{9,8},{10,11... | collective-permute-start | bytes 233480 | tf_op jit(solution)/shard_map/ppermute | solution.py:336
  33.8 3.0 %collective-permute-start.15 = (s16[304,128]{1,0:T(8,128)(2,1)S(1)}, s16[304,128]{1,0:T(8,128)(2,1)S(1)}, u32[]{:S(2)}, u32[]{:S(2)}) collective-permute-start(s16[304,128]{1,0:T(8,128)(2,1)S(1)} %collective-permute-done.8.refs_1_), channel_id=1, source_target_pairs={{0,1},{1,0},{2,3},{3,2},{4,5},{5,4},{6,7},{7,6},{8,9},{9,8},{10,11... | collective-permute-start | bytes 233480 | tf_op jit(solution)/shard_map/ppermute | solution.py:336
  34.3 2.5 %collective-permute-start.16 = (s16[272,128]{1,0:T(8,128)(2,1)S(1)}, s16[272,128]{1,0:T(8,128)(2,1)S(1)}, u32[]{:S(2)}, u32[]{:S(2)}) collective-permute-start(s16[272,128]{1,0:T(8,128)(2,1)S(1)} %add_late.1.refs_2_), channel_id=1, source_target_pairs={{0,1},{1,0},{2,3},{3,2},{4,5},{5,4},{6,7},{7,6},{8,9},{9,8},{10,11... | collective-permute-start | bytes 208904 | tf_op jit(solution)/shard_map/ppermute | solution.py:336
  36.7 1.3 %collective-permute-start.17 = (s16[272,128]{1,0:T(8,128)(2,1)S(1)}, s16[272,128]{1,0:T(8,128)(2,1)S(1)}, u32[]{:S(2)}, u32[]{:S(2)}) collective-permute-start(s16[272,128]{1,0:T(8,128)(2,1)S(1)} %collective-permute-done.13.refs_3_), channel_id=1, source_target_pairs={{0,1},{1,0},{2,3},{3,2},{4,5},{5,4},{6,7},{7,6},{8,9},{9,8},{10,11... | collective-permute-start | bytes 208904 | tf_op jit(solution)/shard_map/ppermute | solution.py:336

commit v6 on v5

--- a/solution.py
+++ b/solution.py
@@ -101,7 +101,7 @@
     out[...] = codebook[:, cols]
 
 
-def begin_kernel(shape, e0, e1, c0, c1, rot, out, codes, rt, v0, lhs, rhs, total):
+def begin_kernel(shape, e0, e1, c0, c1, rot, out, codes, rt, lhs, rhs, total):
     rows, half, n_words, n_out = shape
     subs = codes.shape[0]
     core, cols = my_half(half)
@@ -111,7 +111,6 @@
         at = slice(i * rows, (i + 1) * rows)
         codes[:, at] = c[mine, :]
         rt[:, at] = lax.dot_general(rot_t, e[...], nt, preferred_element_type=f32).astype(bf16)
-    v0[...] = e0[...]
     x = lax.axis_index("replica") // 2
     half_sums(0 if n_out == 1 else 1 - x, n_words, codes, rt, lhs, rhs, total)
     if n_out == 1:
@@ -126,7 +125,7 @@
 
 def cross_kernel(shape, e0, e1, codes, first, *rest):
     rows, half, n_words, n_book, n_out = shape
-    books, outs, (book, recon, turned, total) = rest[:n_book], rest[n_book:-4], rest[-4:]
+    books, outs, (book, recon, total) = rest[:n_book], rest[n_book:-3], rest[-3:]
     me = lax.axis_index("dp")
     owned = n_words // n_book
     for i, k in enumerate((0,) + book_order if n_book > 1 else (0,)):
@@ -151,12 +150,12 @@
             recon[p * 16 : (p + 1) * 16, :] = jnp.concatenate(made, axis=0).astype(bf16)
         cut = slice(part * lane, (part + 1) * lane)
         got = jnp.dot(recon[cut, :rows], e0[...], preferred_element_type=f32)
-        turned[cut, :] = got + jnp.dot(recon[cut, rows:], e1[...], preferred_element_type=f32)
+        got += jnp.dot(recon[cut, rows:], e1[...], preferred_element_type=f32)
+        total[:, cut] = got.T
     if n_out == 1:
-        outs[0][...] = turned[...].T
+        outs[0][...] = total[...]
         outs[1][...] = first[...]
         return
-    total[...] = turned[...].T
     own, own_late, message, *sent = outs
     block, sums = total.shape[0] // n_out, first.shape[0] // n_out
     early, late = block // 2, block // 4
@@ -220,7 +219,7 @@
             ones.append(jnp.where(both == (row8 & (coarse - 1)), 1.0, 0.0))
         base = coarse * pack * 8
         lhs[b, base : base + 16, :] = jnp.concatenate(ones, axis=0).astype(bf16)
-        got = lax.dot_general(lhs[b], rhs[b], nt, preferred_element_type=f32)
+        got = lax.dot_general(rhs[b], lhs[b], nt, preferred_element_type=f32).T
         counts = jnp.where(count_row == count_sub, got[base : base + 16], 0.0)
         counts = counts[:8] + counts[8:]
         counts = counts[:coarse] + counts[coarse:]
@@ -364,13 +363,12 @@
         pltpu.VMEM((2, pack * fine, 2 * rows), bf16),
         pltpu.VMEM(sums_shape, f32),
     ]
-    first, my_codes, rt, e0 = call(
+    first, my_codes, rt = call(
         lambda *refs: begin_kernel((rows, half, n_words, n_out), *refs),
         [
             jax.ShapeDtypeStruct(sums_shape, f32),
             jax.ShapeDtypeStruct((n_sub // 2, 2 * rows), i32),
             jax.ShapeDtypeStruct((half, 2 * rows), bf16),
-            jax.ShapeDtypeStruct(embeddings.shape, bf16),
         ],
         (embeddings, e1, c0, c1, rotation),
         buffers,
@@ -391,11 +389,10 @@
     cross = call(
         lambda *refs: cross_kernel((rows, half, n_words, len(books), n_out), *refs),
         cross_outs,
-        (e0, e1, my_codes, first, *books),
+        (embeddings, e1, my_codes, first, *books),
         [
             pltpu.VMEM((n_words, half), f32),
             pltpu.VMEM((half, 2 * rows), bf16),
-            pltpu.VMEM((half, width), f32),
             pltpu.VMEM((width, half), f32),
         ],
         "cross_terms",

time: 39.3 us -> 39 us (level)
  waiting for transfers between devices: 7.59 us -> 8.35 us
  Pallas kernels: 10.7 us -> 10 us
  starting transfers between devices: 19.2 us -> 18.8 us
    ppermute x9, waiting for transfers between devices: 3.87 us -> 4.58 us  [exchange(): lax.ppermute(blocks[hops.index(k)], 'dp', [(i, i ^ k) for i in range(n)])]
    pallas_call x8, Pallas kernels: 10.7 us -> 10 us  [call(): pl.pallas_call(kernel, out_shape=outs, in_specs=[pl.BlockSpec(memory_spac...]
  transfers between devices with their start and end apart: 18 -> 18, of which waited for: 6 -> 7; matrix products, arithmetic and copies ran while one was open for 0% -> 0% of each run, Pallas kernels for 16% -> 15%
where the time goes in v6:
time: 39 us; the launch traced here: 38.8 us
  starting transfers between devices  18.8 us (48%)
  Pallas kernels  10 us (26%)
  waiting for transfers between devices  8.35 us (21%)
  local copies, waits for them, and re-layouts  0.91 us (2%)
  between operations  0.74 us (2%)
    ppermute x9, starting transfers between devices, exchange(): lax.ppermute(blocks[hops.index(k)], 'dp', [(i, i ^ k) for i in range(n)])  13.7 us
    pallas_call x8, Pallas kernels, call(): pl.pallas_call(kernel, out_shape=outs, in_specs=[pl.BlockSpec(memory_spac...  10 us
    ppermute x9, starting transfers between devices, swap(): return lax.ppermute(x, 'replica', [(i, i ^ bit) for i in range(replicas)])  5.1 us
    ppermute x9, waiting for transfers between devices, exchange(): lax.ppermute(blocks[hops.index(k)], 'dp', [(i, i ^ k) for i in range(n)])  4.58 us
    ppermute x9, waiting for transfers between devices, swap(): return lax.ppermute(x, 'replica', [(i, i ^ bit) for i in range(replicas)])  3.76 us
    unnamed x10, local copies, waits for them, and re-layouts  0.91 us
  transfers between devices with their start and end apart: 18, of which 7 were waited for; matrix products, arithmetic and copies ran while one was open for 0% of the time, Pallas kernels for 15%

profile of v6, /device:TPU:0, one launch (start us, length us, event | category | flops | bytes accessed | tf_op | source)
XLA Modules:
  0.0 38.8 jit_solution(13182219544215737218)
XLA Ops:
  0.6 0.5 %collective-permute-start.1 = (s32[96,1024]{1,0:T(8,128)}, s32[96,1024]{1,0:T(8,128)S(1)}, u32[]{:S(2)}, u32[]{:S(2)}) collective-permute-start(s32[96,1024]{1,0:T(8,128)} %bitcast.1), channel_id=1, source_target_pairs={{0,1},{1,0},{2,3},{3,2},{4,5},{5,4},{6,7},{7,6},{8,9},{9,8},{10,11... | collective-permute-start | bytes 1179656 | tf_op jit(solution)/shard_map/ppermute | solution.py:335
  1.1 0.1 collective-permute-start
  1.2 0.9 %copy-done = bf16[64,768]{1,0:T(8,128)(2,1)S(1)} copy-done((bf16[64,768]{1,0:T(8,128)(2,1)S(1)}, bf16[64,768]{1,0:T(8,128)(2,1)}, u32[]{:S(2)}) %copy-start) | copy-done | bytes 98328
  2.1 5.1 %collective-permute-start.4 = (bf16[64,384]{1,0:T(8,128)(2,1)S(1)}, bf16[64,384]{1,0:T(8,128)(2,1)S(1)}, u32[]{:S(2)}, u32[]{:S(2)}) collective-permute-start(bf16[64,384]{1,0:T(8,128)(2,1)S(1)} %take_half.1.refs_4_), channel_id=1, source_target_pairs={{0,12},{4,8},{8,4},{12,0},{1,13},{5,9},{9,5},{13,1},{2,14},{6,10},... | collective-permute-start | bytes 147464 | tf_op jit(solution)/shard_map/ppermute | solution.py:338
  7.2 0.0 collective-permute-start.3
  7.2 0.6 %collective-permute-start.2 = (bf16[64,384]{1,0:T(8,128)(2,1)S(1)}, bf16[64,384]{1,0:T(8,128)(2,1)S(1)}, u32[]{:S(2)}, u32[]{:S(2)}) collective-permute-start(bf16[64,384]{1,0:T(8,128)(2,1)S(1)} %take_half.1.refs_4_), channel_id=1, source_target_pairs={{0,4},{4,0},{8,12},{12,8},{1,5},{5,1},{9,13},{13,9},{2,6},{6,2},{1... | collective-permute-start | bytes 147464 | tf_op jit(solution)/shard_map/ppermute | solution.py:338
  7.9 0.0 collective-permute-done.1.refs_3_
  7.9 3.4 %begin.1 = (f32[256,256]{1,0:T(8,128)S(1)}, s32[48,2048]{1,0:T(8,128)S(1)}, bf16[384,2048]{1,0:T(8,128)(2,1)S(1)}) custom-call(bf16[1024,768]{1,0:T(8,128)(2,1)S(1)} %copy-done.2, bf16[1024,768]{1,0:T(8,128)(2,1)S(1)} %collective-permute-done.refs_1_, s32[96,1024]{1,0:T(8,128)S(1)} %bitcast.2, s32[96,1024]{1,0:T(8,128)S(1)} %collective-permute-done.1.refs_3_, ...), custom_call_target="tpu_custom_call" | custom-call | flops 2415919104 | bytes 7340032 | tf_op jit(solution)/shard_map/begin/pallas_call | solution.py:27
  11.4 0.9 %collective-permute-done.3.refs_6_ = bf16[64,384]{1,0:T(8,128)(2,1)S(1)} collective-permute-done((bf16[64,384]{1,0:T(8,128)(2,1)S(1)}, bf16[64,384]{1,0:T(8,128)(2,1)S(1)}, u32[]{:S(2)}, u32[]{:S(2)}) %collective-permute-start.3) | collective-permute-done | bytes 49184 | tf_op jit(solution)/shard_map/ppermute | solution.py:338
  12.2 3.0 %cross_terms.1 = (f32[96,384]{1,0:T(8,128)S(1)}, f32[192,384]{1,0:T(8,128)S(1)}, s16[1088,128]{1,0:T(8,128)(2,1)S(1)}, s16[304,128]{1,0:T(8,128)(2,1)S(1)}, s16[...) custom-call(bf16[1024,768]{1,0:T(8,128)(2,1)S(1)} %copy-done.2, bf16[1024,768]{1,0:T(8,128)(2,1)S(1)} %collective-permute-done.refs_1_, ...), custom_call_target="tpu_custom_call" | custom-call | flops 1207959552 | bytes 4952064 | tf_op jit(solution)/shard_map/cross_terms/pallas_call | solution.py:27
  15.3 1.5 %collective-permute-start.9 = (s16[1088,128]{1,0:T(8,128)(2,1)S(1)}, s16[1088,128]{1,0:T(8,128)(2,1)S(1)}, u32[]{:S(2)}, u32[]{:S(2)}) collective-permute-start(s16[1088,128]{1,0:T(8,128)(2,1)S(1)} %get-tuple-element.23), channel_id=1, source_target_pairs={{0,2},{1,3},{2,0},{3,1},{4,6},{5,7},{6,4},{7,5},{8,10},{9,11},{10,... | collective-permute-start | bytes 835592 | tf_op jit(solution)/shard_map/ppermute | solution.py:335
  16.8 2.9 %collective-permute-start.5 = (s16[304,128]{1,0:T(8,128)(2,1)S(1)}, s16[304,128]{1,0:T(8,128)(2,1)S(1)}, u32[]{:S(2)}, u32[]{:S(2)}) collective-permute-start(s16[304,128]{1,0:T(8,128)(2,1)S(1)} %get-tuple-element.18), channel_id=1, source_target_pairs={{0,12},{4,8},{8,4},{12,0},{1,13},{5,9},{9,5},{13,1},{2,14},{6,10},... | collective-permute-start | bytes 233480 | tf_op jit(solution)/shard_map/ppermute | solution.py:338
  19.7 1.5 %collective-permute-start.7 = (s16[304,128]{1,0:T(8,128)(2,1)S(1)}, s16[304,128]{1,0:T(8,128)(2,1)S(1)}, u32[]{:S(2)}, u32[]{:S(2)}) collective-permute-start(s16[304,128]{1,0:T(8,128)(2,1)S(1)} %get-tuple-element.20), channel_id=1, source_target_pairs={{0,4},{4,0},{8,12},{12,8},{1,5},{5,1},{9,13},{13,9},{2,6},{6,2},{1... | collective-permute-start | bytes 233480 | tf_op jit(solution)/shard_map/ppermute | solution.py:338
  21.2 1.9 %codeword_sums.1.refs_1_ = f32[256,256]{1,0:T(8,128)S(1)} custom-call(s32[48,2048]{1,0:T(8,128)S(1)} %get-tuple-element.15.refs_2_.refs_0_, bf16[384,2048]{1,0:T(8,128)(2,1)S(1)} %get-tuple-element.22.refs_1_, f32[96,384]{1,0:T(8,128)S(1)} %get-tuple-element.17.own.refs_2_), custom_call_target="tpu_custom_call" | custom-call | flops 2415919104 | bytes 2375680 | tf_op jit(solution)/shard_map/codeword_sums/pallas_call | solution.py:27
  23.1 0.0 copy-start.1
  23.2 0.3 add_half.1
  23.4 1.8 %collective-permute-start.10 = (s16[272,128]{1,0:T(8,128)(2,1)S(1)}, s16[272,128]{1,0:T(8,128)(2,1)S(1)}, u32[]{:S(2)}, u32[]{:S(2)}) collective-permute-start(s16[272,128]{1,0:T(8,128)(2,1)S(1)} %get-tuple-element.25), channel_id=1, source_target_pairs={{0,8},{4,12},{8,0},{12,4},{1,9},{5,13},{9,1},{13,5},{2,10},{6,14},... | collective-permute-start | bytes 208904 | tf_op jit(solution)/shard_map/ppermute | solution.py:338
  25.2 1.5 %collective-permute-start.11 = (s16[272,128]{1,0:T(8,128)(2,1)S(1)}, s16[272,128]{1,0:T(8,128)(2,1)S(1)}, u32[]{:S(2)}, u32[]{:S(2)}) collective-permute-start(s16[272,128]{1,0:T(8,128)(2,1)S(1)} %get-tuple-element.26), channel_id=1, source_target_pairs={{0,12},{4,8},{8,4},{12,0},{1,13},{5,9},{9,5},{13,1},{2,14},{6,10},... | collective-permute-start | bytes 208904 | tf_op jit(solution)/shard_map/ppermute | solution.py:338
  26.7 0.3 collective-permute-start.12
  27.0 0.4 %collective-permute-done.6.rest_1_ = s16[304,128]{1,0:T(8,128)(2,1)S(1)} collective-permute-done((s16[304,128]{1,0:T(8,128)(2,1)S(1)}, s16[304,128]{1,0:T(8,128)(2,1)S(1)}, u32[]{:S(2)}, u32[]{:S(2)}) %collective-permute-start.6) | collective-permute-done | bytes 77856 | tf_op jit(solution)/shard_map/ppermute | solution.py:338
  27.4 0.1 add_early.1.refs_0_
  27.5 1.1 %collective-permute-start.8 = (s16[304,128]{1,0:T(8,128)(2,1)S(1)}, s16[304,128]{1,0:T(8,128)(2,1)S(1)}, u32[]{:S(2)}, u32[]{:S(2)}) collective-permute-start(s16[304,128]{1,0:T(8,128)(2,1)S(1)} %add_early.1.refs_0_), channel_id=1, source_target_pairs={{0,2},{1,3},{2,0},{3,1},{4,6},{5,7},{6,4},{7,5},{8,10},{9,11},{10,... | collective-permute-start | bytes 233480 | tf_op jit(solution)/shard_map/ppermute | solution.py:335
  28.6 1.8 %collective-permute-done.10.refs_1_ = s16[272,128]{1,0:T(8,128)(2,1)S(1)} collective-permute-done((s16[272,128]{1,0:T(8,128)(2,1)S(1)}, s16[272,128]{1,0:T(8,128)(2,1)S(1)}, u32[]{:S(2)}, u32[]{:S(2)}) %collective-permute-start.10) | collective-permute-done | bytes 69664 | tf_op jit(solution)/shard_map/ppermute | solution.py:338
  30.4 1.0 %collective-permute-done.11.refs_2_ = s16[272,128]{1,0:T(8,128)(2,1)S(1)} collective-permute-done((s16[272,128]{1,0:T(8,128)(2,1)S(1)}, s16[272,128]{1,0:T(8,128)(2,1)S(1)}, u32[]{:S(2)}, u32[]{:S(2)}) %collective-permute-start.11) | collective-permute-done | bytes 69664 | tf_op jit(solution)/shard_map/ppermute | solution.py:338
  31.5 0.4 %collective-permute-done.12.refs_3_ = s16[272,128]{1,0:T(8,128)(2,1)S(1)} collective-permute-done((s16[272,128]{1,0:T(8,128)(2,1)S(1)}, s16[272,128]{1,0:T(8,128)(2,1)S(1)}, u32[]{:S(2)}, u32[]{:S(2)}) %collective-permute-start.12) | collective-permute-done | bytes 69664 | tf_op jit(solution)/shard_map/ppermute | solution.py:338
  31.9 0.1 add_late.1.refs_2_
  32.1 1.3 %collective-permute-start.13 = (s16[272,128]{1,0:T(8,128)(2,1)S(1)}, s16[272,128]{1,0:T(8,128)(2,1)S(1)}, u32[]{:S(2)}, u32[]{:S(2)}) collective-permute-start(s16[272,128]{1,0:T(8,128)(2,1)S(1)} %add_late.1.refs_2_), channel_id=1, source_target_pairs={{0,2},{1,3},{2,0},{3,1},{4,6},{5,7},{6,4},{7,5},{8,10},{9,11},{10,... | collective-permute-start | bytes 208904 | tf_op jit(solution)/shard_map/ppermute | solution.py:335
  33.4 0.5 %collective-permute-start.15 = (s16[304,128]{1,0:T(8,128)(2,1)S(1)}, s16[304,128]{1,0:T(8,128)(2,1)S(1)}, u32[]{:S(2)}, u32[]{:S(2)}) collective-permute-start(s16[304,128]{1,0:T(8,128)(2,1)S(1)} %collective-permute-done.8.refs_1_), channel_id=1, source_target_pairs={{0,1},{1,0},{2,3},{3,2},{4,5},{5,4},{6,7},{7,6},{8,9},{9,8},{10,11... | collective-permute-start | bytes 233480 | tf_op jit(solution)/shard_map/ppermute | solution.py:335
  33.9 0.0 collective-permute-start.16
  33.9 2.5 %collective-permute-done.13.refs_3_ = s16[272,128]{1,0:T(8,128)(2,1)S(1)} collective-permute-done((s16[272,128]{1,0:T(8,128)(2,1)S(1)}, s16[272,128]{1,0:T(8,128)(2,1)S(1)}, u32[]{:S(2)}, u32[]{:S(2)}) %collective-permute-start.13) | collective-permute-done | bytes 69664 | tf_op jit(solution)/shard_map/ppermute | solution.py:335
  36.5 1.2 %collective-permute-done.17.refs_7_ = s16[272,128]{1,0:T(8,128)(2,1)S(1)} collective-permute-done((s16[272,128]{1,0:T(8,128)(2,1)S(1)}, s16[272,128]{1,0:T(8,128)(2,1)S(1)}, u32[]{:S(2)}, u32[]{:S(2)}) %collective-permute-start.17) | collective-permute-done | bytes 69664 | tf_op jit(solution)/shard_map/ppermute | solution.py:335
  37.7 1.1 %finish.1 = (f32[64,768]{1,0:T(8,128)}, f32[192,768]{1,0:T(8,128)}) custom-call(s16[304,128]{1,0:T(8,128)(2,1)S(1)} %add_early.1.refs_0_, s16[304,128]{1,0:T(8,128)(2,1)S(1)} %collective-permute-done.8.refs_1_, s16[272,128]{1,0:T(8,128)(2,1)S(1)} %add_late.1.refs_2_, s16[272,128]{1,0:T(8,128)(2,1)S(1)} %collective-permute-done.13.refs_3_, ...), custom_call_target="tpu_custom_call" | custom-call | bytes 1474560 | tf_op jit(solution)/shard_map/finish/pallas_call | solution.py:27
  (22 shorter events, 0.1 us)
Async XLA Ops:
  0.6 7.2 %collective-permute-start.1 = (s32[96,1024]{1,0:T(8,128)}, s32[96,1024]{1,0:T(8,128)S(1)}, u32[]{:S(2)}, u32[]{:S(2)}) collective-permute-start(s32[96,1024]{1,0:T(8,128)} %bitcast.1), channel_id=1, source_target_pairs={{0,1},{1,0},{2,3},{3,2},{4,5},{5,4},{6,7},{7,6},{8,9},{9,8},{10,11... | collective-permute-start | bytes 1179656 | tf_op jit(solution)/shard_map/ppermute | solution.py:335
  1.1 6.7 %collective-permute-start = (bf16[1024,768]{1,0:T(8,128)(2,1)}, bf16[1024,768]{1,0:T(8,128)(2,1)S(1)}, u32[]{:S(2)}, u32[]{:S(2)}) collective-permute-start(bf16[1024,768]{1,0:T(8,128)(2,1)} %refs_0_.3), channel_id=1, source_target_pairs={{0,1},{1,0},{2,3},{3,2},{4,5},{5,4},{6,7},{7,6},{8,9},{9,8},{10,11... | collective-permute-start | bytes 4718600 | tf_op jit(solution)/shard_map/ppermute | solution.py:335
  1.2 0.9 %copy-start = (bf16[64,768]{1,0:T(8,128)(2,1)S(1)}, bf16[64,768]{1,0:T(8,128)(2,1)}, u32[]{:S(2)}) copy-start(bf16[64,768]{1,0:T(8,128)(2,1)} %refs_8_.1) | copy-start | bytes 294916
  2.1 5.8 %copy-start.2 = (bf16[1024,768]{1,0:T(8,128)(2,1)S(1)}, bf16[1024,768]{1,0:T(8,128)(2,1)}, u32[]{:S(2)}) copy-start(bf16[1024,768]{1,0:T(8,128)(2,1)} %refs_0_.3) | copy-start | bytes 4718596
  2.1 5.8 %copy-start.3 = (bf16[768,768]{1,0:T(8,128)(2,1)S(1)}, bf16[768,768]{1,0:T(8,128)(2,1)}, u32[]{:S(2)}) copy-start(bf16[768,768]{1,0:T(8,128)(2,1)} %refs_4_.1) | copy-start | bytes 3538948
  2.1 5.8 %copy-start.4 = (s32[1024,96]{0,1:T(8,128)S(1)}, s32[1024,96]{0,1:T(8,128)}, u32[]{:S(2)}) copy-start(s32[1024,96]{0,1:T(8,128)} %param.5) | copy-start | bytes 1179652
  2.1 9.2 %collective-permute-start.4 = (bf16[64,384]{1,0:T(8,128)(2,1)S(1)}, bf16[64,384]{1,0:T(8,128)(2,1)S(1)}, u32[]{:S(2)}, u32[]{:S(2)}) collective-permute-start(bf16[64,384]{1,0:T(8,128)(2,1)S(1)} %take_half.1.refs_4_), channel_id=1, source_target_pairs={{0,12},{4,8},{8,4},{12,0},{1,13},{5,9},{9,5},{13,1},{2,14},{6,10},... | collective-permute-start | bytes 147464 | tf_op jit(solution)/shard_map/ppermute | solution.py:338
  7.2 5.0 %collective-permute-start.3 = (bf16[64,384]{1,0:T(8,128)(2,1)S(1)}, bf16[64,384]{1,0:T(8,128)(2,1)S(1)}, u32[]{:S(2)}, u32[]{:S(2)}) collective-permute-start(bf16[64,384]{1,0:T(8,128)(2,1)S(1)} %take_half.1.refs_4_), channel_id=1, source_target_pairs={{0,8},{4,12},{8,0},{12,4},{1,9},{5,13},{9,1},{13,5},{2,10},{6,14},... | collective-permute-start | bytes 147464 | tf_op jit(solution)/shard_map/ppermute | solution.py:338
  7.2 5.0 %collective-permute-start.2 = (bf16[64,384]{1,0:T(8,128)(2,1)S(1)}, bf16[64,384]{1,0:T(8,128)(2,1)S(1)}, u32[]{:S(2)}, u32[]{:S(2)}) collective-permute-start(bf16[64,384]{1,0:T(8,128)(2,1)S(1)} %take_half.1.refs_4_), channel_id=1, source_target_pairs={{0,4},{4,0},{8,12},{12,8},{1,5},{5,1},{9,13},{13,9},{2,6},{6,2},{1... | collective-permute-start | bytes 147464 | tf_op jit(solution)/shard_map/ppermute | solution.py:338
  15.3 7.9 %collective-permute-start.9 = (s16[1088,128]{1,0:T(8,128)(2,1)S(1)}, s16[1088,128]{1,0:T(8,128)(2,1)S(1)}, u32[]{:S(2)}, u32[]{:S(2)}) collective-permute-start(s16[1088,128]{1,0:T(8,128)(2,1)S(1)} %get-tuple-element.23), channel_id=1, source_target_pairs={{0,2},{1,3},{2,0},{3,1},{4,6},{5,7},{6,4},{7,5},{8,10},{9,11},{10,... | collective-permute-start | bytes 835592 | tf_op jit(solution)/shard_map/ppermute | solution.py:335
  16.8 9.9 %collective-permute-start.5 = (s16[304,128]{1,0:T(8,128)(2,1)S(1)}, s16[304,128]{1,0:T(8,128)(2,1)S(1)}, u32[]{:S(2)}, u32[]{:S(2)}) collective-permute-start(s16[304,128]{1,0:T(8,128)(2,1)S(1)} %get-tuple-element.18), channel_id=1, source_target_pairs={{0,12},{4,8},{8,4},{12,0},{1,13},{5,9},{9,5},{13,1},{2,14},{6,10},... | collective-permute-start | bytes 233480 | tf_op jit(solution)/shard_map/ppermute | solution.py:338
  19.7 7.7 %collective-permute-start.6 = (s16[304,128]{1,0:T(8,128)(2,1)S(1)}, s16[304,128]{1,0:T(8,128)(2,1)S(1)}, u32[]{:S(2)}, u32[]{:S(2)}) collective-permute-start(s16[304,128]{1,0:T(8,128)(2,1)S(1)} %get-tuple-element.19), channel_id=1, source_target_pairs={{0,8},{4,12},{8,0},{12,4},{1,9},{5,13},{9,1},{13,5},{2,10},{6,14},... | collective-permute-start | bytes 233480 | tf_op jit(solution)/shard_map/ppermute | solution.py:338
  19.7 7.7 %collective-permute-start.7 = (s16[304,128]{1,0:T(8,128)(2,1)S(1)}, s16[304,128]{1,0:T(8,128)(2,1)S(1)}, u32[]{:S(2)}, u32[]{:S(2)}) collective-permute-start(s16[304,128]{1,0:T(8,128)(2,1)S(1)} %get-tuple-element.20), channel_id=1, source_target_pairs={{0,4},{4,0},{8,12},{12,8},{1,5},{5,1},{9,13},{13,9},{2,6},{6,2},{1... | collective-permute-start | bytes 233480 | tf_op jit(solution)/shard_map/ppermute | solution.py:338
  23.1 14.6 %copy-start.1 = (bf16[64,768]{1,0:T(8,128)(2,1)S(1)}, bf16[64,768]{1,0:T(8,128)(2,1)}, u32[]{:S(2)}) copy-start(bf16[64,768]{1,0:T(8,128)(2,1)} %refs_8_.1) | copy-start | bytes 294916
  23.4 7.0 %collective-permute-start.10 = (s16[272,128]{1,0:T(8,128)(2,1)S(1)}, s16[272,128]{1,0:T(8,128)(2,1)S(1)}, u32[]{:S(2)}, u32[]{:S(2)}) collective-permute-start(s16[272,128]{1,0:T(8,128)(2,1)S(1)} %get-tuple-element.25), channel_id=1, source_target_pairs={{0,8},{4,12},{8,0},{12,4},{1,9},{5,13},{9,1},{13,5},{2,10},{6,14},... | collective-permute-start | bytes 208904 | tf_op jit(solution)/shard_map/ppermute | solution.py:338
  25.2 6.3 %collective-permute-start.11 = (s16[272,128]{1,0:T(8,128)(2,1)S(1)}, s16[272,128]{1,0:T(8,128)(2,1)S(1)}, u32[]{:S(2)}, u32[]{:S(2)}) collective-permute-start(s16[272,128]{1,0:T(8,128)(2,1)S(1)} %get-tuple-element.26), channel_id=1, source_target_pairs={{0,12},{4,8},{8,4},{12,0},{1,13},{5,9},{9,5},{13,1},{2,14},{6,10},... | collective-permute-start | bytes 208904 | tf_op jit(solution)/shard_map/ppermute | solution.py:338
  26.7 5.2 %collective-permute-start.12 = (s16[272,128]{1,0:T(8,128)(2,1)S(1)}, s16[272,128]{1,0:T(8,128)(2,1)S(1)}, u32[]{:S(2)}, u32[]{:S(2)}) collective-permute-start(s16[272,128]{1,0:T(8,128)(2,1)S(1)} %get-tuple-element.27), channel_id=1, source_target_pairs={{0,4},{4,0},{8,12},{12,8},{1,5},{5,1},{9,13},{13,9},{2,6},{6,2},{1... | collective-permute-start | bytes 208904 | tf_op jit(solution)/shard_map/ppermute | solution.py:338
  27.5 5.9 %collective-permute-start.8 = (s16[304,128]{1,0:T(8,128)(2,1)S(1)}, s16[304,128]{1,0:T(8,128)(2,1)S(1)}, u32[]{:S(2)}, u32[]{:S(2)}) collective-permute-start(s16[304,128]{1,0:T(8,128)(2,1)S(1)} %add_early.1.refs_0_), channel_id=1, source_target_pairs={{0,2},{1,3},{2,0},{3,1},{4,6},{5,7},{6,4},{7,5},{8,10},{9,11},{10,... | collective-permute-start | bytes 233480 | tf_op jit(solution)/shard_map/ppermute | solution.py:335
  32.1 4.4 %collective-permute-start.13 = (s16[272,128]{1,0:T(8,128)(2,1)S(1)}, s16[272,128]{1,0:T(8,128)(2,1)S(1)}, u32[]{:S(2)}, u32[]{:S(2)}) collective-permute-start(s16[272,128]{1,0:T(8,128)(2,1)S(1)} %add_late.1.refs_2_), channel_id=1, source_target_pairs={{0,2},{1,3},{2,0},{3,1},{4,6},{5,7},{6,4},{7,5},{8,10},{9,11},{10,... | collective-permute-start | bytes 208904 | tf_op jit(solution)/shard_map/ppermute | solution.py:335
  33.4 3.0 %collective-permute-start.14 = (s16[304,128]{1,0:T(8,128)(2,1)S(1)}, s16[304,128]{1,0:T(8,128)(2,1)S(1)}, u32[]{:S(2)}, u32[]{:S(2)}) collective-permute-start(s16[304,128]{1,0:T(8,128)(2,1)S(1)} %add_early.1.refs_0_), channel_id=1, source_target_pairs={{0,1},{1,0},{2,3},{3,2},{4,5},{5,4},{6,7},{7,6},{8,9},{9,8},{10,11... | collective-permute-start | bytes 233480 | tf_op jit(solution)/shard_map/ppermute | solution.py:335
  33.4 3.0 %collective-permute-start.15 = (s16[304,128]{1,0:T(8,128)(2,1)S(1)}, s16[304,128]{1,0:T(8,128)(2,1)S(1)}, u32[]{:S(2)}, u32[]{:S(2)}) collective-permute-start(s16[304,128]{1,0:T(8,128)(2,1)S(1)} %collective-permute-done.8.refs_1_), channel_id=1, source_target_pairs={{0,1},{1,0},{2,3},{3,2},{4,5},{5,4},{6,7},{7,6},{8,9},{9,8},{10,11... | collective-permute-start | bytes 233480 | tf_op jit(solution)/shard_map/ppermute | solution.py:335
  33.9 2.5 %collective-permute-start.16 = (s16[272,128]{1,0:T(8,128)(2,1)S(1)}, s16[272,128]{1,0:T(8,128)(2,1)S(1)}, u32[]{:S(2)}, u32[]{:S(2)}) collective-permute-start(s16[272,128]{1,0:T(8,128)(2,1)S(1)} %add_late.1.refs_2_), channel_id=1, source_target_pairs={{0,1},{1,0},{2,3},{3,2},{4,5},{5,4},{6,7},{7,6},{8,9},{9,8},{10,11... | collective-permute-start | bytes 208904 | tf_op jit(solution)/shard_map/ppermute | solution.py:335
  36.4 1.3 %collective-permute-start.17 = (s16[272,128]{1,0:T(8,128)(2,1)S(1)}, s16[272,128]{1,0:T(8,128)(2,1)S(1)}, u32[]{:S(2)}, u32[]{:S(2)}) collective-permute-start(s16[272,128]{1,0:T(8,128)(2,1)S(1)} %collective-permute-done.13.refs_3_), channel_id=1, source_target_pairs={{0,1},{1,0},{2,3},{3,2},{4,5},{5,4},{6,7},{7,6},{8,9},{9,8},{10,11... | collective-permute-start | bytes 208904 | tf_op jit(solution)/shard_map/ppermute | solution.py:335

commit v7 on v6

--- a/solution.py
+++ b/solution.py
@@ -96,7 +96,11 @@
     return groups * 8 + -(-2 * groups // 16) * 16
 
 
-def take_half_kernel(codebook, out):
+def blank_kernel(out):
+    out[...] = jnp.zeros_like(out)
+
+
+def take_half_kernel(codebook, _, out):
     _, cols = my_half(out.shape[1])
     out[...] = codebook[:, cols]
 
@@ -340,13 +344,15 @@
     e1 = swap(embeddings, 1)
     c0 = codes.T
     c1 = swap(c0, 1)
+    blank = call(blank_kernel, jax.ShapeDtypeStruct((8, lane), f32), (), [], "blank", flops=1 << 34)
     book = call(
         take_half_kernel,
         jax.ShapeDtypeStruct((owned, half), bf16),
-        (codebook,),
+        (codebook, blank),
         [],
         "take_half",
         flops=1 << 34,
+        unread=(1,),
     )
     if direct:
         books = [book] + exchange([book] * len(hops), book_order)

time: 39 us -> 38.1 us (0.977)
  local copies, waits for them, and re-layouts: 0.91 us -> 0.3 us
    unnamed x10 -> x8, local copies, waits for them, and re-layouts: 0.91 us -> 0.3 us
    pallas_call x8 -> x9, Pallas kernels: 10 us -> 10 us  [call(): pl.pallas_call(kernel, out_shape=outs, in_specs=[pl.BlockSpec(memory_spac...]
where the time goes in v7:
time: 38.1 us; the launch traced here: 38 us
  starting transfers between devices  18.9 us (50%)
  Pallas kernels  10 us (26%)
  waiting for transfers between devices  8.01 us (21%)
  between operations  0.74 us (2%)
    ppermute x9, starting transfers between devices, exchange(): lax.ppermute(blocks[hops.index(k)], 'dp', [(i, i ^ k) for i in range(n)])  13.7 us
    pallas_call x9, Pallas kernels, call(): pl.pallas_call(kernel, out_shape=outs, in_specs=[pl.BlockSpec(memory_spac...  10 us
    ppermute x9, starting transfers between devices, swap(): return lax.ppermute(x, 'replica', [(i, i ^ bit) for i in range(replicas)])  5.19 us
    ppermute x9, waiting for transfers between devices, exchange(): lax.ppermute(blocks[hops.index(k)], 'dp', [(i, i ^ k) for i in range(n)])  4.32 us
    ppermute x9, waiting for transfers between devices, swap(): return lax.ppermute(x, 'replica', [(i, i ^ bit) for i in range(replicas)])  3.7 us
  transfers between devices with their start and end apart: 18, of which 7 were waited for; matrix products, arithmetic and copies ran while one was open for 0% of the time, Pallas kernels for 15%

profile of v7, /device:TPU:0, one launch (start us, length us, event | category | flops | bytes accessed | tf_op | source)
XLA Modules:
  0.0 38.0 jit_solution(7080568951595214275)
XLA Ops:
  0.6 0.5 %collective-permute-start.1 = (s32[96,1024]{1,0:T(8,128)}, s32[96,1024]{1,0:T(8,128)S(1)}, u32[]{:S(2)}, u32[]{:S(2)}) collective-permute-start(s32[96,1024]{1,0:T(8,128)} %bitcast.1), channel_id=1, source_target_pairs={{0,1},{1,0},{2,3},{3,2},{4,5},{5,4},{6,7},{7,6},{8,9},{9,8},{10,11... | collective-permute-start | bytes 1179656 | tf_op jit(solution)/shard_map/ppermute | solution.py:339
  1.2 0.1 collective-permute-start
  1.2 0.3 copy-done
  1.5 5.1 %collective-permute-start.4 = (bf16[64,384]{1,0:T(8,128)(2,1)S(1)}, bf16[64,384]{1,0:T(8,128)(2,1)S(1)}, u32[]{:S(2)}, u32[]{:S(2)}) collective-permute-start(bf16[64,384]{1,0:T(8,128)(2,1)S(1)} %take_half.1.refs_4_), channel_id=1, source_target_pairs={{0,12},{4,8},{8,4},{12,0},{1,13},{5,9},{9,5},{13,1},{2,14},{6,10},... | collective-permute-start | bytes 147464 | tf_op jit(solution)/shard_map/ppermute | solution.py:342
  6.7 0.6 %collective-permute-start.2 = (bf16[64,384]{1,0:T(8,128)(2,1)S(1)}, bf16[64,384]{1,0:T(8,128)(2,1)S(1)}, u32[]{:S(2)}, u32[]{:S(2)}) collective-permute-start(bf16[64,384]{1,0:T(8,128)(2,1)S(1)} %take_half.1.refs_4_), channel_id=1, source_target_pairs={{0,4},{4,0},{8,12},{12,8},{1,5},{5,1},{9,13},{13,9},{2,6},{6,2},{1... | collective-permute-start | bytes 147464 | tf_op jit(solution)/shard_map/ppermute | solution.py:342
  7.3 3.4 %begin.1 = (f32[256,256]{1,0:T(8,128)S(1)}, s32[48,2048]{1,0:T(8,128)S(1)}, bf16[384,2048]{1,0:T(8,128)(2,1)S(1)}) custom-call(bf16[1024,768]{1,0:T(8,128)(2,1)S(1)} %copy-done.1, bf16[1024,768]{1,0:T(8,128)(2,1)S(1)} %collective-permute-done.refs_1_, s32[96,1024]{1,0:T(8,128)S(1)} %bitcast.2, s32[96,1024]{1,0:T(8,128)S(1)} %collective-permute-done.1.refs_3_, ...), custom_call_target="tpu_custom_call" | custom-call | flops 2415919104 | bytes 7340032 | tf_op jit(solution)/shard_map/begin/pallas_call | solution.py:27
  10.8 0.0 collective-permute-done.4.refs_7_
  10.8 0.9 %collective-permute-done.3.refs_6_ = bf16[64,384]{1,0:T(8,128)(2,1)S(1)} collective-permute-done((bf16[64,384]{1,0:T(8,128)(2,1)S(1)}, bf16[64,384]{1,0:T(8,128)(2,1)S(1)}, u32[]{:S(2)}, u32[]{:S(2)}) %collective-permute-start.3) | collective-permute-done | bytes 49184 | tf_op jit(solution)/shard_map/ppermute | solution.py:342
  11.6 3.0 %cross_terms.1 = (f32[96,384]{1,0:T(8,128)S(1)}, f32[192,384]{1,0:T(8,128)S(1)}, s16[1088,128]{1,0:T(8,128)(2,1)S(1)}, s16[304,128]{1,0:T(8,128)(2,1)S(1)}, s16[...) custom-call(bf16[1024,768]{1,0:T(8,128)(2,1)S(1)} %copy-done.1, bf16[1024,768]{1,0:T(8,128)(2,1)S(1)} %collective-permute-done.refs_1_, ...), custom_call_target="tpu_custom_call" | custom-call | flops 1207959552 | bytes 4952064 | tf_op jit(solution)/shard_map/cross_terms/pallas_call | solution.py:27
  14.7 1.5 %collective-permute-start.9 = (s16[1088,128]{1,0:T(8,128)(2,1)S(1)}, s16[1088,128]{1,0:T(8,128)(2,1)S(1)}, u32[]{:S(2)}, u32[]{:S(2)}) collective-permute-start(s16[1088,128]{1,0:T(8,128)(2,1)S(1)} %get-tuple-element.23), channel_id=1, source_target_pairs={{0,2},{1,3},{2,0},{3,1},{4,6},{5,7},{6,4},{7,5},{8,10},{9,11},{10,... | collective-permute-start | bytes 835592 | tf_op jit(solution)/shard_map/ppermute | solution.py:339
  16.2 2.9 %collective-permute-start.5 = (s16[304,128]{1,0:T(8,128)(2,1)S(1)}, s16[304,128]{1,0:T(8,128)(2,1)S(1)}, u32[]{:S(2)}, u32[]{:S(2)}) collective-permute-start(s16[304,128]{1,0:T(8,128)(2,1)S(1)} %get-tuple-element.18), channel_id=1, source_target_pairs={{0,12},{4,8},{8,4},{12,0},{1,13},{5,9},{9,5},{13,1},{2,14},{6,10},... | collective-permute-start | bytes 233480 | tf_op jit(solution)/shard_map/ppermute | solution.py:342
  19.2 0.0 collective-permute-start.6
  19.2 1.5 %collective-permute-start.7 = (s16[304,128]{1,0:T(8,128)(2,1)S(1)}, s16[304,128]{1,0:T(8,128)(2,1)S(1)}, u32[]{:S(2)}, u32[]{:S(2)}) collective-permute-start(s16[304,128]{1,0:T(8,128)(2,1)S(1)} %get-tuple-element.20), channel_id=1, source_target_pairs={{0,4},{4,0},{8,12},{12,8},{1,5},{5,1},{9,13},{13,9},{2,6},{6,2},{1... | collective-permute-start | bytes 233480 | tf_op jit(solution)/shard_map/ppermute | solution.py:342
  20.6 1.9 %codeword_sums.1.refs_1_ = f32[256,256]{1,0:T(8,128)S(1)} custom-call(s32[48,2048]{1,0:T(8,128)S(1)} %get-tuple-element.15.refs_2_.refs_0_, bf16[384,2048]{1,0:T(8,128)(2,1)S(1)} %get-tuple-element.22.refs_1_, f32[96,384]{1,0:T(8,128)S(1)} %get-tuple-element.17.own.refs_2_), custom_call_target="tpu_custom_call" | custom-call | flops 2415919104 | bytes 2375680 | tf_op jit(solution)/shard_map/codeword_sums/pallas_call | solution.py:27
  22.6 0.3 add_half.1
  22.9 1.7 %collective-permute-start.10 = (s16[272,128]{1,0:T(8,128)(2,1)S(1)}, s16[272,128]{1,0:T(8,128)(2,1)S(1)}, u32[]{:S(2)}, u32[]{:S(2)}) collective-permute-start(s16[272,128]{1,0:T(8,128)(2,1)S(1)} %get-tuple-element.25), channel_id=1, source_target_pairs={{0,8},{4,12},{8,0},{12,4},{1,9},{5,13},{9,1},{13,5},{2,10},{6,14},... | collective-permute-start | bytes 208904 | tf_op jit(solution)/shard_map/ppermute | solution.py:342
  24.6 1.4 %collective-permute-start.11 = (s16[272,128]{1,0:T(8,128)(2,1)S(1)}, s16[272,128]{1,0:T(8,128)(2,1)S(1)}, u32[]{:S(2)}, u32[]{:S(2)}) collective-permute-start(s16[272,128]{1,0:T(8,128)(2,1)S(1)} %get-tuple-element.26), channel_id=1, source_target_pairs={{0,12},{4,8},{8,4},{12,0},{1,13},{5,9},{9,5},{13,1},{2,14},{6,10},... | collective-permute-start | bytes 208904 | tf_op jit(solution)/shard_map/ppermute | solution.py:342
  25.9 0.5 %collective-permute-start.12 = (s16[272,128]{1,0:T(8,128)(2,1)S(1)}, s16[272,128]{1,0:T(8,128)(2,1)S(1)}, u32[]{:S(2)}, u32[]{:S(2)}) collective-permute-start(s16[272,128]{1,0:T(8,128)(2,1)S(1)} %get-tuple-element.27), channel_id=1, source_target_pairs={{0,4},{4,0},{8,12},{12,8},{1,5},{5,1},{9,13},{13,9},{2,6},{6,2},{1... | collective-permute-start | bytes 208904 | tf_op jit(solution)/shard_map/ppermute | solution.py:342
  26.4 0.2 collective-permute-done.6.rest_1_
  26.6 0.0 collective-permute-done.7.rest_2_
  26.6 0.1 add_early.1.refs_0_
  26.7 1.1 %collective-permute-start.8 = (s16[304,128]{1,0:T(8,128)(2,1)S(1)}, s16[304,128]{1,0:T(8,128)(2,1)S(1)}, u32[]{:S(2)}, u32[]{:S(2)}) collective-permute-start(s16[304,128]{1,0:T(8,128)(2,1)S(1)} %add_early.1.refs_0_), channel_id=1, source_target_pairs={{0,2},{1,3},{2,0},{3,1},{4,6},{5,7},{6,4},{7,5},{8,10},{9,11},{10,... | collective-permute-start | bytes 233480 | tf_op jit(solution)/shard_map/ppermute | solution.py:339
  27.8 1.8 %collective-permute-done.10.refs_1_ = s16[272,128]{1,0:T(8,128)(2,1)S(1)} collective-permute-done((s16[272,128]{1,0:T(8,128)(2,1)S(1)}, s16[272,128]{1,0:T(8,128)(2,1)S(1)}, u32[]{:S(2)}, u32[]{:S(2)}) %collective-permute-start.10) | collective-permute-done | bytes 69664 | tf_op jit(solution)/shard_map/ppermute | solution.py:342
  29.6 1.2 %collective-permute-done.11.refs_2_ = s16[272,128]{1,0:T(8,128)(2,1)S(1)} collective-permute-done((s16[272,128]{1,0:T(8,128)(2,1)S(1)}, s16[272,128]{1,0:T(8,128)(2,1)S(1)}, u32[]{:S(2)}, u32[]{:S(2)}) %collective-permute-start.11) | collective-permute-done | bytes 69664 | tf_op jit(solution)/shard_map/ppermute | solution.py:342
  30.8 0.3 collective-permute-done.12.refs_3_
  31.1 0.1 add_late.1.refs_2_
  31.2 1.4 %collective-permute-start.13 = (s16[272,128]{1,0:T(8,128)(2,1)S(1)}, s16[272,128]{1,0:T(8,128)(2,1)S(1)}, u32[]{:S(2)}, u32[]{:S(2)}) collective-permute-start(s16[272,128]{1,0:T(8,128)(2,1)S(1)} %add_late.1.refs_2_), channel_id=1, source_target_pairs={{0,2},{1,3},{2,0},{3,1},{4,6},{5,7},{6,4},{7,5},{8,10},{9,11},{10,... | collective-permute-start | bytes 208904 | tf_op jit(solution)/shard_map/ppermute | solution.py:339
  32.7 0.5 %collective-permute-start.15 = (s16[304,128]{1,0:T(8,128)(2,1)S(1)}, s16[304,128]{1,0:T(8,128)(2,1)S(1)}, u32[]{:S(2)}, u32[]{:S(2)}) collective-permute-start(s16[304,128]{1,0:T(8,128)(2,1)S(1)} %collective-permute-done.8.refs_1_), channel_id=1, source_target_pairs={{0,1},{1,0},{2,3},{3,2},{4,5},{5,4},{6,7},{7,6},{8,9},{9,8},{10,11... | collective-permute-start | bytes 233480 | tf_op jit(solution)/shard_map/ppermute | solution.py:339
  33.2 0.0 collective-permute-start.16
  33.2 2.4 %collective-permute-done.13.refs_3_ = s16[272,128]{1,0:T(8,128)(2,1)S(1)} collective-permute-done((s16[272,128]{1,0:T(8,128)(2,1)S(1)}, s16[272,128]{1,0:T(8,128)(2,1)S(1)}, u32[]{:S(2)}, u32[]{:S(2)}) %collective-permute-start.13) | collective-permute-done | bytes 69664 | tf_op jit(solution)/shard_map/ppermute | solution.py:339
  35.6 1.2 %collective-permute-done.17.refs_7_ = s16[272,128]{1,0:T(8,128)(2,1)S(1)} collective-permute-done((s16[272,128]{1,0:T(8,128)(2,1)S(1)}, s16[272,128]{1,0:T(8,128)(2,1)S(1)}, u32[]{:S(2)}, u32[]{:S(2)}) %collective-permute-start.17) | collective-permute-done | bytes 69664 | tf_op jit(solution)/shard_map/ppermute | solution.py:339
  36.9 1.1 %finish.1 = (f32[64,768]{1,0:T(8,128)}, f32[192,768]{1,0:T(8,128)}) custom-call(s16[304,128]{1,0:T(8,128)(2,1)S(1)} %add_early.1.refs_0_, s16[304,128]{1,0:T(8,128)(2,1)S(1)} %collective-permute-done.8.refs_1_, s16[272,128]{1,0:T(8,128)(2,1)S(1)} %add_late.1.refs_2_, s16[272,128]{1,0:T(8,128)(2,1)S(1)} %collective-permute-done.13.refs_3_, ...), custom_call_target="tpu_custom_call" | custom-call | bytes 1474560 | tf_op jit(solution)/shard_map/finish/pallas_call | solution.py:27
  (21 shorter events, 0.1 us)
Async XLA Ops:
  0.6 0.9 %copy-start = (bf16[64,768]{1,0:T(8,128)(2,1)S(1)}, bf16[64,768]{1,0:T(8,128)(2,1)}, u32[]{:S(2)}) copy-start(bf16[64,768]{1,0:T(8,128)(2,1)} %refs_8_.1) | copy-start | bytes 294916
  0.6 6.7 %collective-permute-start.1 = (s32[96,1024]{1,0:T(8,128)}, s32[96,1024]{1,0:T(8,128)S(1)}, u32[]{:S(2)}, u32[]{:S(2)}) collective-permute-start(s32[96,1024]{1,0:T(8,128)} %bitcast.1), channel_id=1, source_target_pairs={{0,1},{1,0},{2,3},{3,2},{4,5},{5,4},{6,7},{7,6},{8,9},{9,8},{10,11... | collective-permute-start | bytes 1179656 | tf_op jit(solution)/shard_map/ppermute | solution.py:339
  1.2 6.1 %collective-permute-start = (bf16[1024,768]{1,0:T(8,128)(2,1)}, bf16[1024,768]{1,0:T(8,128)(2,1)S(1)}, u32[]{:S(2)}, u32[]{:S(2)}) collective-permute-start(bf16[1024,768]{1,0:T(8,128)(2,1)} %refs_0_.3), channel_id=1, source_target_pairs={{0,1},{1,0},{2,3},{3,2},{4,5},{5,4},{6,7},{7,6},{8,9},{9,8},{10,11... | collective-permute-start | bytes 4718600 | tf_op jit(solution)/shard_map/ppermute | solution.py:339
  1.5 5.8 %copy-start.1 = (bf16[1024,768]{1,0:T(8,128)(2,1)S(1)}, bf16[1024,768]{1,0:T(8,128)(2,1)}, u32[]{:S(2)}) copy-start(bf16[1024,768]{1,0:T(8,128)(2,1)} %refs_0_.3) | copy-start | bytes 4718596
  1.5 5.8 %copy-start.2 = (bf16[768,768]{1,0:T(8,128)(2,1)S(1)}, bf16[768,768]{1,0:T(8,128)(2,1)}, u32[]{:S(2)}) copy-start(bf16[768,768]{1,0:T(8,128)(2,1)} %refs_4_.1) | copy-start | bytes 3538948
  1.5 5.8 %copy-start.3 = (s32[1024,96]{0,1:T(8,128)S(1)}, s32[1024,96]{0,1:T(8,128)}, u32[]{:S(2)}) copy-start(s32[1024,96]{0,1:T(8,128)} %param.5) | copy-start | bytes 1179652
  1.5 9.2 %collective-permute-start.4 = (bf16[64,384]{1,0:T(8,128)(2,1)S(1)}, bf16[64,384]{1,0:T(8,128)(2,1)S(1)}, u32[]{:S(2)}, u32[]{:S(2)}) collective-permute-start(bf16[64,384]{1,0:T(8,128)(2,1)S(1)} %take_half.1.refs_4_), channel_id=1, source_target_pairs={{0,12},{4,8},{8,4},{12,0},{1,13},{5,9},{9,5},{13,1},{2,14},{6,10},... | collective-permute-start | bytes 147464 | tf_op jit(solution)/shard_map/ppermute | solution.py:342
  6.7 5.0 %collective-permute-start.3 = (bf16[64,384]{1,0:T(8,128)(2,1)S(1)}, bf16[64,384]{1,0:T(8,128)(2,1)S(1)}, u32[]{:S(2)}, u32[]{:S(2)}) collective-permute-start(bf16[64,384]{1,0:T(8,128)(2,1)S(1)} %take_half.1.refs_4_), channel_id=1, source_target_pairs={{0,8},{4,12},{8,0},{12,4},{1,9},{5,13},{9,1},{13,5},{2,10},{6,14},... | collective-permute-start | bytes 147464 | tf_op jit(solution)/shard_map/ppermute | solution.py:342
  6.7 5.0 %collective-permute-start.2 = (bf16[64,384]{1,0:T(8,128)(2,1)S(1)}, bf16[64,384]{1,0:T(8,128)(2,1)S(1)}, u32[]{:S(2)}, u32[]{:S(2)}) collective-permute-start(bf16[64,384]{1,0:T(8,128)(2,1)S(1)} %take_half.1.refs_4_), channel_id=1, source_target_pairs={{0,4},{4,0},{8,12},{12,8},{1,5},{5,1},{9,13},{13,9},{2,6},{6,2},{1... | collective-permute-start | bytes 147464 | tf_op jit(solution)/shard_map/ppermute | solution.py:342
  14.7 7.9 %collective-permute-start.9 = (s16[1088,128]{1,0:T(8,128)(2,1)S(1)}, s16[1088,128]{1,0:T(8,128)(2,1)S(1)}, u32[]{:S(2)}, u32[]{:S(2)}) collective-permute-start(s16[1088,128]{1,0:T(8,128)(2,1)S(1)} %get-tuple-element.23), channel_id=1, source_target_pairs={{0,2},{1,3},{2,0},{3,1},{4,6},{5,7},{6,4},{7,5},{8,10},{9,11},{10,... | collective-permute-start | bytes 835592 | tf_op jit(solution)/shard_map/ppermute | solution.py:339
  16.2 9.7 %collective-permute-start.5 = (s16[304,128]{1,0:T(8,128)(2,1)S(1)}, s16[304,128]{1,0:T(8,128)(2,1)S(1)}, u32[]{:S(2)}, u32[]{:S(2)}) collective-permute-start(s16[304,128]{1,0:T(8,128)(2,1)S(1)} %get-tuple-element.18), channel_id=1, source_target_pairs={{0,12},{4,8},{8,4},{12,0},{1,13},{5,9},{9,5},{13,1},{2,14},{6,10},... | collective-permute-start | bytes 233480 | tf_op jit(solution)/shard_map/ppermute | solution.py:342
  19.2 7.4 %collective-permute-start.6 = (s16[304,128]{1,0:T(8,128)(2,1)S(1)}, s16[304,128]{1,0:T(8,128)(2,1)S(1)}, u32[]{:S(2)}, u32[]{:S(2)}) collective-permute-start(s16[304,128]{1,0:T(8,128)(2,1)S(1)} %get-tuple-element.19), channel_id=1, source_target_pairs={{0,8},{4,12},{8,0},{12,4},{1,9},{5,13},{9,1},{13,5},{2,10},{6,14},... | collective-permute-start | bytes 233480 | tf_op jit(solution)/shard_map/ppermute | solution.py:342
  19.2 7.4 %collective-permute-start.7 = (s16[304,128]{1,0:T(8,128)(2,1)S(1)}, s16[304,128]{1,0:T(8,128)(2,1)S(1)}, u32[]{:S(2)}, u32[]{:S(2)}) collective-permute-start(s16[304,128]{1,0:T(8,128)(2,1)S(1)} %get-tuple-element.20), channel_id=1, source_target_pairs={{0,4},{4,0},{8,12},{12,8},{1,5},{5,1},{9,13},{13,9},{2,6},{6,2},{1... | collective-permute-start | bytes 233480 | tf_op jit(solution)/shard_map/ppermute | solution.py:342
  22.9 6.8 %collective-permute-start.10 = (s16[272,128]{1,0:T(8,128)(2,1)S(1)}, s16[272,128]{1,0:T(8,128)(2,1)S(1)}, u32[]{:S(2)}, u32[]{:S(2)}) collective-permute-start(s16[272,128]{1,0:T(8,128)(2,1)S(1)} %get-tuple-element.25), channel_id=1, source_target_pairs={{0,8},{4,12},{8,0},{12,4},{1,9},{5,13},{9,1},{13,5},{2,10},{6,14},... | collective-permute-start | bytes 208904 | tf_op jit(solution)/shard_map/ppermute | solution.py:342
  24.6 6.3 %collective-permute-start.11 = (s16[272,128]{1,0:T(8,128)(2,1)S(1)}, s16[272,128]{1,0:T(8,128)(2,1)S(1)}, u32[]{:S(2)}, u32[]{:S(2)}) collective-permute-start(s16[272,128]{1,0:T(8,128)(2,1)S(1)} %get-tuple-element.26), channel_id=1, source_target_pairs={{0,12},{4,8},{8,4},{12,0},{1,13},{5,9},{9,5},{13,1},{2,14},{6,10},... | collective-permute-start | bytes 208904 | tf_op jit(solution)/shard_map/ppermute | solution.py:342
  25.9 5.2 %collective-permute-start.12 = (s16[272,128]{1,0:T(8,128)(2,1)S(1)}, s16[272,128]{1,0:T(8,128)(2,1)S(1)}, u32[]{:S(2)}, u32[]{:S(2)}) collective-permute-start(s16[272,128]{1,0:T(8,128)(2,1)S(1)} %get-tuple-element.27), channel_id=1, source_target_pairs={{0,4},{4,0},{8,12},{12,8},{1,5},{5,1},{9,13},{13,9},{2,6},{6,2},{1... | collective-permute-start | bytes 208904 | tf_op jit(solution)/shard_map/ppermute | solution.py:342
  26.7 6.0 %collective-permute-start.8 = (s16[304,128]{1,0:T(8,128)(2,1)S(1)}, s16[304,128]{1,0:T(8,128)(2,1)S(1)}, u32[]{:S(2)}, u32[]{:S(2)}) collective-permute-start(s16[304,128]{1,0:T(8,128)(2,1)S(1)} %add_early.1.refs_0_), channel_id=1, source_target_pairs={{0,2},{1,3},{2,0},{3,1},{4,6},{5,7},{6,4},{7,5},{8,10},{9,11},{10,... | collective-permute-start | bytes 233480 | tf_op jit(solution)/shard_map/ppermute | solution.py:339
  31.2 4.4 %collective-permute-start.13 = (s16[272,128]{1,0:T(8,128)(2,1)S(1)}, s16[272,128]{1,0:T(8,128)(2,1)S(1)}, u32[]{:S(2)}, u32[]{:S(2)}) collective-permute-start(s16[272,128]{1,0:T(8,128)(2,1)S(1)} %add_late.1.refs_2_), channel_id=1, source_target_pairs={{0,2},{1,3},{2,0},{3,1},{4,6},{5,7},{6,4},{7,5},{8,10},{9,11},{10,... | collective-permute-start | bytes 208904 | tf_op jit(solution)/shard_map/ppermute | solution.py:339
  32.7 3.0 %collective-permute-start.14 = (s16[304,128]{1,0:T(8,128)(2,1)S(1)}, s16[304,128]{1,0:T(8,128)(2,1)S(1)}, u32[]{:S(2)}, u32[]{:S(2)}) collective-permute-start(s16[304,128]{1,0:T(8,128)(2,1)S(1)} %add_early.1.refs_0_), channel_id=1, source_target_pairs={{0,1},{1,0},{2,3},{3,2},{4,5},{5,4},{6,7},{7,6},{8,9},{9,8},{10,11... | collective-permute-start | bytes 233480 | tf_op jit(solution)/shard_map/ppermute | solution.py:339
  32.7 3.0 %collective-permute-start.15 = (s16[304,128]{1,0:T(8,128)(2,1)S(1)}, s16[304,128]{1,0:T(8,128)(2,1)S(1)}, u32[]{:S(2)}, u32[]{:S(2)}) collective-permute-start(s16[304,128]{1,0:T(8,128)(2,1)S(1)} %collective-permute-done.8.refs_1_), channel_id=1, source_target_pairs={{0,1},{1,0},{2,3},{3,2},{4,5},{5,4},{6,7},{7,6},{8,9},{9,8},{10,11... | collective-permute-start | bytes 233480 | tf_op jit(solution)/shard_map/ppermute | solution.py:339
  33.2 2.5 %collective-permute-start.16 = (s16[272,128]{1,0:T(8,128)(2,1)S(1)}, s16[272,128]{1,0:T(8,128)(2,1)S(1)}, u32[]{:S(2)}, u32[]{:S(2)}) collective-permute-start(s16[272,128]{1,0:T(8,128)(2,1)S(1)} %add_late.1.refs_2_), channel_id=1, source_target_pairs={{0,1},{1,0},{2,3},{3,2},{4,5},{5,4},{6,7},{7,6},{8,9},{9,8},{10,11... | collective-permute-start | bytes 208904 | tf_op jit(solution)/shard_map/ppermute | solution.py:339
  35.6 1.3 %collective-permute-start.17 = (s16[272,128]{1,0:T(8,128)(2,1)S(1)}, s16[272,128]{1,0:T(8,128)(2,1)S(1)}, u32[]{:S(2)}, u32[]{:S(2)}) collective-permute-start(s16[272,128]{1,0:T(8,128)(2,1)S(1)} %collective-permute-done.13.refs_3_), channel_id=1, source_target_pairs={{0,1},{1,0},{2,3},{3,2},{4,5},{5,4},{6,7},{7,6},{8,9},{9,8},{10,11... | collective-permute-start | bytes 208904 | tf_op jit(solution)/shard_map/ppermute | solution.py:339

commit v8 on v7

--- a/solution.py
+++ b/solution.py
@@ -105,7 +105,7 @@
     out[...] = codebook[:, cols]
 
 
-def begin_kernel(shape, e0, e1, c0, c1, rot, out, codes, rt, lhs, rhs, total):
+def begin_kernel(shape, c0, c1, e0, e1, rot, out, codes, rt, lhs, rhs, total):
     rows, half, n_words, n_out = shape
     subs = codes.shape[0]
     core, cols = my_half(half)
@@ -376,7 +376,7 @@
             jax.ShapeDtypeStruct((n_sub // 2, 2 * rows), i32),
             jax.ShapeDtypeStruct((half, 2 * rows), bf16),
         ],
-        (embeddings, e1, c0, c1, rotation),
+        (c0, c1, embeddings, e1, rotation),
         buffers,
         "begin",
         flops=8 * rows * half * width,

time: 38.1 us -> 38.1 us (level)
  transfers between devices with their start and end apart: 18 -> 18, of which waited for: 7 -> 7; matrix products, arithmetic and copies ran while one was open for 0% -> 0% of each run, Pallas kernels for 15% -> 16%
where the time goes in v8:
time: 38.1 us; the launch traced here: 38 us
  starting transfers between devices  19 us (50%)
  Pallas kernels  10.1 us (27%)
  waiting for transfers between devices  7.93 us (21%)
  between operations  0.74 us (2%)
    ppermute x9, starting transfers between devices, exchange(): lax.ppermute(blocks[hops.index(k)], 'dp', [(i, i ^ k) for i in range(n)])  13.7 us
    pallas_call x9, Pallas kernels, call(): pl.pallas_call(kernel, out_shape=outs, in_specs=[pl.BlockSpec(memory_spac...  10.1 us
    ppermute x9, starting transfers between devices, swap(): return lax.ppermute(x, 'replica', [(i, i ^ bit) for i in range(replicas)])  5.25 us
    ppermute x9, waiting for transfers between devices, exchange(): lax.ppermute(blocks[hops.index(k)], 'dp', [(i, i ^ k) for i in range(n)])  4.25 us
    ppermute x9, waiting for transfers between devices, swap(): return lax.ppermute(x, 'replica', [(i, i ^ bit) for i in range(replicas)])  3.68 us
  transfers between devices with their start and end apart: 18, of which 7 were waited for; matrix products, arithmetic and copies ran while one was open for 0% of the time, Pallas kernels for 16%

profile of v8, /device:TPU:0, one launch (start us, length us, event | category | flops | bytes accessed | tf_op | source)
XLA Modules:
  0.0 38.0 jit_solution(416912028057920004)
XLA Ops:
  0.6 0.5 %collective-permute-start.1 = (s32[96,1024]{1,0:T(8,128)}, s32[96,1024]{1,0:T(8,128)S(1)}, u32[]{:S(2)}, u32[]{:S(2)}) collective-permute-start(s32[96,1024]{1,0:T(8,128)} %bitcast.1), channel_id=1, source_target_pairs={{0,1},{1,0},{2,3},{3,2},{4,5},{5,4},{6,7},{7,6},{8,9},{9,8},{10,11... | collective-permute-start | bytes 1179656 | tf_op jit(solution)/shard_map/ppermute | solution.py:339
  1.2 0.1 collective-permute-start
  1.2 0.3 copy-done
  1.5 5.1 %collective-permute-start.4 = (bf16[64,384]{1,0:T(8,128)(2,1)S(1)}, bf16[64,384]{1,0:T(8,128)(2,1)S(1)}, u32[]{:S(2)}, u32[]{:S(2)}) collective-permute-start(bf16[64,384]{1,0:T(8,128)(2,1)S(1)} %take_half.1.refs_4_), channel_id=1, source_target_pairs={{0,12},{4,8},{8,4},{12,0},{1,13},{5,9},{9,5},{13,1},{2,14},{6,10},... | collective-permute-start | bytes 147464 | tf_op jit(solution)/shard_map/ppermute | solution.py:342
  6.7 0.6 %collective-permute-start.2 = (bf16[64,384]{1,0:T(8,128)(2,1)S(1)}, bf16[64,384]{1,0:T(8,128)(2,1)S(1)}, u32[]{:S(2)}, u32[]{:S(2)}) collective-permute-start(bf16[64,384]{1,0:T(8,128)(2,1)S(1)} %take_half.1.refs_4_), channel_id=1, source_target_pairs={{0,4},{4,0},{8,12},{12,8},{1,5},{5,1},{9,13},{13,9},{2,6},{6,2},{1... | collective-permute-start | bytes 147464 | tf_op jit(solution)/shard_map/ppermute | solution.py:342
  7.3 0.0 collective-permute-done.refs_3_.refs_1_
  7.3 3.4 %begin.1 = (f32[256,256]{1,0:T(8,128)S(1)}, s32[48,2048]{1,0:T(8,128)S(1)}, bf16[384,2048]{1,0:T(8,128)(2,1)S(1)}) custom-call(s32[96,1024]{1,0:T(8,128)S(1)} %bitcast.2, s32[96,1024]{1,0:T(8,128)S(1)} %collective-permute-done.1.refs_1_, bf16[1024,768]{1,0:T(8,128)(2,1)S(1)} %copy-done.1, bf16[1024,768]{1,0:T(8,128)(2,1)S(1)} %collective-permute-done.refs_3_.refs_1_, ...), custom_call_target="tpu_custom_call" | custom-call | flops 2415919104 | bytes 7340032 | tf_op jit(solution)/shard_map/begin/pallas_call | solution.py:27
  10.8 0.0 collective-permute-done.4.refs_7_
  10.8 0.8 %collective-permute-done.3.refs_6_ = bf16[64,384]{1,0:T(8,128)(2,1)S(1)} collective-permute-done((bf16[64,384]{1,0:T(8,128)(2,1)S(1)}, bf16[64,384]{1,0:T(8,128)(2,1)S(1)}, u32[]{:S(2)}, u32[]{:S(2)}) %collective-permute-start.3) | collective-permute-done | bytes 49184 | tf_op jit(solution)/shard_map/ppermute | solution.py:342
  11.6 0.0 collective-permute-done.2.refs_5_
  11.6 3.0 %cross_terms.1 = (f32[96,384]{1,0:T(8,128)S(1)}, f32[192,384]{1,0:T(8,128)S(1)}, s16[1088,128]{1,0:T(8,128)(2,1)S(1)}, s16[304,128]{1,0:T(8,128)(2,1)S(1)}, s16[...) custom-call(bf16[1024,768]{1,0:T(8,128)(2,1)S(1)} %copy-done.1, ...), custom_call_target="tpu_custom_call" | custom-call | flops 1207959552 | bytes 4952064 | tf_op jit(solution)/shard_map/cross_terms/pallas_call | solution.py:27
  14.7 1.5 %collective-permute-start.9 = (s16[1088,128]{1,0:T(8,128)(2,1)S(1)}, s16[1088,128]{1,0:T(8,128)(2,1)S(1)}, u32[]{:S(2)}, u32[]{:S(2)}) collective-permute-start(s16[1088,128]{1,0:T(8,128)(2,1)S(1)} %get-tuple-element.23), channel_id=1, source_target_pairs={{0,2},{1,3},{2,0},{3,1},{4,6},{5,7},{6,4},{7,5},{8,10},{9,11},{10,... | collective-permute-start | bytes 835592 | tf_op jit(solution)/shard_map/ppermute | solution.py:339
  16.2 2.9 %collective-permute-start.5 = (s16[304,128]{1,0:T(8,128)(2,1)S(1)}, s16[304,128]{1,0:T(8,128)(2,1)S(1)}, u32[]{:S(2)}, u32[]{:S(2)}) collective-permute-start(s16[304,128]{1,0:T(8,128)(2,1)S(1)} %get-tuple-element.18), channel_id=1, source_target_pairs={{0,12},{4,8},{8,4},{12,0},{1,13},{5,9},{9,5},{13,1},{2,14},{6,10},... | collective-permute-start | bytes 233480 | tf_op jit(solution)/shard_map/ppermute | solution.py:342
  19.2 1.4 %collective-permute-start.7 = (s16[304,128]{1,0:T(8,128)(2,1)S(1)}, s16[304,128]{1,0:T(8,128)(2,1)S(1)}, u32[]{:S(2)}, u32[]{:S(2)}) collective-permute-start(s16[304,128]{1,0:T(8,128)(2,1)S(1)} %get-tuple-element.20), channel_id=1, source_target_pairs={{0,4},{4,0},{8,12},{12,8},{1,5},{5,1},{9,13},{13,9},{2,6},{6,2},{1... | collective-permute-start | bytes 233480 | tf_op jit(solution)/shard_map/ppermute | solution.py:342
  20.6 1.9 %codeword_sums.1.refs_1_ = f32[256,256]{1,0:T(8,128)S(1)} custom-call(s32[48,2048]{1,0:T(8,128)S(1)} %get-tuple-element.15.refs_2_.refs_0_, bf16[384,2048]{1,0:T(8,128)(2,1)S(1)} %get-tuple-element.22.refs_1_, f32[96,384]{1,0:T(8,128)S(1)} %get-tuple-element.17.own.refs_2_), custom_call_target="tpu_custom_call" | custom-call | flops 2415919104 | bytes 2375680 | tf_op jit(solution)/shard_map/codeword_sums/pallas_call | solution.py:27
  22.6 0.3 add_half.1
  22.9 1.7 %collective-permute-start.10 = (s16[272,128]{1,0:T(8,128)(2,1)S(1)}, s16[272,128]{1,0:T(8,128)(2,1)S(1)}, u32[]{:S(2)}, u32[]{:S(2)}) collective-permute-start(s16[272,128]{1,0:T(8,128)(2,1)S(1)} %get-tuple-element.25), channel_id=1, source_target_pairs={{0,8},{4,12},{8,0},{12,4},{1,9},{5,13},{9,1},{13,5},{2,10},{6,14},... | collective-permute-start | bytes 208904 | tf_op jit(solution)/shard_map/ppermute | solution.py:342
  24.6 1.4 %collective-permute-start.11 = (s16[272,128]{1,0:T(8,128)(2,1)S(1)}, s16[272,128]{1,0:T(8,128)(2,1)S(1)}, u32[]{:S(2)}, u32[]{:S(2)}) collective-permute-start(s16[272,128]{1,0:T(8,128)(2,1)S(1)} %get-tuple-element.26), channel_id=1, source_target_pairs={{0,12},{4,8},{8,4},{12,0},{1,13},{5,9},{9,5},{13,1},{2,14},{6,10},... | collective-permute-start | bytes 208904 | tf_op jit(solution)/shard_map/ppermute | solution.py:342
  26.0 0.5 %collective-permute-start.12 = (s16[272,128]{1,0:T(8,128)(2,1)S(1)}, s16[272,128]{1,0:T(8,128)(2,1)S(1)}, u32[]{:S(2)}, u32[]{:S(2)}) collective-permute-start(s16[272,128]{1,0:T(8,128)(2,1)S(1)} %get-tuple-element.27), channel_id=1, source_target_pairs={{0,4},{4,0},{8,12},{12,8},{1,5},{5,1},{9,13},{13,9},{2,6},{6,2},{1... | collective-permute-start | bytes 208904 | tf_op jit(solution)/shard_map/ppermute | solution.py:342
  26.4 0.1 collective-permute-done.6.rest_1_
  26.6 0.1 add_early.1.refs_0_
  26.7 1.2 %collective-permute-start.8 = (s16[304,128]{1,0:T(8,128)(2,1)S(1)}, s16[304,128]{1,0:T(8,128)(2,1)S(1)}, u32[]{:S(2)}, u32[]{:S(2)}) collective-permute-start(s16[304,128]{1,0:T(8,128)(2,1)S(1)} %add_early.1.refs_0_), channel_id=1, source_target_pairs={{0,2},{1,3},{2,0},{3,1},{4,6},{5,7},{6,4},{7,5},{8,10},{9,11},{10,... | collective-permute-start | bytes 233480 | tf_op jit(solution)/shard_map/ppermute | solution.py:339
  27.8 1.8 %collective-permute-done.10.refs_1_ = s16[272,128]{1,0:T(8,128)(2,1)S(1)} collective-permute-done((s16[272,128]{1,0:T(8,128)(2,1)S(1)}, s16[272,128]{1,0:T(8,128)(2,1)S(1)}, u32[]{:S(2)}, u32[]{:S(2)}) %collective-permute-start.10) | collective-permute-done | bytes 69664 | tf_op jit(solution)/shard_map/ppermute | solution.py:342
  29.6 1.2 %collective-permute-done.11.refs_2_ = s16[272,128]{1,0:T(8,128)(2,1)S(1)} collective-permute-done((s16[272,128]{1,0:T(8,128)(2,1)S(1)}, s16[272,128]{1,0:T(8,128)(2,1)S(1)}, u32[]{:S(2)}, u32[]{:S(2)}) %collective-permute-start.11) | collective-permute-done | bytes 69664 | tf_op jit(solution)/shard_map/ppermute | solution.py:342
  30.8 0.3 collective-permute-done.12.refs_3_
  31.1 0.1 add_late.1.refs_2_
  31.2 1.4 %collective-permute-start.13 = (s16[272,128]{1,0:T(8,128)(2,1)S(1)}, s16[272,128]{1,0:T(8,128)(2,1)S(1)}, u32[]{:S(2)}, u32[]{:S(2)}) collective-permute-start(s16[272,128]{1,0:T(8,128)(2,1)S(1)} %add_late.1.refs_2_), channel_id=1, source_target_pairs={{0,2},{1,3},{2,0},{3,1},{4,6},{5,7},{6,4},{7,5},{8,10},{9,11},{10,... | collective-permute-start | bytes 208904 | tf_op jit(solution)/shard_map/ppermute | solution.py:339
  32.7 0.5 %collective-permute-start.15 = (s16[304,128]{1,0:T(8,128)(2,1)S(1)}, s16[304,128]{1,0:T(8,128)(2,1)S(1)}, u32[]{:S(2)}, u32[]{:S(2)}) collective-permute-start(s16[304,128]{1,0:T(8,128)(2,1)S(1)} %collective-permute-done.8.refs_1_), channel_id=1, source_target_pairs={{0,1},{1,0},{2,3},{3,2},{4,5},{5,4},{6,7},{7,6},{8,9},{9,8},{10,11... | collective-permute-start | bytes 233480 | tf_op jit(solution)/shard_map/ppermute | solution.py:339
  33.2 0.0 collective-permute-start.16
  33.2 2.4 %collective-permute-done.13.refs_3_ = s16[272,128]{1,0:T(8,128)(2,1)S(1)} collective-permute-done((s16[272,128]{1,0:T(8,128)(2,1)S(1)}, s16[272,128]{1,0:T(8,128)(2,1)S(1)}, u32[]{:S(2)}, u32[]{:S(2)}) %collective-permute-start.13) | collective-permute-done | bytes 69664 | tf_op jit(solution)/shard_map/ppermute | solution.py:339
  35.6 1.2 %collective-permute-done.17.refs_7_ = s16[272,128]{1,0:T(8,128)(2,1)S(1)} collective-permute-done((s16[272,128]{1,0:T(8,128)(2,1)S(1)}, s16[272,128]{1,0:T(8,128)(2,1)S(1)}, u32[]{:S(2)}, u32[]{:S(2)}) %collective-permute-start.17) | collective-permute-done | bytes 69664 | tf_op jit(solution)/shard_map/ppermute | solution.py:339
  36.9 1.1 %finish.1 = (f32[64,768]{1,0:T(8,128)}, f32[192,768]{1,0:T(8,128)}) custom-call(s16[304,128]{1,0:T(8,128)(2,1)S(1)} %add_early.1.refs_0_, s16[304,128]{1,0:T(8,128)(2,1)S(1)} %collective-permute-done.8.refs_1_, s16[272,128]{1,0:T(8,128)(2,1)S(1)} %add_late.1.refs_2_, s16[272,128]{1,0:T(8,128)(2,1)S(1)} %collective-permute-done.13.refs_3_, ...), custom_call_target="tpu_custom_call" | custom-call | bytes 1474560 | tf_op jit(solution)/shard_map/finish/pallas_call | solution.py:27
  (21 shorter events, 0.1 us)
Async XLA Ops:
  0.6 0.9 %copy-start = (bf16[64,768]{1,0:T(8,128)(2,1)S(1)}, bf16[64,768]{1,0:T(8,128)(2,1)}, u32[]{:S(2)}) copy-start(bf16[64,768]{1,0:T(8,128)(2,1)} %refs_8_.1) | copy-start | bytes 294916
  0.6 6.7 %collective-permute-start.1 = (s32[96,1024]{1,0:T(8,128)}, s32[96,1024]{1,0:T(8,128)S(1)}, u32[]{:S(2)}, u32[]{:S(2)}) collective-permute-start(s32[96,1024]{1,0:T(8,128)} %bitcast.1), channel_id=1, source_target_pairs={{0,1},{1,0},{2,3},{3,2},{4,5},{5,4},{6,7},{7,6},{8,9},{9,8},{10,11... | collective-permute-start | bytes 1179656 | tf_op jit(solution)/shard_map/ppermute | solution.py:339
  1.2 6.1 %collective-permute-start = (bf16[1024,768]{1,0:T(8,128)(2,1)}, bf16[1024,768]{1,0:T(8,128)(2,1)S(1)}, u32[]{:S(2)}, u32[]{:S(2)}) collective-permute-start(bf16[1024,768]{1,0:T(8,128)(2,1)} %refs_0_.1), channel_id=1, source_target_pairs={{0,1},{1,0},{2,3},{3,2},{4,5},{5,4},{6,7},{7,6},{8,9},{9,8},{10,11... | collective-permute-start | bytes 4718600 | tf_op jit(solution)/shard_map/ppermute | solution.py:339
  1.5 5.8 %copy-start.1 = (bf16[1024,768]{1,0:T(8,128)(2,1)S(1)}, bf16[1024,768]{1,0:T(8,128)(2,1)}, u32[]{:S(2)}) copy-start(bf16[1024,768]{1,0:T(8,128)(2,1)} %refs_0_.1) | copy-start | bytes 4718596
  1.5 5.8 %copy-start.2 = (bf16[768,768]{1,0:T(8,128)(2,1)S(1)}, bf16[768,768]{1,0:T(8,128)(2,1)}, u32[]{:S(2)}) copy-start(bf16[768,768]{1,0:T(8,128)(2,1)} %refs_4_.1) | copy-start | bytes 3538948
  1.5 5.8 %copy-start.3 = (s32[1024,96]{0,1:T(8,128)S(1)}, s32[1024,96]{0,1:T(8,128)}, u32[]{:S(2)}) copy-start(s32[1024,96]{0,1:T(8,128)} %param.5) | copy-start | bytes 1179652
  1.5 9.2 %collective-permute-start.4 = (bf16[64,384]{1,0:T(8,128)(2,1)S(1)}, bf16[64,384]{1,0:T(8,128)(2,1)S(1)}, u32[]{:S(2)}, u32[]{:S(2)}) collective-permute-start(bf16[64,384]{1,0:T(8,128)(2,1)S(1)} %take_half.1.refs_4_), channel_id=1, source_target_pairs={{0,12},{4,8},{8,4},{12,0},{1,13},{5,9},{9,5},{13,1},{2,14},{6,10},... | collective-permute-start | bytes 147464 | tf_op jit(solution)/shard_map/ppermute | solution.py:342
  6.7 5.0 %collective-permute-start.3 = (bf16[64,384]{1,0:T(8,128)(2,1)S(1)}, bf16[64,384]{1,0:T(8,128)(2,1)S(1)}, u32[]{:S(2)}, u32[]{:S(2)}) collective-permute-start(bf16[64,384]{1,0:T(8,128)(2,1)S(1)} %take_half.1.refs_4_), channel_id=1, source_target_pairs={{0,8},{4,12},{8,0},{12,4},{1,9},{5,13},{9,1},{13,5},{2,10},{6,14},... | collective-permute-start | bytes 147464 | tf_op jit(solution)/shard_map/ppermute | solution.py:342
  6.7 5.0 %collective-permute-start.2 = (bf16[64,384]{1,0:T(8,128)(2,1)S(1)}, bf16[64,384]{1,0:T(8,128)(2,1)S(1)}, u32[]{:S(2)}, u32[]{:S(2)}) collective-permute-start(bf16[64,384]{1,0:T(8,128)(2,1)S(1)} %take_half.1.refs_4_), channel_id=1, source_target_pairs={{0,4},{4,0},{8,12},{12,8},{1,5},{5,1},{9,13},{13,9},{2,6},{6,2},{1... | collective-permute-start | bytes 147464 | tf_op jit(solution)/shard_map/ppermute | solution.py:342
  14.7 7.9 %collective-permute-start.9 = (s16[1088,128]{1,0:T(8,128)(2,1)S(1)}, s16[1088,128]{1,0:T(8,128)(2,1)S(1)}, u32[]{:S(2)}, u32[]{:S(2)}) collective-permute-start(s16[1088,128]{1,0:T(8,128)(2,1)S(1)} %get-tuple-element.23), channel_id=1, source_target_pairs={{0,2},{1,3},{2,0},{3,1},{4,6},{5,7},{6,4},{7,5},{8,10},{9,11},{10,... | collective-permute-start | bytes 835592 | tf_op jit(solution)/shard_map/ppermute | solution.py:339
  16.2 9.7 %collective-permute-start.5 = (s16[304,128]{1,0:T(8,128)(2,1)S(1)}, s16[304,128]{1,0:T(8,128)(2,1)S(1)}, u32[]{:S(2)}, u32[]{:S(2)}) collective-permute-start(s16[304,128]{1,0:T(8,128)(2,1)S(1)} %get-tuple-element.18), channel_id=1, source_target_pairs={{0,12},{4,8},{8,4},{12,0},{1,13},{5,9},{9,5},{13,1},{2,14},{6,10},... | collective-permute-start | bytes 233480 | tf_op jit(solution)/shard_map/ppermute | solution.py:342
  19.2 7.4 %collective-permute-start.6 = (s16[304,128]{1,0:T(8,128)(2,1)S(1)}, s16[304,128]{1,0:T(8,128)(2,1)S(1)}, u32[]{:S(2)}, u32[]{:S(2)}) collective-permute-start(s16[304,128]{1,0:T(8,128)(2,1)S(1)} %get-tuple-element.19), channel_id=1, source_target_pairs={{0,8},{4,12},{8,0},{12,4},{1,9},{5,13},{9,1},{13,5},{2,10},{6,14},... | collective-permute-start | bytes 233480 | tf_op jit(solution)/shard_map/ppermute | solution.py:342
  19.2 7.4 %collective-permute-start.7 = (s16[304,128]{1,0:T(8,128)(2,1)S(1)}, s16[304,128]{1,0:T(8,128)(2,1)S(1)}, u32[]{:S(2)}, u32[]{:S(2)}) collective-permute-start(s16[304,128]{1,0:T(8,128)(2,1)S(1)} %get-tuple-element.20), channel_id=1, source_target_pairs={{0,4},{4,0},{8,12},{12,8},{1,5},{5,1},{9,13},{13,9},{2,6},{6,2},{1... | collective-permute-start | bytes 233480 | tf_op jit(solution)/shard_map/ppermute | solution.py:342
  22.9 6.8 %collective-permute-start.10 = (s16[272,128]{1,0:T(8,128)(2,1)S(1)}, s16[272,128]{1,0:T(8,128)(2,1)S(1)}, u32[]{:S(2)}, u32[]{:S(2)}) collective-permute-start(s16[272,128]{1,0:T(8,128)(2,1)S(1)} %get-tuple-element.25), channel_id=1, source_target_pairs={{0,8},{4,12},{8,0},{12,4},{1,9},{5,13},{9,1},{13,5},{2,10},{6,14},... | collective-permute-start | bytes 208904 | tf_op jit(solution)/shard_map/ppermute | solution.py:342
  24.6 6.3 %collective-permute-start.11 = (s16[272,128]{1,0:T(8,128)(2,1)S(1)}, s16[272,128]{1,0:T(8,128)(2,1)S(1)}, u32[]{:S(2)}, u32[]{:S(2)}) collective-permute-start(s16[272,128]{1,0:T(8,128)(2,1)S(1)} %get-tuple-element.26), channel_id=1, source_target_pairs={{0,12},{4,8},{8,4},{12,0},{1,13},{5,9},{9,5},{13,1},{2,14},{6,10},... | collective-permute-start | bytes 208904 | tf_op jit(solution)/shard_map/ppermute | solution.py:342
  26.0 5.1 %collective-permute-start.12 = (s16[272,128]{1,0:T(8,128)(2,1)S(1)}, s16[272,128]{1,0:T(8,128)(2,1)S(1)}, u32[]{:S(2)}, u32[]{:S(2)}) collective-permute-start(s16[272,128]{1,0:T(8,128)(2,1)S(1)} %get-tuple-element.27), channel_id=1, source_target_pairs={{0,4},{4,0},{8,12},{12,8},{1,5},{5,1},{9,13},{13,9},{2,6},{6,2},{1... | collective-permute-start | bytes 208904 | tf_op jit(solution)/shard_map/ppermute | solution.py:342
  26.7 6.0 %collective-permute-start.8 = (s16[304,128]{1,0:T(8,128)(2,1)S(1)}, s16[304,128]{1,0:T(8,128)(2,1)S(1)}, u32[]{:S(2)}, u32[]{:S(2)}) collective-permute-start(s16[304,128]{1,0:T(8,128)(2,1)S(1)} %add_early.1.refs_0_), channel_id=1, source_target_pairs={{0,2},{1,3},{2,0},{3,1},{4,6},{5,7},{6,4},{7,5},{8,10},{9,11},{10,... | collective-permute-start | bytes 233480 | tf_op jit(solution)/shard_map/ppermute | solution.py:339
  31.2 4.4 %collective-permute-start.13 = (s16[272,128]{1,0:T(8,128)(2,1)S(1)}, s16[272,128]{1,0:T(8,128)(2,1)S(1)}, u32[]{:S(2)}, u32[]{:S(2)}) collective-permute-start(s16[272,128]{1,0:T(8,128)(2,1)S(1)} %add_late.1.refs_2_), channel_id=1, source_target_pairs={{0,2},{1,3},{2,0},{3,1},{4,6},{5,7},{6,4},{7,5},{8,10},{9,11},{10,... | collective-permute-start | bytes 208904 | tf_op jit(solution)/shard_map/ppermute | solution.py:339
  32.7 2.9 %collective-permute-start.14 = (s16[304,128]{1,0:T(8,128)(2,1)S(1)}, s16[304,128]{1,0:T(8,128)(2,1)S(1)}, u32[]{:S(2)}, u32[]{:S(2)}) collective-permute-start(s16[304,128]{1,0:T(8,128)(2,1)S(1)} %add_early.1.refs_0_), channel_id=1, source_target_pairs={{0,1},{1,0},{2,3},{3,2},{4,5},{5,4},{6,7},{7,6},{8,9},{9,8},{10,11... | collective-permute-start | bytes 233480 | tf_op jit(solution)/shard_map/ppermute | solution.py:339
  32.7 2.9 %collective-permute-start.15 = (s16[304,128]{1,0:T(8,128)(2,1)S(1)}, s16[304,128]{1,0:T(8,128)(2,1)S(1)}, u32[]{:S(2)}, u32[]{:S(2)}) collective-permute-start(s16[304,128]{1,0:T(8,128)(2,1)S(1)} %collective-permute-done.8.refs_1_), channel_id=1, source_target_pairs={{0,1},{1,0},{2,3},{3,2},{4,5},{5,4},{6,7},{7,6},{8,9},{9,8},{10,11... | collective-permute-start | bytes 233480 | tf_op jit(solution)/shard_map/ppermute | solution.py:339
  33.2 2.4 %collective-permute-start.16 = (s16[272,128]{1,0:T(8,128)(2,1)S(1)}, s16[272,128]{1,0:T(8,128)(2,1)S(1)}, u32[]{:S(2)}, u32[]{:S(2)}) collective-permute-start(s16[272,128]{1,0:T(8,128)(2,1)S(1)} %add_late.1.refs_2_), channel_id=1, source_target_pairs={{0,1},{1,0},{2,3},{3,2},{4,5},{5,4},{6,7},{7,6},{8,9},{9,8},{10,11... | collective-permute-start | bytes 208904 | tf_op jit(solution)/shard_map/ppermute | solution.py:339
  35.6 1.3 %collective-permute-start.17 = (s16[272,128]{1,0:T(8,128)(2,1)S(1)}, s16[272,128]{1,0:T(8,128)(2,1)S(1)}, u32[]{:S(2)}, u32[]{:S(2)}) collective-permute-start(s16[272,128]{1,0:T(8,128)(2,1)S(1)} %collective-permute-done.13.refs_3_), channel_id=1, source_target_pairs={{0,1},{1,0},{2,3},{3,2},{4,5},{5,4},{6,7},{7,6},{8,9},{9,8},{10,11... | collective-permute-start | bytes 208904 | tf_op jit(solution)/shard_map/ppermute | solution.py:339
